TPU v7x, 128 devices: a whole 4x4x4 slice. The times are simulated.
128 devices in a mesh: mlp: 16 (over z, y_hi, core), seq: 8 (over x, y_lo).
Axes of the slice: x: 4, y: 4 (y_hi: 2, y_lo: 2; y = y_hi * 2 + y_lo), z: 4, core: 2. Of those that a mesh axis runs over, the one named last changes fastest.
Arguments:
- tokens: bfloat16 [65536, 1024], P(('mlp', 'seq')), may hold values from -6 to 6
- qkv_weight: bfloat16 [1024, 3072], P(('mlp', 'seq')), may hold values from -0.25 to 0.25
- out_weight: bfloat16 [1024, 1024], P(('mlp', 'seq')), may hold values from -0.75 to 0.75
- up_weight: bfloat16 [1024, 4096], P('seq', 'mlp'), may hold values from -0.1875 to 0.1875
- down_weight: bfloat16 [4096, 1024], P('mlp', 'seq'), may hold values from -0.09375 to 0.09375
- ln1_gain: float32 [1024], replicated, may hold values from 0.1 to 1.9
- ln1_bias: float32 [1024], replicated, may hold values from -1.75 to 1.75
- q_bias: float32 [1024], replicated, may hold values from -1.75 to 1.75
- v_bias: float32 [1024], replicated, may hold values from -1.75 to 1.75
- out_bias: float32 [1024], replicated, may hold values from -1.75 to 1.75
- ln2_gain: float32 [1024], replicated, may hold values from 0.1 to 1.9
- ln2_bias: float32 [1024], replicated, may hold values from -1.75 to 1.75
- up_bias: float32 [4096], replicated, may hold values from -1.75 to 1.75
- down_bias: float32 [1024], replicated, may hold values from -1.75 to 1.75
- segment_ids: int32 [65536], P(('mlp', 'seq')), may hold values from 0 to 127, never falling along the last dimension, each value on 1 to 2048 neighbouring positions
- cotangent: bfloat16 [65536, 1024], P(('mlp', 'seq')), may hold values from -6 to 6
Outputs:
- output: bfloat16 [65536, 1024], P(('mlp', 'seq'))
- input_grad: float32 [65536, 1024], P(('mlp', 'seq'))
- qkv_weight_grad: float32 [1024, 3072], P(('mlp', 'seq'))
- out_weight_grad: float32 [1024, 1024], P(('mlp', 'seq'))
- up_weight_grad: float32 [1024, 4096], P('seq', 'mlp')
- down_weight_grad: float32 [4096, 1024], P('mlp', 'seq')
- ln1_gain_grad: float32 [1024], replicated
- ln1_bias_grad: float32 [1024], replicated
- q_bias_grad: float32 [1024], replicated
- v_bias_grad: float32 [1024], replicated
- out_bias_grad: float32 [1024], replicated
- ln2_gain_grad: float32 [1024], replicated
- ln2_bias_grad: float32 [1024], replicated
- up_bias_grad: float32 [4096], replicated
- down_bias_grad: float32 [1024], replicated
Inputs may be any that keep to these rules, and one draw needn't show every extreme that they name: `segment_ids`: clip numbers never fall along the tokens; each clip holds 1 to 2048 tokens.
All inputs are finite; a program needn't handle non-finite values.
Results may differ from a plain program's by a relative error of at most 0.018.
Values may be sent and summed in bfloat16 or wider, within the bound.
No kernel may reach another device: no remote copies, remote signals or barrier semaphores. Data moves between devices by JAX's collectives and lax.ppermute only.
A program may use at most 256 MiB of HBM per device.

v0:
```python
import jax
import jax.numpy as jnp
from jax import lax
from jax.sharding import PartitionSpec as P

HEADS = 16
HEAD_DIM = 64
BLOCK = 128


def layer_norm(values, gain_vec, bias_vec):
    center = values - jnp.mean(values, axis=-1, keepdims=True)
    spread = jnp.mean(center * center, axis=-1, keepdims=True)
    return center * lax.rsqrt(spread + 1e-05) * gain_vec + bias_vec


def blocked(values):
    return values.reshape(values.shape[0] // BLOCK, BLOCK, HEADS, HEAD_DIM)


def allowed_pairs(clip_ids):
    clip_blocks = clip_ids.reshape(-1, BLOCK)
    row_index = lax.broadcasted_iota(jnp.int32, (BLOCK, BLOCK), 0)
    col_index = lax.broadcasted_iota(jnp.int32, (BLOCK, BLOCK), 1)
    same_clip = clip_blocks[:, :, None] == clip_blocks[:, None, :]
    return (same_clip & (row_index >= col_index)[None])[:, None]


def masked_scores(query_blocks, key_blocks, allowed):
    raw_scores = jnp.einsum(
        "bqhd,bkhd->bhqk", query_blocks, key_blocks, preferred_element_type=jnp.float32
    ) * HEAD_DIM ** (-0.5)
    return jnp.where(allowed, raw_scores, -1e30)


def contract_rows(left, right):
    return lax.dot_general(
        left, right, (((0,), (0,)), ((), ())), preferred_element_type=jnp.float32
    )


def contract_cols(left, right):
    return lax.dot_general(
        left, right, (((1,), (1,)), ((), ())), preferred_element_type=jnp.float32
    )


def on_device(
    tokens,
    qkv_weight,
    out_weight,
    up_weight,
    down_weight,
    ln1_gain,
    ln1_bias,
    q_bias,
    v_bias,
    out_bias,
    ln2_gain,
    ln2_bias,
    up_bias,
    down_bias,
    segment_ids,
    cotangent,
):
    tok_rows = tokens.shape[0]
    width = tokens.shape[1]
    inputs = tokens.astype(jnp.float32)
    normed_one, norm_one_back = jax.vjp(layer_norm, inputs, ln1_gain, ln1_bias)
    normed_one_low = normed_one.astype(jnp.bfloat16)
    full_qkv, full_out = (
        lax.all_gather(qkv_weight, ("mlp", "seq"), axis=0, tiled=True),
        lax.all_gather(out_weight, ("mlp", "seq"), axis=0, tiled=True),
    )
    projected = jnp.dot(normed_one_low, full_qkv, preferred_element_type=jnp.float32)
    projected = projected + jnp.concatenate([q_bias, jnp.zeros_like(q_bias), v_bias])
    query_blocks = blocked(projected[:, :width].astype(jnp.bfloat16))
    key_blocks = blocked(projected[:, width : 2 * width].astype(jnp.bfloat16))
    value_blocks = blocked(projected[:, 2 * width :].astype(jnp.bfloat16))
    allowed = allowed_pairs(segment_ids)
    scores = masked_scores(query_blocks, key_blocks, allowed)
    row_peak = jnp.max(scores, axis=-1, keepdims=True)
    powers = jnp.exp(scores - row_peak)
    row_total = jnp.sum(powers, axis=-1, keepdims=True)
    weights_low = (powers / row_total).astype(jnp.bfloat16)
    log_total = row_peak + jnp.log(row_total)
    mixed_low = (
        jnp.einsum("bhqk,bkhd->bqhd", weights_low, value_blocks, preferred_element_type=jnp.float32)
        .reshape(tok_rows, width)
        .astype(jnp.bfloat16)
    )
    hidden = inputs + jnp.dot(mixed_low, full_out, preferred_element_type=jnp.float32) + out_bias
    normed_two, norm_two_back = jax.vjp(layer_norm, hidden, ln2_gain, ln2_bias)
    normed_two_low = normed_two.astype(jnp.bfloat16)
    up_part, down_part = (
        lax.all_gather(up_weight, "seq", axis=0, tiled=True),
        lax.all_gather(down_weight, "seq", axis=1, tiled=True),
    )
    column_in = lax.all_gather(normed_two_low, "mlp", axis=0, tiled=True)
    hidden_units = up_part.shape[1]
    offset = lax.axis_index("mlp") * hidden_units
    pre_act = jnp.dot(
        column_in, up_part, preferred_element_type=jnp.float32
    ) + lax.dynamic_slice_in_dim(up_bias, offset, hidden_units)
    activation, gelu_back = jax.vjp(jax.nn.gelu, pre_act)
    activation_low = activation.astype(jnp.bfloat16)
    feed_out = lax.psum_scatter(
        jnp.dot(activation_low, down_part, preferred_element_type=jnp.float32).astype(jnp.bfloat16),
        "mlp",
        scatter_dimension=0,
        tiled=True,
    ).astype(jnp.float32)
    column_grad = lax.all_gather(cotangent, "mlp", axis=0, tiled=True)
    grad_pre = gelu_back(contract_cols(column_grad, down_part))[0].astype(jnp.bfloat16)
    up_grad_part = contract_rows(column_in, grad_pre)
    down_grad_part = contract_rows(activation_low, column_grad)
    grad_normed_two = lax.psum_scatter(
        contract_cols(grad_pre, up_part).astype(jnp.bfloat16),
        "mlp",
        scatter_dimension=0,
        tiled=True,
    ).astype(jnp.float32)
    up_bias_grad = lax.dynamic_update_slice_in_dim(
        jnp.zeros_like(up_bias), jnp.sum(grad_pre.astype(jnp.float32), axis=0), offset, 0
    )
    output = (hidden + feed_out + down_bias).astype(jnp.bfloat16)
    up_grad, down_grad = (
        lax.psum_scatter(
            up_grad_part.astype(jnp.bfloat16), "seq", scatter_dimension=0, tiled=True
        ).astype(jnp.float32),
        lax.psum_scatter(
            down_grad_part.astype(jnp.bfloat16), "seq", scatter_dimension=1, tiled=True
        ).astype(jnp.float32),
    )
    grad_hidden_norm, ln2_gain_grad, ln2_bias_grad = norm_two_back(grad_normed_two)
    grad_out = cotangent.astype(jnp.float32)
    grad_hidden = grad_out + grad_hidden_norm
    grad_hidden_low = grad_hidden.astype(jnp.bfloat16)
    back_qkv, back_out = (
        lax.all_gather(qkv_weight, ("mlp", "seq"), axis=0, tiled=True),
        lax.all_gather(out_weight, ("mlp", "seq"), axis=0, tiled=True),
    )
    out_weight_grad = contract_rows(mixed_low, grad_hidden_low)
    grad_mixed_blocks = blocked(contract_cols(grad_hidden_low, back_out).astype(jnp.bfloat16))
    probs = jnp.exp(masked_scores(query_blocks, key_blocks, allowed) - log_total)
    grad_probs = jnp.einsum(
        "bqhd,bkhd->bhqk", grad_mixed_blocks, value_blocks, preferred_element_type=jnp.float32
    )
    grad_scores = (
        probs * (grad_probs - jnp.sum(probs * grad_probs, axis=-1, keepdims=True))
    ).astype(jnp.bfloat16)
    score_scale = HEAD_DIM ** (-0.5)
    grad_query = (
        (
            jnp.einsum(
                "bhqk,bkhd->bqhd", grad_scores, key_blocks, preferred_element_type=jnp.float32
            )
            * score_scale
        )
        .reshape(tok_rows, width)
        .astype(jnp.bfloat16)
    )
    grad_key = (
        (
            jnp.einsum(
                "bhqk,bqhd->bkhd", grad_scores, query_blocks, preferred_element_type=jnp.float32
            )
            * score_scale
        )
        .reshape(tok_rows, width)
        .astype(jnp.bfloat16)
    )
    grad_value = (
        jnp.einsum(
            "bhqk,bqhd->bkhd",
            probs.astype(jnp.bfloat16),
            grad_mixed_blocks,
            preferred_element_type=jnp.float32,
        )
        .reshape(tok_rows, width)
        .astype(jnp.bfloat16)
    )
    grad_projected = jnp.concatenate([grad_query, grad_key, grad_value], axis=1)
    qkv_weight_grad = contract_rows(normed_one_low, grad_projected)
    grad_normed_one = contract_cols(grad_projected, back_qkv)
    grad_input_norm, ln1_gain_grad, ln1_bias_grad = norm_one_back(grad_normed_one)
    grad_tokens = grad_hidden + grad_input_norm
    qkv_grad, out_grad = (
        lax.psum_scatter(qkv_weight_grad, ("mlp", "seq"), scatter_dimension=0, tiled=True),
        lax.psum_scatter(out_weight_grad, ("mlp", "seq"), scatter_dimension=0, tiled=True),
    )
    summed = lax.psum(
        (
            ln1_gain_grad,
            ln1_bias_grad,
            jnp.sum(grad_query.astype(jnp.float32), axis=0),
            jnp.sum(grad_value.astype(jnp.float32), axis=0),
            jnp.sum(grad_hidden, axis=0),
            ln2_gain_grad,
            ln2_bias_grad,
            up_bias_grad,
            jnp.sum(grad_out, axis=0),
        ),
        ("mlp", "seq"),
    )
    return (
        output,
        grad_tokens,
        qkv_grad,
        out_grad,
        up_grad,
        down_grad,
        summed[0],
        summed[1],
        summed[2],
        summed[3],
        summed[4],
        summed[5],
        summed[6],
        summed[7],
        summed[8],
    )


def solution(mesh):
    placed = (
        P(("mlp", "seq"), None),
        P(("mlp", "seq"), None),
        P(("mlp", "seq"), None),
        P("seq", "mlp"),
        P("mlp", "seq"),
        P(),
        P(),
        P(),
        P(),
        P(),
        P(),
        P(),
        P(),
        P(),
        P(("mlp", "seq")),
        P(("mlp", "seq"), None),
    )
    return jax.shard_map(
        on_device,
        mesh=mesh,
        in_specs=placed,
        out_specs=(
            P(("mlp", "seq"), None),
            P(("mlp", "seq"), None),
            P(("mlp", "seq"), None),
            P(("mlp", "seq"), None),
            P("seq", "mlp"),
            P("mlp", "seq"),
            P(),
            P(),
            P(),
            P(),
            P(),
            P(),
            P(),
            P(),
            P(),
        ),
        check_vma=False,
    )
```

profile of v0, /device:TPU:0, one launch (start us, length us, event | category | flops | bytes accessed | tf_op | source)
XLA Modules:
  0.0 2568.9 jit_solution(6397906699506046712)
XLA Ops:
  14.0 308.8 %all-gather.5.cloned.1.call-done = bf16[1024,3072]{1,0:T(8,128)(2,1)} async-done(((bf16[8,3072]{1,0:T(8,128)(2,1)}), bf16[1024,3072]{1,0:T(8,128)(2,1)}) %all-gather.5.cloned.1.call-update) | async-done | bytes 6291472 | tf_op jit(solution)/shard_map/all_gather | solution.py:72
  322.9 6.7 add_convert_fusion
  333.1 2.8 copy.67
  341.2 4.3 reshape.148
  345.5 3.7 copy.68
  354.8 272.0 %all-gather.7.cloned.1.call-done = bf16[1024,1024]{1,0:T(8,128)(2,1)} async-done(((bf16[8,1024]{1,0:T(8,128)(2,1)}), bf16[1024,1024]{1,0:T(8,128)(2,1)}) %all-gather.7.cloned.1.call-update) | async-done | bytes 2097168 | tf_op jit(solution)/shard_map/all_gather | solution.py:73
  626.8 3.3 fusion.54
  632.8 31.3 %all_gather.23 = bf16[1024,256]{1,0:T(8,128)(2,1)} all-gather(bf16[128,256]{1,0:T(8,128)(2,1)S(1)} %copy-done.18), channel_id=1, replica_groups=mesh['mlp'=16,'seq'=8] {'seq'}, dimensions={0}, use_global_device_ids=true | all-gather | bytes 589824 | tf_op jit(solution)/shard_map/all_gather | solution.py:96
  664.1 27.3 %all_gather.24 = bf16[256,1024]{1,0:T(8,128)(2,1)} all-gather(bf16[256,128]{1,0:T(8,128)(2,1)S(1)} %copy-done.19), channel_id=1, replica_groups=mesh['mlp'=16,'seq'=8] {'seq'}, dimensions={1}, use_global_device_ids=true | all-gather | bytes 589824 | tf_op jit(solution)/shard_map/all_gather | solution.py:97
  691.3 57.7 %all-gather.11.cloned.1.call-done = bf16[8192,1024]{1,0:T(8,128)(2,1)} async-done(((bf16[512,1024]{1,0:T(8,128)(2,1)}), bf16[8192,1024]{1,0:T(8,128)(2,1)}) %all-gather.11.cloned.1.call-update) | async-done | bytes 16777232 | tf_op jit(solution)/shard_map/all_gather | solution.py:113
  749.1 13.6 fusion.55
  762.7 95.9 %all-gather.9.cloned.1.call-done = bf16[8192,1024]{1,0:T(8,128)(2,1)} async-done(((bf16[512,1024]{1,0:T(8,128)(2,1)}), bf16[8192,1024]{1,0:T(8,128)(2,1)}) %all-gather.9.cloned.1.call-update) | async-done | bytes 16777232 | tf_op jit(solution)/shard_map/all_gather | solution.py:99
  858.6 17.1 convert_reduce_fusion
  875.7 12.6 convolution_convert_fusion
  888.3 13.4 convolution_convert_fusion.1
  901.8 18.2 convolution_convert_fusion.3
  922.6 13.0 convolution_convert_fusion.4
  935.7 97.1 %reduce-scatter.11.cloned.1.call-done = bf16[512,1024]{1,0:T(8,128)(2,1)} async-done(((bf16[8192,1024]{1,0:T(8,128)(2,1)}), bf16[512,1024]{1,0:T(8,128)(2,1)}) %reduce-scatter.11.cloned.1.call-update) | async-done | bytes 1048592 | tf_op jit(solution)/shard_map/reduce_scatter | solution.py:117
  1036.0 145.8 %reduce-scatter.9.cloned.1.call-done = bf16[512,1024]{1,0:T(8,128)(2,1)} async-done(((bf16[8192,1024]{1,0:T(8,128)(2,1)}), bf16[512,1024]{1,0:T(8,128)(2,1)}) %reduce-scatter.9.cloned.1.call-update) | async-done | bytes 1048592 | tf_op jit(solution)/shard_map/reduce_scatter | solution.py:107
  1181.8 3.5 fusion.51
  1186.7 3.2 fusion.35
  1191.5 3.9 convolution_convert_fusion.2
  1195.4 4.0 reshape.151
  1199.4 3.6 copy.72
  1203.0 4.3 convert_reduce_fusion.4
  1217.0 7.1 fusion.44
  1226.1 32.4 %reduce-scatter.17.cloned.1.call-done = bf16[128,256]{1,0:T(8,128)(2,1)} async-done(((bf16[1024,256]{1,0:T(8,128)(2,1)}), bf16[128,256]{1,0:T(8,128)(2,1)}) %reduce-scatter.17.cloned.1.call-update) | async-done | bytes 65552 | tf_op jit(solution)/shard_map/reduce_scatter | solution.py:128
  1260.1 6.9 fusion.49
  1269.3 64.4 %all-reduce = (f32[1024]{0:T(1024)}, f32[1024]{0:T(1024)}, f32[1024]{0:T(1024)}, f32[1024]{0:T(1024)}, f32[1024]{0:T(1024)}, /*index=5*/f32[1024]{0:T(1024)}, f32[1024]{0:T(1024)}, f32[4096]{0:T(1024)}, f32[1024]{0:T(1024)}) all-reduce(f32[1024]{0:T(1024)S(1)} %get-tuple-element.17, ...), channel_id=1, replica_groups=mesh['mlp'=16,'seq'=8] {'mlp','seq'}, use_global_device_ids=true, to_apply=%region_18.19 | all-reduce | flops 12288 | bytes 98304 | tf_op jit(solution)/shard_map/psum | solution.py:192
  1333.7 3.6 add_add_fusion.2
  1337.3 566.5 %reduce-scatter.15.cloned.1.call-done = f32[8,1024]{1,0:T(8,128)} async-done(((f32[1024,1024]{1,0:T(8,128)}), f32[8,1024]{1,0:T(8,128)}) %reduce-scatter.15.cloned.1.call-update) | async-done | bytes 32784 | tf_op jit(solution)/shard_map/reduce_scatter | solution.py:190
  1903.9 658.0 %reduce-scatter.13.cloned.1.call-done = f32[8,3072]{1,0:T(8,128)} async-done(((f32[1024,3072]{1,0:T(8,128)}), f32[8,3072]{1,0:T(8,128)}) %reduce-scatter.13.cloned.1.call-update) | async-done | bytes 98320 | tf_op jit(solution)/shard_map/reduce_scatter | solution.py:189
  (122 shorter events, 47.9 us)
Async XLA Ops:
  7.2 315.7 %copy-start.2 = (bf16[512,1024]{1,0:T(8,128)(2,1)S(1)}, bf16[512,1024]{1,0:T(8,128)(2,1)}, u32[]{:S(2)}) copy-start(bf16[512,1024]{1,0:T(8,128)(2,1)} %param.16) | copy-start | bytes 3145732
  7.2 6.7 copy-start.23
  7.2 315.7 %copy-start.22 = (f32[1024]{0:T(1024)S(1)}, f32[1024]{0:T(1024)}, u32[]{:S(2)}) copy-start(f32[1024]{0:T(1024)} %param.21) | copy-start | bytes 12292
  7.2 315.7 %copy-start.26 = (f32[1024]{0:T(1024)S(1)}, f32[1024]{0:T(1024)}, u32[]{:S(2)}) copy-start(f32[1024]{0:T(1024)} %param.22) | copy-start | bytes 12292
  7.2 315.7 %all-gather.5.cloned.1.call-start = ((), (), s32[]{:S(2)}) async-start(), calls=%async_computation.6 | async-start | bytes 6340608 | tf_op jit(solution)/shard_map/all_gather | solution.py:72
  8.0 618.9 %all-gather.7.cloned.1.call-start = ((), (), s32[]{:S(2)}) async-start(), calls=%async_computation.7 | async-start | bytes 2113536 | tf_op jit(solution)/shard_map/all_gather | solution.py:73
  8.7 740.3 %all-gather.11.cloned.1.call-start = ((), (), s32[]{:S(2)}) async-start(), calls=%async_computation.10 | async-start | bytes 17825792 | tf_op jit(solution)/shard_map/all_gather | solution.py:113
  9.4 849.2 %all-gather.9.cloned.1.call-start = ((), (), s32[]{:S(2)}) async-start(), calls=%async_computation.8 | async-start | bytes 17825792 | tf_op jit(solution)/shard_map/all_gather | solution.py:99
  336.0 13.2 copy-start.7
  341.1 8.0 copy-start.9
  350.2 2.8 copy-start
  350.2 2.0 copy-start.13
  352.1 274.7 %copy-start.17 = (f32[1024]{0:T(1024)S(1)}, f32[1024]{0:T(1024)}, u32[]{:S(2)}) copy-start(f32[1024]{0:T(1024)} %param.25) | copy-start | bytes 12292
  626.8 3.7 copy-start.16
  626.8 3.7 copy-start.25
  630.1 2.6 copy-start.18
  630.2 33.9 %copy-start.19 = (bf16[256,128]{1,0:T(8,128)(2,1)S(1)}, bf16[256,128]{1,0:T(8,128)(2,1)}, u32[]{:S(2)}) copy-start(bf16[256,128]{1,0:T(8,128)(2,1)} %param.20) | copy-start | bytes 196612
  631.9 400.9 %reduce-scatter.11.cloned.1.call-start = ((), (), s32[]{:S(2)}) async-start(), calls=%async_computation.11 | async-start | bytes 17825792 | tf_op jit(solution)/shard_map/reduce_scatter | solution.py:117
  888.3 293.6 %reduce-scatter.9.cloned.1.call-start = ((), (), s32[]{:S(2)}) async-start(), calls=%async_computation.9 | async-start | bytes 17825792 | tf_op jit(solution)/shard_map/reduce_scatter | solution.py:107
  901.8 322.7 %reduce-scatter.19.cloned.1.call-start = ((), (), s32[]{:S(2)}) async-start(), calls=%async_computation.15 | async-start | bytes 589824
  922.1 336.3 %reduce-scatter.17.cloned.1.call-start = ((), (), s32[]{:S(2)}) async-start(), calls=%async_computation.14 | async-start | bytes 589824 | tf_op jit(solution)/shard_map/reduce_scatter | solution.py:128
  935.7 246.1 %copy-start.24 = (f32[1024]{0:T(1024)S(1)}, f32[1024]{0:T(1024)}, u32[]{:S(2)}) copy-start(f32[1024]{0:T(1024)} %param.29) | copy-start | bytes 12292
  935.7 968.2 %reduce-scatter.15.cloned.1.call-start = ((), (), s32[]{:S(2)}) async-start(), calls=%async_computation.13 | async-start | bytes 4227072 | tf_op jit(solution)/shard_map/reduce_scatter | solution.py:190
  1032.9 2.0 copy-start.6
  1181.8 4.9 copy-start.5
  1189.9 1371.9 %reduce-scatter.13.cloned.1.call-start = ((), (), s32[]{:S(2)}) async-start(), calls=%async_computation.12 | async-start | bytes 12681216 | tf_op jit(solution)/shard_map/reduce_scatter | solution.py:189
  1203.0 5.2 copy-start.1
  1203.0 5.2 copy-start.11
  1203.0 5.2 copy-start.14
  1210.7 1.7 copy-start.10
  1215.3 1.7 copy-start.15
  1260.1 6.9 copy-start.21
  (5 other events, 6.1 us)
Sparse Core Ops, SparseCore 0:
  9.7 313.0 all-gather.4
  324.6 302.2 all-gather.6
  629.3 119.7 all-gather.10
  751.9 106.5 all-gather.8
  888.4 144.4 reduce-scatter.10
  1037.0 144.7 reduce-scatter.8
  1184.2 35.4 reduce-scatter.18
  1222.1 36.2 reduce-scatter.16
  1261.4 642.4 reduce-scatter.14
  1906.8 655.0 reduce-scatter.12
where the time goes:
time: 2580 us; the launch traced here: 2570 us
  waiting for transfers between devices  2240 us (87%)
  matrix products  129 us (5%)
  blocking collectives  123 us (5%)
  local copies, waits for them, and re-layouts  43.5 us (2%)
    reduce_scatter x1, waiting for transfers between devices, on_device(): lax.psum_scatter(qkv_weight_grad, ('mlp', 'seq'), scatter_dimension=0, ti...  658 us
    reduce_scatter x1, waiting for transfers between devices, on_device(): lax.psum_scatter(out_weight_grad, ('mlp', 'seq'), scatter_dimension=0, ti...  567 us
    all_gather x1, waiting for transfers between devices, on_device(): lax.all_gather(qkv_weight, ('mlp', 'seq'), axis=0, tiled=True)  309 us
    all_gather x1, waiting for transfers between devices, on_device(): lax.all_gather(out_weight, ('mlp', 'seq'), axis=0, tiled=True)  272 us
    reduce_scatter x1, waiting for transfers between devices, on_device(): lax.psum_scatter(jnp.dot(activation_low, down_part, preferred_element_typ...  146 us
    reduce_scatter x1, waiting for transfers between devices, on_device(): lax.psum_scatter(contract_cols(grad_pre, up_part).astype(jnp.bfloat16), '...  97.1 us
    all_gather x1, waiting for transfers between devices, on_device(): column_in = lax.all_gather(normed_two_low, 'mlp', axis=0, tiled=True)  95.9 us
    psum x1, blocking collectives, on_device(): lax.psum((ln1_gain_grad, ln1_bias_grad, jnp.sum(grad_query.astype(jnp.flo...  64.4 us
  transfers between devices with their start and end apart: 10, of which 9 were waited for; matrix products, arithmetic and copies ran while one was open for 6% of the time, Pallas kernels for 0%

commit v1 on v0

v1 whole, which is shorter than its diff:
```python
import itertools

import jax
import jax.numpy as jnp
from jax import lax
from jax.sharding import Mesh, PartitionSpec as P

HEADS = 16
HEAD_DIM = 64
BLOCK = 128
AXES = ("z", "yh", "c", "x", "yl")


def device_number(place):
    return (
        ((place["z"] * 2 + place["y"] // 2) * 2 + place["c"]) * 4 + place["x"]
    ) * 2 + place["y"] % 2


def exchange_pairs(axis, second):
    pairs = []
    for z, y, c, x in itertools.product(range(4), range(4), range(2), range(4)):
        here = {"z": z, "y": y, "c": c, "x": x}
        mask = 1 if (c == 0) != second else 3
        there = dict(here)
        there[axis] = here[axis] ^ mask
        pairs.append((device_number(here), device_number(there)))
    return pairs


def swap_axis(values, axis, second):
    return lax.ppermute(values, AXES, exchange_pairs(axis, second))


def swap_core(values):
    return lax.ppermute(values, "c", [(0, 1), (1, 0)])


def position(axis):
    if axis == "y":
        return lax.axis_index("yh") * 2 + lax.axis_index("yl")
    return lax.axis_index(axis)


def masks():
    core = lax.axis_index("c")
    first = jnp.where(core == 0, 1, 3)
    return first, 4 - first


def place_pieces(pieces, slots):
    out = jnp.zeros((len(pieces),) + pieces[0].shape, pieces[0].dtype)
    for piece, slot in zip(pieces, slots):
        out = lax.dynamic_update_index_in_dim(out, piece, slot, 0)
    return out


def gather_all(values, order):
    first, second = masks()
    for axis in order:
        here = position(axis)
        near = swap_axis(values, axis, False)
        far = swap_axis(jnp.stack([values, near]), axis, True)
        values = place_pieces(
            [values, near, far[0], far[1]],
            [here, here ^ first, here ^ second, here ^ second ^ first],
        )
    core = lax.axis_index("c")
    other = swap_core(values)
    return place_pieces([values, other], [core, 1 - core])


def scatter_sum(values, order):
    first, second = masks()
    core = lax.axis_index("c")

    def at(array, slot):
        return lax.dynamic_index_in_dim(array, slot, 0, keepdims=False)

    def add(left, right):
        return (left.astype(jnp.float32) + right.astype(jnp.float32)).astype(jnp.bfloat16)

    values = add(at(values, core), swap_core(at(values, 1 - core)))
    for axis in reversed(order):
        here = position(axis)
        far = swap_axis(
            jnp.stack([at(values, here ^ second), at(values, here ^ second ^ first)]), axis, True
        )
        near = swap_axis(add(at(values, here ^ first), far[1]), axis, False)
        values = at(values, here).astype(jnp.float32) + far[0].astype(jnp.float32)
        values = values + near.astype(jnp.float32)
        if axis != order[0]:
            values = values.astype(jnp.bfloat16)
    return values


def sum_everywhere(values):
    for axis in ("x", "y", "z"):
        for second in (False, True):
            values = values + swap_axis(values, axis, second)
    return values + swap_core(values)


def names_of(order):
    return ["c"] + list(reversed(order))


def split_y(array, names):
    at = names.index("y")
    shape = array.shape
    array = array.reshape(shape[:at] + (2, 2) + shape[at + 1 :])
    return array, names[:at] + ["yh", "yl"] + names[at + 1 :]


ROW_LAYOUT = ["z", "yh", "c", "x", "yl", "r", "k"]
UP_LAYOUT = ["x", "yl", "r", "z", "yh", "c", "k"]
DOWN_LAYOUT = ["z", "yh", "c", "r", "x", "yl", "k"]


def whole(array, order, layout, shape):
    array, names = split_y(array, names_of(order))
    names = names + ["r", "k"]
    return array.transpose([names.index(n) for n in layout]).reshape(shape)


def pieces_of(array, order, layout, rows, cols):
    sizes = {"z": 4, "yh": 2, "c": 2, "x": 4, "yl": 2, "r": rows, "k": cols}
    array = array.reshape([sizes[n] for n in layout])
    names = []
    for n in names_of(order):
        names += ["yh", "yl"] if n == "y" else [n]
    names += ["r", "k"]
    array = array.transpose([layout.index(n) for n in names])
    return array.reshape((2, 4, 4, 4, rows, cols))


def layer_norm(values, gain_vec, bias_vec):
    center = values - jnp.mean(values, axis=-1, keepdims=True)
    spread = jnp.mean(center * center, axis=-1, keepdims=True)
    return center * lax.rsqrt(spread + 1e-05) * gain_vec + bias_vec


def blocked(values):
    return values.reshape(values.shape[0] // BLOCK, BLOCK, HEADS, HEAD_DIM)


def allowed_pairs(clip_ids):
    clip_blocks = clip_ids.reshape(-1, BLOCK)
    row_index = lax.broadcasted_iota(jnp.int32, (BLOCK, BLOCK), 0)
    col_index = lax.broadcasted_iota(jnp.int32, (BLOCK, BLOCK), 1)
    same_clip = clip_blocks[:, :, None] == clip_blocks[:, None, :]
    return (same_clip & (row_index >= col_index)[None])[:, None]


def masked_scores(query_blocks, key_blocks, allowed):
    raw_scores = jnp.einsum(
        "bqhd,bkhd->bhqk", query_blocks, key_blocks, preferred_element_type=jnp.float32
    ) * HEAD_DIM ** (-0.5)
    return jnp.where(allowed, raw_scores, -1e30)


def contract_rows(left, right):
    return lax.dot_general(
        left, right, (((0,), (0,)), ((), ())), preferred_element_type=jnp.float32
    )


def contract_cols(left, right):
    return lax.dot_general(
        left, right, (((1,), (1,)), ((), ())), preferred_element_type=jnp.float32
    )


Q_ORDER, K_ORDER, V_ORDER = ("x", "y", "z"), ("y", "z", "x"), ("z", "x", "y")
OUT_ORDER, UP_ORDER, DOWN_ORDER = ("x", "y", "z"), ("y", "z", "x"), ("z", "x", "y")


def on_device(
    tokens,
    qkv_weight,
    out_weight,
    up_weight,
    down_weight,
    ln1_gain,
    ln1_bias,
    q_bias,
    v_bias,
    out_bias,
    ln2_gain,
    ln2_bias,
    up_bias,
    down_bias,
    segment_ids,
    cotangent,
):
    tok_rows = tokens.shape[0]
    width = tokens.shape[1]
    rows = qkv_weight.shape[0]
    hidden_units = up_bias.shape[0]
    f32, bf16 = jnp.float32, jnp.bfloat16

    qkv_orders = (Q_ORDER, K_ORDER, V_ORDER)
    qkv_parts = [
        whole(
            gather_all(qkv_weight[:, i * width : (i + 1) * width], order),
            order,
            ROW_LAYOUT,
            (width, width),
        )
        for i, order in enumerate(qkv_orders)
    ]
    full_out = whole(gather_all(out_weight, OUT_ORDER), OUT_ORDER, ROW_LAYOUT, (width, width))
    full_up = whole(gather_all(up_weight, UP_ORDER), UP_ORDER, UP_LAYOUT, (width, hidden_units))
    full_down = whole(
        gather_all(down_weight, DOWN_ORDER), DOWN_ORDER, DOWN_LAYOUT, (hidden_units, width)
    )

    inputs = tokens.astype(f32)
    normed_one, norm_one_back = jax.vjp(layer_norm, inputs, ln1_gain, ln1_bias)
    normed_one_low = normed_one.astype(bf16)
    projected = [jnp.dot(normed_one_low, part, preferred_element_type=f32) for part in qkv_parts]
    query_blocks = blocked((projected[0] + q_bias).astype(bf16))
    key_blocks = blocked(projected[1].astype(bf16))
    value_blocks = blocked((projected[2] + v_bias).astype(bf16))
    allowed = allowed_pairs(segment_ids)
    scores = masked_scores(query_blocks, key_blocks, allowed)
    row_peak = jnp.max(scores, axis=-1, keepdims=True)
    powers = jnp.exp(scores - row_peak)
    row_total = jnp.sum(powers, axis=-1, keepdims=True)
    probs = powers / row_total
    weights_low = probs.astype(bf16)
    mixed_low = (
        jnp.einsum("bhqk,bkhd->bqhd", weights_low, value_blocks, preferred_element_type=f32)
        .reshape(tok_rows, width)
        .astype(bf16)
    )
    hidden = inputs + jnp.dot(mixed_low, full_out, preferred_element_type=f32) + out_bias
    normed_two, norm_two_back = jax.vjp(layer_norm, hidden, ln2_gain, ln2_bias)
    normed_two_low = normed_two.astype(bf16)
    pre_act = jnp.dot(normed_two_low, full_up, preferred_element_type=f32) + up_bias
    activation, gelu_back = jax.vjp(jax.nn.gelu, pre_act)
    activation_low = activation.astype(bf16)
    output = (
        hidden + jnp.dot(activation_low, full_down, preferred_element_type=f32) + down_bias
    ).astype(bf16)

    down_grad_part = contract_rows(activation_low, cotangent).astype(bf16)
    grad_pre = gelu_back(contract_cols(cotangent, full_down))[0].astype(bf16)
    up_grad_part = contract_rows(normed_two_low, grad_pre).astype(bf16)
    down_grad = scatter_sum(
        pieces_of(down_grad_part, DOWN_ORDER, DOWN_LAYOUT, *down_weight.shape), DOWN_ORDER
    )
    up_grad = scatter_sum(
        pieces_of(up_grad_part, UP_ORDER, UP_LAYOUT, *up_weight.shape), UP_ORDER
    )
    grad_normed_two = contract_cols(grad_pre, full_up)
    up_bias_grad = jnp.sum(grad_pre.astype(f32), axis=0)
    grad_hidden_norm, ln2_gain_grad, ln2_bias_grad = norm_two_back(grad_normed_two)
    grad_out = cotangent.astype(f32)
    grad_hidden = grad_out + grad_hidden_norm
    grad_hidden_low = grad_hidden.astype(bf16)
    out_grad_part = contract_rows(mixed_low, grad_hidden_low).astype(bf16)
    out_grad = scatter_sum(pieces_of(out_grad_part, OUT_ORDER, ROW_LAYOUT, rows, width), OUT_ORDER)
    grad_mixed_blocks = blocked(contract_cols(grad_hidden_low, full_out).astype(bf16))
    grad_probs = jnp.einsum(
        "bqhd,bkhd->bhqk", grad_mixed_blocks, value_blocks, preferred_element_type=f32
    )
    grad_scores = (
        probs * (grad_probs - jnp.sum(probs * grad_probs, axis=-1, keepdims=True))
    ).astype(bf16)
    score_scale = HEAD_DIM ** (-0.5)
    grad_query = (
        (
            jnp.einsum("bhqk,bkhd->bqhd", grad_scores, key_blocks, preferred_element_type=f32)
            * score_scale
        )
        .reshape(tok_rows, width)
        .astype(bf16)
    )
    grad_key = (
        (
            jnp.einsum("bhqk,bqhd->bkhd", grad_scores, query_blocks, preferred_element_type=f32)
            * score_scale
        )
        .reshape(tok_rows, width)
        .astype(bf16)
    )
    grad_value = (
        jnp.einsum("bhqk,bqhd->bkhd", weights_low, grad_mixed_blocks, preferred_element_type=f32)
        .reshape(tok_rows, width)
        .astype(bf16)
    )
    grad_parts = (grad_query, grad_key, grad_value)
    qkv_grad = jnp.concatenate(
        [
            scatter_sum(
                pieces_of(
                    contract_rows(normed_one_low, grad).astype(bf16), order, ROW_LAYOUT, rows, width
                ),
                order,
            )
            for grad, order in zip(grad_parts, qkv_orders)
        ],
        axis=1,
    )
    grad_normed_one = (
        contract_cols(grad_query, qkv_parts[0])
        + contract_cols(grad_key, qkv_parts[1])
        + contract_cols(grad_value, qkv_parts[2])
    )
    grad_input_norm, ln1_gain_grad, ln1_bias_grad = norm_one_back(grad_normed_one)
    grad_tokens = grad_hidden + grad_input_norm
    vectors = (
        ln1_gain_grad,
        ln1_bias_grad,
        jnp.sum(grad_query.astype(f32), axis=0),
        jnp.sum(grad_value.astype(f32), axis=0),
        jnp.sum(grad_hidden, axis=0),
        ln2_gain_grad,
        ln2_bias_grad,
        up_bias_grad,
        jnp.sum(grad_out, axis=0),
    )
    summed = sum_everywhere(jnp.concatenate(vectors).reshape(-1, 128)).reshape(-1)
    cuts, start = [], 0
    for vector in vectors:
        cuts.append(summed[start : start + vector.shape[0]])
        start += vector.shape[0]
    return (output, grad_tokens, qkv_grad, out_grad, up_grad, down_grad, *cuts)


def solution(mesh):
    fine = Mesh(mesh.devices.reshape(4, 2, 2, 4, 2), AXES)
    every, ff, model = AXES, ("z", "yh", "c"), ("x", "yl")
    weights = (P(every, None), P(every, None), P(model, ff), P(ff, model))
    return jax.shard_map(
        on_device,
        mesh=fine,
        in_specs=(P(every, None), *weights, *[P()] * 9, P(every), P(every, None)),
        out_specs=(P(every, None), P(every, None), *weights, *[P()] * 9),
        check_vma=False,
    )
```

time: 2580 us -> 568 us (0.22)
  the two profiles are of different devices: /device:TPU:0 before, /device:TPU:12 now
where the time goes in v1:
time: 568 us; the launch traced here: 557 us
  local copies, waits for them, and re-layouts  204 us (36%)
  starting transfers between devices  119 us (21%)
  matrix products  103 us (18%)
  waiting for transfers between devices  88.5 us (16%)
  other arithmetic  38.4 us (7%)
    ppermute x78, starting transfers between devices, swap_axis(): return lax.ppermute(values, AXES, exchange_pairs(axis, second))  115 us
    ppermute x78, waiting for transfers between devices, swap_axis(): return lax.ppermute(values, AXES, exchange_pairs(axis, second))  88.4 us
    dynamic_update_slice x82, local copies, waits for them, and re-layouts, place_pieces(): out = lax.dynamic_update_index_in_dim(out, piece, slot, 0)  33.3 us
    dot_general x6, matrix products, contract_rows(): lax.dot_general(left, right, (((0,), (0,)), ((), ())), preferred_element_...  30.6 us
    transpose x6, local copies, waits for them, and re-layouts, whole(): return array.transpose([names.index(n) for n in layout]).reshape(shape)  29.7 us
    reshape x2, local copies, waits for them, and re-layouts, pieces_of(): array = array.reshape([sizes[n] for n in layout])  28.8 us
    reshape x2, local copies, waits for them, and re-layouts, whole(): return array.transpose([names.index(n) for n in layout]).reshape(shape)  28.7 us
    dot_general x6, matrix products, contract_cols(): lax.dot_general(left, right, (((1,), (1,)), ((), ())), preferred_element_...  26.8 us
  transfers between devices with their start and end apart: 91, of which 29 were waited for; matrix products, arithmetic and copies ran while one was open for 36% of the time, Pallas kernels for 0%

profile of v1, /device:TPU:12, one launch (start us, length us, event | category | flops | bytes accessed | tf_op | source)
XLA Modules:
  0.0 556.5 jit_solution(8074294573298426782)
XLA Ops:
  15.8 3.9 collective-permute-start.1
  74.5 4.0 collective-permute-done.39
  136.3 5.2 fusion.107
  156.6 6.0 %bitcast_dynamic-update-slice_fusion = bf16[2,4,4,4,256,128]{5,4,3,2,1,0:T(8,128)(2,1)S(1)} fusion(bf16[2,4,4,4,256,128]{5,4,3,2,1,0:T(8,128)(2,1)S(1)} %bitcast_dynamic-update-slice_fusion.1, s32[]{:T(128)S(6)} %select_n.253, bf16[4,4,4,256,128]{4,3,2,1,0:T(8,128)(2,1)} %collective-permute-done.41), kind=kLoop, calls=%fused_computation.23 | loop fusion | bytes 8388612 | tf_op jit(solution)/shard_map/jit(dynamic_update_index_in_dim)/dynamic_update_slice | solution.py:54
  162.6 7.9 %copy.88 = bf16[4,2,2,256,4,2,128]{6,5,4,3,2,1,0:T(2,128)(2,1)} copy(bf16[4,2,2,256,4,2,128]{6,3,0,4,5,1,2:T(8,128)(2,1)S(1)} %bitcast.391) | data formatting | bytes 16777216 | tf_op jit(solution)/shard_map/transpose | solution.py:123
  170.5 14.3 %reshape.376 = bf16[4096,1024]{1,0:T(8,128)(2,1)} reshape(bf16[4,2,2,256,4,2,128]{6,5,4,3,2,1,0:T(2,128)(2,1)} %copy.88) | data formatting | bytes 16777216 | tf_op jit(solution)/shard_map/reshape | solution.py:123
  184.8 4.6 bitcast_dynamic-update-slice_fusion.2
  189.4 16.5 %copy.87 = bf16[4,2,128,4,2,2,256]{6,5,4,3,2,1,0:T(2,128)(2,1)} copy(bf16[4,2,128,4,2,2,256]{6,2,1,4,3,0,5:T(8,128)(2,1)} %bitcast.388) | data formatting | bytes 16777216 | tf_op jit(solution)/shard_map/transpose | solution.py:123
  206.0 14.4 %reshape.374 = bf16[1024,4096]{1,0:T(8,128)(2,1)} reshape(bf16[4,2,128,4,2,2,256]{6,5,4,3,2,1,0:T(2,128)(2,1)} %copy.87) | data formatting | bytes 16777216 | tf_op jit(solution)/shard_map/reshape | solution.py:123
  220.5 10.9 %fusion.96 = f32[512,4096]{1,0:T(8,128)} fusion(bf16[1024,4096]{1,0:T(8,128)(2,1)} %reshape.374, f32[512,1024]{1,0:T(8,128)S(1)} %get-tuple-element.82, f32[1024]{0:T(1024)S(1)} %copy-done.58, f32[1024]{0:T(1024)S(1)} %copy-done.54, f32[512]{0:T(512)S(1)} %fusion.92, f32[512]{0:T(512)S(1)} %broadcast_multiply_fusion), kind=kOutput, calls=%fused_computation.381 | convolution fusion | flops 4297588736 | bytes 18886656 | tf_op jit(solution)/shard_map/dot_general | solution.py:240
  231.4 13.2 %convert_reduce_fusion = (f32[4096]{0:T(1024)S(1)}, bf16[512,4096]{1,0:T(8,128)(2,1)S(1)}) fusion(f32[512,4096]{1,0:T(8,128)} %fusion.96, f32[4096]{0:T(1024)S(1)} %copy-done.55, bf16[4096,1024]{1,0:T(8,128)(2,1)} %reshape.376, bf16[512,1024]{1,0:T(8,128)(2,1)S(1)} %copy-done.29), kind=kOutput, calls=%fused_computation.19 | convolution fusion | flops 4343197696 | bytes 22052864 | tf_op jit(solution)/shard_map/dot_general | solution.py:169
  244.6 5.0 multiply_reduce_fusion.1
  254.1 4.0 reshape.400
  261.9 5.2 convert_reduce_fusion.3
  282.2 7.5 %convolution_convert_fusion.1 = bf16[1024,4096]{1,0:T(8,128)(2,1)} fusion(bf16[512,4096]{1,0:T(8,128)(2,1)S(1)} %copy-done.62, f32[512,1024]{1,0:T(8,128)S(1)} %get-tuple-element.82, f32[1024]{0:T(1024)S(1)} %copy-done.58, f32[1024]{0:T(1024)S(1)} %copy-done.54, f32[512]{0:T(512)S(1)} %fusion.92, f32[512]{0:T(512)S(1)} %broadcast_multiply_fusion), kind=kOutput, calls=%fused_computation.22 | convolution fusion | flops 4301783040 | bytes 14692352 | tf_op jit(solution)/shard_map/dot_general | solution.py:163
  289.6 13.3 %convolution_convert_fusion = bf16[4096,1024]{1,0:T(8,128)(2,1)} fusion(bf16[512,1024]{1,0:T(8,128)(2,1)S(1)} %copy-done.30, f32[512,4096]{1,0:T(8,128)} %fusion.96, f32[4096]{0:T(1024)S(1)} %copy-done.55), kind=kOutput, calls=%fused_computation.21 | convolution fusion | flops 4320133120 | bytes 17842176 | tf_op jit(solution)/shard_map/dot_general | solution.py:163
  303.0 10.0 %add_convert_fusion.2 = bf16[512,1024]{1,0:T(8,128)(2,1)} fusion(f32[512,1024]{1,0:T(8,128)S(1)} %get-tuple-element.82, bf16[4096,1024]{1,0:T(8,128)(2,1)S(1)} %bitcast.395, f32[1024]{0:T(1024)S(1)} %copy-done.59, f32[512,4096]{1,0:T(8,128)} %fusion.96, f32[4096]{0:T(1024)S(1)} %copy-done.55), kind=kOutput, calls=%fused_computation.79 | convolution fusion | flops 4317511680 | bytes 19943424 | tf_op jit(solution)/shard_map/dot_general | solution.py:244
  344.6 14.5 %reshape.386 = bf16[4,2,128,4,2,2,256]{6,5,4,3,2,1,0:T(2,128)(2,1)} reshape(bf16[1024,4096]{1,0:T(8,128)(2,1)} %convolution_convert_fusion.1) | data formatting | bytes 16777216 | tf_op jit(solution)/shard_map/reshape | solution.py:128
  359.1 9.8 %copy.105 = bf16[2,4,4,2,2,128,256]{6,5,4,3,2,1,0:T(8,128)(2,1)} copy(bf16[2,4,4,2,2,128,256]{6,0,3,2,5,4,1:T(2,128)(2,1)} %bitcast.389) | data formatting | bytes 16777216 | tf_op jit(solution)/shard_map/transpose | solution.py:133
  370.8 4.7 dynamic-slice_bitcast_fusion.1
  375.5 14.3 %reshape.388 = bf16[4,2,2,256,4,2,128]{6,5,4,3,2,1,0:T(2,128)(2,1)} reshape(bf16[4096,1024]{1,0:T(8,128)(2,1)} %convolution_convert_fusion) | data formatting | bytes 16777216 | tf_op jit(solution)/shard_map/reshape | solution.py:128
  389.8 8.9 %copy.106 = bf16[2,2,2,4,4,256,128]{6,5,4,3,2,1,0:T(8,128)(2,1)} copy(bf16[2,2,2,4,4,256,128]{6,2,3,5,0,1,4:T(2,128)(2,1)} %bitcast.390) | data formatting | bytes 16777216 | tf_op jit(solution)/shard_map/transpose | solution.py:133
  398.9 4.9 dynamic-slice_bitcast_fusion
  419.9 3.8 collective-permute-start.58
  444.4 7.4 %collective-permute-start.46 = (bf16[4,8,1024]{2,1,0:T(8,128)(2,1)}, bf16[4,8,1024]{2,1,0:T(8,128)(2,1)}, u32[]{:S(2)}, u32[]{:S(2)}) collective-permute-start(bf16[4,8,1024]{2,1,0:T(8,128)(2,1)} %fusion.81), channel_id=1, source_target_pairs={{0,1},{2,3},{4,5},{6,7},{8,25},{10,27},{12,29},{14,31},{1,0},{3,2}... | collective-permute-start | bytes 196616 | tf_op jit(solution)/shard_map/ppermute | solution.py:32
  455.4 4.0 fusion.9
  463.8 3.8 fusion.8
  475.0 20.9 %collective-permute-done.54 = bf16[2,8,1024]{2,1,0:T(8,128)(2,1)S(1)} collective-permute-done((bf16[2,8,1024]{2,1,0:T(8,128)(2,1)S(1)}, bf16[2,8,1024]{2,1,0:T(8,128)(2,1)S(1)}, u32[]{:S(2)}, u32[]{:S(2)}) %collective-permute-start.54) | collective-permute-done | bytes 32800 | tf_op jit(solution)/shard_map/ppermute | solution.py:32
  499.3 4.7 collective-permute-start.48
  507.8 17.1 %collective-permute-done.72 = bf16[4,4,128,256]{3,2,1,0:T(8,128)(2,1)S(1)} collective-permute-done((bf16[4,4,128,256]{3,2,1,0:T(8,128)(2,1)S(1)}, bf16[4,4,128,256]{3,2,1,0:T(8,128)(2,1)S(1)}, u32[]{:S(2)}, u32[]{:S(2)}) %collective-permute-start.72) | collective-permute-done | bytes 1048608 | tf_op jit(solution)/shard_map/ppermute | solution.py:32
  529.1 7.2 %collective-permute-done.73 = bf16[2,4,128,256]{3,2,1,0:T(8,128)(2,1)S(1)} collective-permute-done((bf16[2,4,128,256]{3,2,1,0:T(8,128)(2,1)S(1)}, bf16[2,4,128,256]{3,2,1,0:T(8,128)(2,1)S(1)}, u32[]{:S(2)}, u32[]{:S(2)}) %collective-permute-start.73) | collective-permute-done | bytes 524320 | tf_op jit(solution)/shard_map/ppermute | solution.py:32
  539.0 3.8 collective-permute-done.74
  (595 shorter events, 277.0 us)
Async XLA Ops:
  4.1 19.4 %collective-permute-start.35 = (bf16[256,128]{1,0:T(8,128)(2,1)}, bf16[256,128]{1,0:T(8,128)(2,1)S(1)}, u32[]{:S(2)}, u32[]{:S(2)}) collective-permute-start(bf16[256,128]{1,0:T(8,128)(2,1)} %param.20), channel_id=1, source_target_pairs={{0,32},{2,34},{4,36},{6,38},{8,104},{10,106},{12,108},{14,110},{1,... | collective-permute-start | bytes 196616 | tf_op jit(solution)/shard_map/ppermute | solution.py:32
  6.0 20.0 %collective-permute-start.28 = (bf16[128,256]{1,0:T(8,128)(2,1)}, bf16[128,256]{1,0:T(8,128)(2,1)S(1)}, u32[]{:S(2)}, u32[]{:S(2)}) collective-permute-start(bf16[128,256]{1,0:T(8,128)(2,1)} %param.19), channel_id=1, source_target_pairs={{0,1},{2,3},{4,5},{6,7},{8,25},{10,27},{12,29},{14,31},{1,0},{3,2}... | collective-permute-start | bytes 196616 | tf_op jit(solution)/shard_map/ppermute | solution.py:32
  46.3 16.4 %collective-permute-start.31 = (bf16[2,4,128,256]{3,2,1,0:T(8,128)(2,1)S(1)}, bf16[2,4,128,256]{3,2,1,0:T(8,128)(2,1)S(1)}, u32[]{:S(2)}, u32[]{:S(2)}) collective-permute-start(bf16[2,4,128,256]{3,2,1,0:T(8,128)(2,1)S(1)} %pad_maximum_fusion.8), channel_id=1, source_target_pairs={{0,96},{2,98},{4,100},{6,102},{8,40},{10,42},{12,44},{14,46},{1,97... | collective-permute-start | bytes 1572872 | tf_op jit(solution)/shard_map/ppermute | solution.py:32
  49.7 19.6 %collective-permute-start.26 = (bf16[2,4,4,8,1024]{4,3,2,1,0:T(8,128)(2,1)S(1)}, bf16[2,4,4,8,1024]{4,3,2,1,0:T(8,128)(2,1)S(1)}, u32[]{:S(2)}, u32[]{:S(2)}) collective-permute-start(bf16[2,4,4,8,1024]{4,3,2,1,0:T(8,128)(2,1)S(1)} %pad_maximum_fusion.7), channel_id=1, source_target_pairs={{0,96},{2,98},{4,100},{6,102},{8,40},{10,42},{12,44},{14,46},{1,97... | collective-permute-start | bytes 1572872 | tf_op jit(solution)/shard_map/ppermute | solution.py:32
  51.9 20.5 %collective-permute-start.19 = (bf16[2,4,4,8,1024]{4,3,2,1,0:T(8,128)(2,1)S(1)}, bf16[2,4,4,8,1024]{4,3,2,1,0:T(8,128)(2,1)S(1)}, u32[]{:S(2)}, u32[]{:S(2)}) collective-permute-start(bf16[2,4,4,8,1024]{4,3,2,1,0:T(8,128)(2,1)S(1)} %pad_maximum_fusion.6), channel_id=1, source_target_pairs={{0,6},{2,4},{4,2},{6,0},{8,10},{10,8},{12,14},{14,12},{1,7},{3,5},... | collective-permute-start | bytes 1572872 | tf_op jit(solution)/shard_map/ppermute | solution.py:32
  53.6 19.4 %collective-permute-start.12 = (bf16[2,4,4,8,1024]{4,3,2,1,0:T(8,128)(2,1)S(1)}, bf16[2,4,4,8,1024]{4,3,2,1,0:T(8,128)(2,1)S(1)}, u32[]{:S(2)}, u32[]{:S(2)}) collective-permute-start(bf16[2,4,4,8,1024]{4,3,2,1,0:T(8,128)(2,1)S(1)} %pad_maximum_fusion.5), channel_id=1, source_target_pairs={{0,96},{2,98},{4,100},{6,102},{8,40},{10,42},{12,44},{14,46},{1,97... | collective-permute-start | bytes 1572872 | tf_op jit(solution)/shard_map/ppermute | solution.py:32
  57.2 16.8 %collective-permute-start.5 = (bf16[2,4,4,8,1024]{4,3,2,1,0:T(8,128)(2,1)S(1)}, bf16[2,4,4,8,1024]{4,3,2,1,0:T(8,128)(2,1)S(1)}, u32[]{:S(2)}, u32[]{:S(2)}) collective-permute-start(bf16[2,4,4,8,1024]{4,3,2,1,0:T(8,128)(2,1)S(1)} %pad_maximum_fusion.4), channel_id=1, source_target_pairs={{0,17},{2,19},{4,21},{6,23},{8,9},{10,11},{12,13},{14,15},{1,16},{... | collective-permute-start | bytes 1572872 | tf_op jit(solution)/shard_map/ppermute | solution.py:32
  69.3 15.9 %collective-permute-start.32 = (bf16[4,4,128,256]{3,2,1,0:T(8,128)(2,1)S(1)}, bf16[4,4,128,256]{3,2,1,0:T(8,128)(2,1)S(1)}, u32[]{:S(2)}, u32[]{:S(2)}) collective-permute-start(bf16[4,4,128,256]{3,2,1,0:T(8,128)(2,1)S(1)} %slice_dynamic-update-slice_fusion.6), channel_id=1, source_target_pairs={{0,2},{2,0},{4,6},{6,4},{8,14},{10,12},{12,10},{14,8},{1,3},{3,1},... | collective-permute-start | bytes 3145736 | tf_op jit(solution)/shard_map/ppermute | solution.py:32
  74.0 17.2 %collective-permute-start.13 = (bf16[4,4,4,8,1024]{4,3,2,1,0:T(8,128)(2,1)S(1)}, bf16[4,4,4,8,1024]{4,3,2,1,0:T(8,128)(2,1)S(1)}, u32[]{:S(2)}, u32[]{:S(2)}) collective-permute-start(bf16[4,4,4,8,1024]{4,3,2,1,0:T(8,128)(2,1)S(1)} %slice_dynamic-update-slice_fusion.12), channel_id=1, source_target_pairs={{0,8},{8,0},{1,9},{9,1},{2,10},{10,2},{3,11},{11,3},{4,12},{12,4},... | collective-permute-start | bytes 3145736 | tf_op jit(solution)/shard_map/ppermute | solution.py:36
  80.0 26.8 %collective-permute-start.40 = (bf16[2,4,4,256,128]{4,3,2,1,0:T(8,128)(2,1)}, bf16[2,4,4,256,128]{4,3,2,1,0:T(8,128)(2,1)}, u32[]{:S(2)}, u32[]{:S(2)}) collective-permute-start(bf16[2,4,4,256,128]{4,3,2,1,0:T(8,128)(2,1)} %pad_maximum_fusion.1), channel_id=1, source_target_pairs={{0,17},{2,19},{4,21},{6,23},{8,9},{10,11},{12,13},{14,15},{1,16},{... | collective-permute-start | bytes 6291464 | tf_op jit(solution)/shard_map/ppermute | solution.py:32
  86.7 26.4 %collective-permute-start.33 = (bf16[2,4,4,128,256]{4,3,2,1,0:T(8,128)(2,1)}, bf16[2,4,4,128,256]{4,3,2,1,0:T(8,128)(2,1)}, u32[]{:S(2)}, u32[]{:S(2)}) collective-permute-start(bf16[2,4,4,128,256]{4,3,2,1,0:T(8,128)(2,1)} %pad_maximum_fusion), channel_id=1, source_target_pairs={{0,6},{2,4},{4,2},{6,0},{8,10},{10,8},{12,14},{14,12},{1,7},{3,5},... | collective-permute-start | bytes 6291464 | tf_op jit(solution)/shard_map/ppermute | solution.py:32
  111.5 45.1 %collective-permute-start.41 = (bf16[4,4,4,256,128]{4,3,2,1,0:T(8,128)(2,1)}, bf16[4,4,4,256,128]{4,3,2,1,0:T(8,128)(2,1)}, u32[]{:S(2)}, u32[]{:S(2)}) collective-permute-start(bf16[4,4,4,256,128]{4,3,2,1,0:T(8,128)(2,1)} %slice_dynamic-update-slice_fusion), channel_id=1, source_target_pairs={{0,8},{8,0},{1,9},{9,1},{2,10},{10,2},{3,11},{11,3},{4,12},{12,4},... | collective-permute-start | bytes 12582920 | tf_op jit(solution)/shard_map/ppermute | solution.py:36
  117.6 67.2 %collective-permute-start.34 = (bf16[4,4,4,128,256]{4,3,2,1,0:T(8,128)(2,1)}, bf16[4,4,4,128,256]{4,3,2,1,0:T(8,128)(2,1)}, u32[]{:S(2)}, u32[]{:S(2)}) collective-permute-start(bf16[4,4,4,128,256]{4,3,2,1,0:T(8,128)(2,1)} %slice_dynamic-update-slice_fusion.2), channel_id=1, source_target_pairs={{0,8},{8,0},{1,9},{9,1},{2,10},{10,2},{3,11},{11,3},{4,12},{12,4},... | collective-permute-start | bytes 12582920 | tf_op jit(solution)/shard_map/ppermute | solution.py:36
  331.7 73.7 %collective-permute-start.56 = (bf16[4,4,4,8,1024]{4,3,2,1,0:T(8,128)(2,1)}, bf16[4,4,4,8,1024]{4,3,2,1,0:T(8,128)(2,1)}, u32[]{:S(2)}, u32[]{:S(2)}) collective-permute-start(bf16[4,4,4,8,1024]{4,3,2,1,0:T(8,128)(2,1)} %dynamic-slice_bitcast_fusion.3), channel_id=1, source_target_pairs={{0,8},{8,0},{1,9},{9,1},{2,10},{10,2},{3,11},{11,3},{4,12},{12,4},... | collective-permute-start | bytes 3145736 | tf_op jit(solution)/shard_map/ppermute | solution.py:36
  337.7 69.7 %collective-permute-start.49 = (bf16[4,4,4,8,1024]{4,3,2,1,0:T(8,128)(2,1)}, bf16[4,4,4,8,1024]{4,3,2,1,0:T(8,128)(2,1)}, u32[]{:S(2)}, u32[]{:S(2)}) collective-permute-start(bf16[4,4,4,8,1024]{4,3,2,1,0:T(8,128)(2,1)} %dynamic-slice_bitcast_fusion.4), channel_id=1, source_target_pairs={{0,8},{8,0},{1,9},{9,1},{2,10},{10,2},{3,11},{11,3},{4,12},{12,4},... | collective-permute-start | bytes 3145736 | tf_op jit(solution)/shard_map/ppermute | solution.py:36
  342.3 68.3 %collective-permute-start.42 = (bf16[4,4,4,8,1024]{4,3,2,1,0:T(8,128)(2,1)}, bf16[4,4,4,8,1024]{4,3,2,1,0:T(8,128)(2,1)}, u32[]{:S(2)}, u32[]{:S(2)}) collective-permute-start(bf16[4,4,4,8,1024]{4,3,2,1,0:T(8,128)(2,1)} %dynamic-slice_bitcast_fusion.5), channel_id=1, source_target_pairs={{0,8},{8,0},{1,9},{9,1},{2,10},{10,2},{3,11},{11,3},{4,12},{12,4},... | collective-permute-start | bytes 3145736 | tf_op jit(solution)/shard_map/ppermute | solution.py:36
  343.4 25.6 %collective-permute-start.88 = (f32[96,128]{1,0:T(8,128)S(1)}, f32[96,128]{1,0:T(8,128)S(1)}, u32[]{:S(2)}, u32[]{:S(2)}) collective-permute-start(f32[96,128]{1,0:T(8,128)S(1)} %add.729), channel_id=1, source_target_pairs={{0,32},{2,34},{4,36},{6,38},{8,104},{10,106},{12,108},{14,110},{1,... | collective-permute-start | bytes 147464 | tf_op jit(solution)/shard_map/ppermute | solution.py:32
  344.0 68.6 %collective-permute-start.63 = (bf16[4,4,4,8,1024]{4,3,2,1,0:T(8,128)(2,1)S(1)}, bf16[4,4,4,8,1024]{4,3,2,1,0:T(8,128)(2,1)}, u32[]{:S(2)}, u32[]{:S(2)}) collective-permute-start(bf16[4,4,4,8,1024]{4,3,2,1,0:T(8,128)(2,1)S(1)} %dynamic-slice_bitcast_fusion.2), channel_id=1, source_target_pairs={{0,8},{8,0},{1,9},{9,1},{2,10},{10,2},{3,11},{11,3},{4,12},{12,4},... | collective-permute-start | bytes 3145736 | tf_op jit(solution)/shard_map/ppermute | solution.py:36
  369.0 29.8 %collective-permute-start.89 = (f32[96,128]{1,0:T(8,128)S(1)}, f32[96,128]{1,0:T(8,128)S(1)}, u32[]{:S(2)}, u32[]{:S(2)}) collective-permute-start(f32[96,128]{1,0:T(8,128)S(1)} %add.730), channel_id=1, source_target_pairs={{0,96},{2,98},{4,100},{6,102},{8,40},{10,42},{12,44},{14,46},{1,97... | collective-permute-start | bytes 147464 | tf_op jit(solution)/shard_map/ppermute | solution.py:32
  403.7 51.7 %collective-permute-start.70 = (bf16[4,4,4,128,256]{4,3,2,1,0:T(8,128)(2,1)S(1)}, bf16[4,4,4,128,256]{4,3,2,1,0:T(8,128)(2,1)}, u32[]{:S(2)}, u32[]{:S(2)}) collective-permute-start(bf16[4,4,4,128,256]{4,3,2,1,0:T(8,128)(2,1)S(1)} %copy-done.16), channel_id=1, source_target_pairs={{0,8},{8,0},{1,9},{9,1},{2,10},{10,2},{3,11},{11,3},{4,12},{12,4},... | collective-permute-start | bytes 12582920 | tf_op jit(solution)/shard_map/ppermute | solution.py:36
  405.5 58.3 %collective-permute-start.77 = (bf16[4,4,4,256,128]{4,3,2,1,0:T(8,128)(2,1)}, bf16[4,4,4,256,128]{4,3,2,1,0:T(8,128)(2,1)}, u32[]{:S(2)}, u32[]{:S(2)}) collective-permute-start(bf16[4,4,4,256,128]{4,3,2,1,0:T(8,128)(2,1)} %dynamic-slice_bitcast_fusion), channel_id=1, source_target_pairs={{0,8},{8,0},{1,9},{9,1},{2,10},{10,2},{3,11},{11,3},{4,12},{12,4},... | collective-permute-start | bytes 12582920 | tf_op jit(solution)/shard_map/ppermute | solution.py:36
  444.4 24.0 %collective-permute-start.46 = (bf16[4,8,1024]{2,1,0:T(8,128)(2,1)}, bf16[4,8,1024]{2,1,0:T(8,128)(2,1)}, u32[]{:S(2)}, u32[]{:S(2)}) collective-permute-start(bf16[4,8,1024]{2,1,0:T(8,128)(2,1)} %fusion.81), channel_id=1, source_target_pairs={{0,1},{2,3},{4,5},{6,7},{8,25},{10,27},{12,29},{14,31},{1,0},{3,2}... | collective-permute-start | bytes 196616 | tf_op jit(solution)/shard_map/ppermute | solution.py:32
  452.5 18.7 %collective-permute-start.67 = (bf16[4,8,1024]{2,1,0:T(8,128)(2,1)}, bf16[4,8,1024]{2,1,0:T(8,128)(2,1)}, u32[]{:S(2)}, u32[]{:S(2)}) collective-permute-start(bf16[4,8,1024]{2,1,0:T(8,128)(2,1)} %fusion.84), channel_id=1, source_target_pairs={{0,1},{2,3},{4,5},{6,7},{8,25},{10,27},{12,29},{14,31},{1,0},{3,2}... | collective-permute-start | bytes 196616 | tf_op jit(solution)/shard_map/ppermute | solution.py:32
  454.0 18.2 %collective-permute-start.61 = (bf16[2,8,1024]{2,1,0:T(8,128)(2,1)}, bf16[2,8,1024]{2,1,0:T(8,128)(2,1)}, u32[]{:S(2)}, u32[]{:S(2)}) collective-permute-start(bf16[2,8,1024]{2,1,0:T(8,128)(2,1)} %pad_maximum_fusion.35), channel_id=1, source_target_pairs={{0,96},{2,98},{4,100},{6,102},{8,40},{10,42},{12,44},{14,46},{1,97... | collective-permute-start | bytes 98312 | tf_op jit(solution)/shard_map/ppermute | solution.py:32
  461.1 38.2 %collective-permute-start.71 = (bf16[2,4,4,128,256]{4,3,2,1,0:T(8,128)(2,1)}, bf16[2,4,4,128,256]{4,3,2,1,0:T(8,128)(2,1)S(1)}, u32[]{:S(2)}, u32[]{:S(2)}) collective-permute-start(bf16[2,4,4,128,256]{4,3,2,1,0:T(8,128)(2,1)} %pad_maximum_fusion.2), channel_id=1, source_target_pairs={{0,6},{2,4},{4,2},{6,0},{8,10},{10,8},{12,14},{14,12},{1,7},{3,5},... | collective-permute-start | bytes 6291464 | tf_op jit(solution)/shard_map/ppermute | solution.py:32
  468.1 36.4 %collective-permute-start.78 = (bf16[2,4,4,256,128]{4,3,2,1,0:T(8,128)(2,1)S(1)}, bf16[2,4,4,256,128]{4,3,2,1,0:T(8,128)(2,1)S(1)}, u32[]{:S(2)}, u32[]{:S(2)}) collective-permute-start(bf16[2,4,4,256,128]{4,3,2,1,0:T(8,128)(2,1)S(1)} %pad_maximum_fusion.3), channel_id=1, source_target_pairs={{0,17},{2,19},{4,21},{6,23},{8,9},{10,11},{12,13},{14,15},{1,16},{... | collective-permute-start | bytes 6291464 | tf_op jit(solution)/shard_map/ppermute | solution.py:32
  468.4 27.5 %collective-permute-start.54 = (bf16[2,8,1024]{2,1,0:T(8,128)(2,1)S(1)}, bf16[2,8,1024]{2,1,0:T(8,128)(2,1)S(1)}, u32[]{:S(2)}, u32[]{:S(2)}) collective-permute-start(bf16[2,8,1024]{2,1,0:T(8,128)(2,1)S(1)} %pad_maximum_fusion.34), channel_id=1, source_target_pairs={{0,17},{2,19},{4,21},{6,23},{8,9},{10,11},{12,13},{14,15},{1,16},{... | collective-permute-start | bytes 98312 | tf_op jit(solution)/shard_map/ppermute | solution.py:32
  471.2 24.8 %collective-permute-start.47 = (bf16[2,8,1024]{2,1,0:T(8,128)(2,1)S(1)}, bf16[2,8,1024]{2,1,0:T(8,128)(2,1)S(1)}, u32[]{:S(2)}, u32[]{:S(2)}) collective-permute-start(bf16[2,8,1024]{2,1,0:T(8,128)(2,1)S(1)} %pad_maximum_fusion.33), channel_id=1, source_target_pairs={{0,6},{2,4},{4,2},{6,0},{8,10},{10,8},{12,14},{14,12},{1,7},{3,5},... | collective-permute-start | bytes 98312 | tf_op jit(solution)/shard_map/ppermute | solution.py:32
  472.2 32.2 %collective-permute-start.68 = (bf16[2,8,1024]{2,1,0:T(8,128)(2,1)S(1)}, bf16[2,8,1024]{2,1,0:T(8,128)(2,1)S(1)}, u32[]{:S(2)}, u32[]{:S(2)}) collective-permute-start(bf16[2,8,1024]{2,1,0:T(8,128)(2,1)S(1)} %pad_maximum_fusion.36), channel_id=1, source_target_pairs={{0,6},{2,4},{4,2},{6,0},{8,10},{10,8},{12,14},{14,12},{1,7},{3,5},... | collective-permute-start | bytes 98312 | tf_op jit(solution)/shard_map/ppermute | solution.py:32
  504.4 20.5 %collective-permute-start.72 = (bf16[4,4,128,256]{3,2,1,0:T(8,128)(2,1)S(1)}, bf16[4,4,128,256]{3,2,1,0:T(8,128)(2,1)S(1)}, u32[]{:S(2)}, u32[]{:S(2)}) collective-permute-start(bf16[4,4,128,256]{3,2,1,0:T(8,128)(2,1)S(1)} %fusion.39), channel_id=1, source_target_pairs={{0,2},{2,0},{4,6},{6,4},{8,14},{10,12},{12,10},{14,8},{1,3},{3,1},... | collective-permute-start | bytes 3145736 | tf_op jit(solution)/shard_map/ppermute | solution.py:32
  504.5 32.9 %collective-permute-start.69 = (bf16[8,1024]{1,0:T(8,128)(2,1)S(1)}, bf16[8,1024]{1,0:T(8,128)(2,1)S(1)}, u32[]{:S(2)}, u32[]{:S(2)}) collective-permute-start(bf16[8,1024]{1,0:T(8,128)(2,1)S(1)} %fusion.90), channel_id=1, source_target_pairs={{0,2},{2,0},{4,6},{6,4},{8,14},{10,12},{12,10},{14,8},{1,3},{3,1},... | collective-permute-start | bytes 49160 | tf_op jit(solution)/shard_map/ppermute | solution.py:32
  506.9 20.9 %collective-permute-start.79 = (bf16[4,4,256,128]{3,2,1,0:T(8,128)(2,1)S(1)}, bf16[4,4,256,128]{3,2,1,0:T(8,128)(2,1)S(1)}, u32[]{:S(2)}, u32[]{:S(2)}) collective-permute-start(bf16[4,4,256,128]{3,2,1,0:T(8,128)(2,1)S(1)} %fusion.40), channel_id=1, source_target_pairs={{0,1},{2,3},{4,5},{6,7},{8,25},{10,27},{12,29},{14,31},{1,0},{3,2}... | collective-permute-start | bytes 3145736 | tf_op jit(solution)/shard_map/ppermute | solution.py:32
  (130 other events, 996.4 us)

commit v2 on v1

v2 whole, which is shorter than its diff:
```python
import functools
import itertools

import jax
import jax.numpy as jnp
from jax import lax
from jax.experimental import pallas as pl
from jax.experimental.pallas import tpu as pltpu
from jax.sharding import Mesh, PartitionSpec as P

F32, BF16 = jnp.float32, jnp.bfloat16
TOK, WIDTH, FF = 512, 1024, 4096
CHUNK = 1024
UNIT = 256
ROOT = 0.7978845608028654
CUBE = 0.044715


def dot(a, b):
    return lax.dot_general(a, b, (((1,), (0,)), ((), ())), preferred_element_type=F32)


def dot_t(a, b):
    return lax.dot_general(a, b, (((1,), (1,)), ((), ())), preferred_element_type=F32)


def strides(order):
    return {axis: 4**i for i, axis in enumerate(order)}


def tile_index(slots, side, order, x, y, z):
    step = strides(order)
    return (
        slots[side * 12 + x] * step["x"]
        + slots[side * 12 + 4 + y] * step["y"]
        + slots[side * 12 + 8 + z] * step["z"]
    )


def ffn_kernel(up_order, down_order, slots, low_ref, grad_ref, hidden_ref, gain_ref, down_bias_ref, bias_ref,
               up_own, up_other, down_own, down_other,
               out_ref, grad_hidden_ref, grad_low_ref, bias_grad_ref, vec_ref, dup_own, dup_other, ddown_own, ddown_other,
               up_buf, down_buf, dup_buf, ddown_buf, low_t, act_buf, gpre_buf, total, grad_total,
               up_sem, down_sem, dup_sem, ddown_sem):
    core = slots[24]

    def tiles(chunk):
        for side in (0, 1):
            for yh in (0, 1):
                for x in range(4):
                    for yl in (0, 1):
                        at_up = tile_index(slots, side, up_order, x, yh * 2 + yl, chunk)
                        at_down = tile_index(slots, side, down_order, x, yh * 2 + yl, chunk)
                        model = pl.ds((x * 2 + yl) * 128, 128)
                        unit = pl.ds((side * 2 + yh) * UNIT, UNIT)
                        yield side, at_up, at_down, model, unit

    def fetch(chunk, slot):
        for side, at_up, at_down, model, unit in tiles(chunk):
            pltpu.make_async_copy((up_own, up_other)[side].at[at_up], up_buf.at[slot, model, unit], up_sem.at[slot]).start()
            pltpu.make_async_copy((down_own, down_other)[side].at[at_down], down_buf.at[slot, unit, model], down_sem.at[slot]).start()

    def send(chunk, slot):
        for side, at_up, at_down, model, unit in tiles(chunk):
            pltpu.make_async_copy(dup_buf.at[slot, model, unit], (dup_own, dup_other)[side].at[at_up], dup_sem.at[slot]).start()
            pltpu.make_async_copy(ddown_buf.at[slot, unit, model], (ddown_own, ddown_other)[side].at[at_down], ddown_sem.at[slot]).start()

    def wait(buf, sem, slot):
        pltpu.make_async_copy(buf.at[slot], buf.at[slot], sem.at[slot]).wait()

    fetch(0, 0)
    low_t[...] = low_ref[...].T
    total[...] = jnp.zeros_like(total)
    grad_total[...] = jnp.zeros_like(grad_total)

    @pl.loop(0, 4)
    def _(chunk):
        slot = lax.rem(chunk, 2)

        @pl.when(chunk < 3)
        def _():
            fetch(chunk + 1, 1 - slot)

        wait(up_buf, up_sem, slot)
        wait(down_buf, down_sem, slot)

        @pl.when(chunk >= 2)
        def _():
            wait(dup_buf, dup_sem, slot)
            wait(ddown_buf, ddown_sem, slot)

        for n in range(CHUNK // UNIT):
            cols = slice(n * UNIT, (n + 1) * UNIT)
            side, yh = n // 2, n % 2
            block = (chunk * 2 + yh) * 2 + (core if side == 0 else 1 - core)
            pre = dot(low_ref[...], up_buf[slot, :, cols]) + bias_ref[block]
            gact = dot_t(grad_ref[...], down_buf[slot, cols, :])
            square = pre * pre
            bend = jnp.tanh(ROOT * (pre + CUBE * square * pre))
            half = 0.5 + 0.5 * bend
            act = (pre * half).astype(BF16)
            slope = half + 0.5 * pre * (1.0 - bend * bend) * (ROOT + 3.0 * ROOT * CUBE * square)
            gpre = (gact * slope).astype(BF16)
            act_buf[:, cols] = act
            gpre_buf[:, cols] = gpre
            bias_grad_ref[block] = jnp.sum(gpre.astype(F32), axis=0, keepdims=True)
            ddown_buf[slot, cols, :] = dot(act.T, grad_ref[...]).astype(BF16)
            dup_buf[slot, :, cols] = dot(low_t[...], gpre).astype(BF16)
        send(chunk, slot)
        total[...] += dot(act_buf[...], down_buf[slot])
        grad_total[...] += dot_t(gpre_buf[...], up_buf[slot])

    gain = gain_ref[...]
    vec_ref[...] = jnp.zeros_like(vec_ref)

    @pl.loop(0, TOK // 128)
    def _(part):
        rows = pl.ds(part * 128, 128)
        hidden = hidden_ref[rows, :]
        out_ref[rows, :] = (hidden + total[rows, :] + down_bias_ref[...]).astype(BF16)
        center = hidden - jnp.mean(hidden, axis=-1, keepdims=True)
        scale = lax.rsqrt(jnp.mean(center * center, axis=-1, keepdims=True) + 1e-05)
        norm = center * scale
        gc = grad_total[rows, :]
        edge = gc * gain
        back = (edge - jnp.mean(edge, axis=-1, keepdims=True) - norm * jnp.mean(edge * norm, axis=-1, keepdims=True)) * scale
        gout = grad_ref[rows, :].astype(F32)
        ghid = gout + back
        grad_hidden_ref[rows, :] = ghid
        grad_low_ref[rows, :] = ghid.astype(BF16)
        vec_ref[0:1, :] += jnp.sum(ghid, axis=0, keepdims=True)
        vec_ref[1:2, :] += jnp.sum(gc * norm, axis=0, keepdims=True)
        vec_ref[2:3, :] += jnp.sum(gc, axis=0, keepdims=True)
        vec_ref[3:4, :] += jnp.sum(gout, axis=0, keepdims=True)

    for slot in (0, 1):
        wait(dup_buf, dup_sem, slot)
        wait(ddown_buf, ddown_sem, slot)


def ffn(slots, low, grad, hidden, gain, down_bias, up_bias, up_own, up_other, down_own, down_other, up_order, down_order):
    vmem, anywhere = pl.BlockSpec(memory_space=pltpu.VMEM), pl.BlockSpec(memory_space=pl.ANY)
    tile_u, tile_d = jax.ShapeDtypeStruct((64, 128, 256), BF16), jax.ShapeDtypeStruct((64, 256, 128), BF16)
    big = pltpu.VMEM((2, 1024, 1024), BF16)
    sem = pltpu.SemaphoreType.DMA((2,))
    return pl.pallas_call(
        functools.partial(ffn_kernel, up_order, down_order),
        in_specs=[pl.BlockSpec(memory_space=pltpu.SMEM)] + [vmem] * 6 + [anywhere] * 4,
        out_specs=[vmem] * 5 + [anywhere] * 4,
        out_shape=[
            jax.ShapeDtypeStruct((TOK, WIDTH), BF16),
            jax.ShapeDtypeStruct((TOK, WIDTH), F32),
            jax.ShapeDtypeStruct((TOK, WIDTH), BF16),
            jax.ShapeDtypeStruct((16, 1, UNIT), F32),
            jax.ShapeDtypeStruct((8, WIDTH), F32),
            tile_u, tile_u, tile_d, tile_d,
        ],
        scratch_shapes=[
            big, big, big, big,
            pltpu.VMEM((WIDTH, TOK), BF16),
            pltpu.VMEM((TOK, CHUNK), BF16),
            pltpu.VMEM((TOK, CHUNK), BF16),
            pltpu.VMEM((TOK, WIDTH), F32),
            pltpu.VMEM((TOK, WIDTH), F32),
            sem, sem, sem, sem,
        ],
        compiler_params=pltpu.CompilerParams(vmem_limit_bytes=48 * 2**20),
        cost_estimate=pl.CostEstimate(flops=6 * 2 * TOK * WIDTH * FF, bytes_accessed=40 * 2**20, transcendentals=TOK * FF),
        name="ffn",
    )(slots, low, grad, hidden, gain.reshape(1, WIDTH), down_bias.reshape(1, WIDTH), up_bias.reshape(16, 1, UNIT),
      up_own, up_other, down_own, down_other)


BLOCK = 128
HALF = 512
PART = 3 * HALF
ORDERS = (("y", "x", "z"), ("y", "z", "x"))


def part_tiles(slots, part, rows_of):
    core = slots[24]
    for side in (0, 1):
        first = (core if side == 0 else 1 - core) * 64
        for x in range(4):
            for z in range(4):
                at_x, at_z = slots[side * 12 + x], slots[side * 12 + 8 + z]
                place = at_z * 4 + at_x if part == 0 else at_x * 4 + at_z
                for yh in (0, 1):
                    yield side, place, yh, pl.ds(pl.multiple_of(first + (z * 256 + yh * 128 + x * 16), 16), 16)


def fetch_part(slots, part, own, other, buf, sem):
    for side, place, yh, rows in part_tiles(slots, part, None):
        pltpu.make_async_copy((own, other)[side].at[place, yh], buf.at[part, rows], sem.at[part]).start()


def wait_part(buf, part, sem):
    pltpu.make_async_copy(buf.at[part], buf.at[part], sem.at[part]).wait()


def lane_marks():
    low = lax.broadcasted_iota(jnp.int32, (1, 128), 1) < 64
    return low, jnp.where(low, 1.0, 0.0).astype(BF16), jnp.where(low, 0.0, 1.0).astype(BF16)


def normed(values):
    center = values - jnp.mean(values, axis=-1, keepdims=True)
    scale = lax.rsqrt(jnp.mean(center * center, axis=-1, keepdims=True) + 1e-05)
    return center * scale, scale


def front_kernel(slots, tok_ref, pair_ref, ln1_ref, qkv_bias_ref, out_bias_ref, ln2_ref, own0, other0, own1, other1,
                 low_ref, qkv_ref, prob_ref, mixed_ref, hidden_ref, normed_ref, buf, sem):
    fetch_part(slots, 0, own0, other0, buf, sem)
    fetch_part(slots, 1, own1, other1, buf, sem)

    @pl.loop(0, TOK // 128)
    def _(i):
        rows = pl.ds(i * 128, 128)
        unit, _ = normed(tok_ref[rows, :].astype(F32))
        low_ref[rows, :] = (unit * ln1_ref[0:1, :] + ln1_ref[1:2, :]).astype(BF16)

    for part in (0, 1):
        wait_part(buf, part, sem)
        for n in range(3):
            cols = slice(n * HALF, (n + 1) * HALF)
            qkv_ref[part, :, cols] = (dot(low_ref[...], buf[part, :, cols]) + qkv_bias_ref[part, :, cols]).astype(BF16)
    low, near, far = lane_marks()
    near, far = near * 0.125, far * 0.125

    @pl.loop(0, 8)
    def _(pair):
        part = lax.div(pair, 4)
        start = pl.multiple_of(lax.rem(pair, 4) * 128, 128)
        lanes = pl.ds(pl.multiple_of(pair * 128, 128), 128)
        for block in range(TOK // BLOCK):
            rows = slice(block * BLOCK, (block + 1) * BLOCK)
            query = qkv_ref[part, rows, pl.ds(start, 128)]
            key = qkv_ref[part, rows, pl.ds(start + HALF, 128)]
            value = qkv_ref[part, rows, pl.ds(start + 2 * HALF, 128)]
            bias = pair_ref[block]
            score = dot_t(jnp.concatenate([query * near, query * far], axis=0), key) + jnp.concatenate([bias, bias], axis=0)
            power = jnp.exp(score - jnp.max(score, axis=-1, keepdims=True))
            prob = (power * (1.0 / jnp.sum(power, axis=-1, keepdims=True))).astype(BF16)
            prob_ref[pair, block] = prob
            both = dot(prob, value)
            mixed_ref[rows, lanes] = jnp.where(low, both[:BLOCK], both[BLOCK:]).astype(BF16)

    for part in (0, 1):
        cols = slice(part * HALF, (part + 1) * HALF)
        hidden_ref[:, cols] = tok_ref[:, cols].astype(F32) + dot(mixed_ref[...], buf[part, :, PART:]) + out_bias_ref[:, cols]

    @pl.loop(0, TOK // 128)
    def _(i):
        rows = pl.ds(i * 128, 128)
        unit, _ = normed(hidden_ref[rows, :])
        normed_ref[rows, :] = (unit * ln2_ref[0:1, :] + ln2_ref[1:2, :]).astype(BF16)


VMEM, ANY = pl.BlockSpec(memory_space=pltpu.VMEM), pl.BlockSpec(memory_space=pl.ANY)


def front(slots, tokens, pair_bias, ln1, qkv_bias, out_bias, ln2, parts):
    shape = jax.ShapeDtypeStruct
    return pl.pallas_call(
        front_kernel,
        in_specs=[pl.BlockSpec(memory_space=pltpu.SMEM)] + [VMEM] * 6 + [ANY] * 4,
        out_specs=[VMEM] * 6,
        out_shape=[
            shape((TOK, WIDTH), BF16),
            shape((2, TOK, PART), BF16),
            shape((8, 4, 2 * BLOCK, BLOCK), BF16),
            shape((TOK, WIDTH), BF16),
            shape((TOK, WIDTH), F32),
            shape((TOK, WIDTH), BF16),
        ],
        scratch_shapes=[pltpu.VMEM((2, WIDTH, 2048), BF16), pltpu.SemaphoreType.DMA((2,))],
        compiler_params=pltpu.CompilerParams(vmem_limit_bytes=40 * 2**20),
        cost_estimate=pl.CostEstimate(flops=2 * TOK * WIDTH * 4096 * 2, bytes_accessed=20 * 2**20, transcendentals=TOK * 2048),
        name="front",
    )(slots, tokens, pair_bias, ln1, qkv_bias, out_bias.reshape(1, WIDTH), ln2, *parts[0], *parts[1])


def back_kernel(slots, ghid_ref, glow_ref, tok_ref, ln1_ref, low_ref, qkv_ref, prob_ref, mixed_ref, own0, other0, own1, other1,
                gin_ref, vec_ref, down0, dother0, down1, dother1,
                buf, grad_buf, gmix_ref, gqkv_ref, low_t, total, sem, grad_sem):
    fetch_part(slots, 0, own0, other0, buf, sem)
    fetch_part(slots, 1, own1, other1, buf, sem)
    low_t[...] = mixed_ref[...].T
    vec_ref[...] = jnp.zeros_like(vec_ref)
    wait_part(buf, 0, sem)
    wait_part(buf, 1, sem)
    gmix_ref[...] = (dot_t(glow_ref[:, :HALF], buf[0, :, PART:]) + dot_t(glow_ref[:, HALF:], buf[1, :, PART:])).astype(BF16)
    for part in (0, 1):
        grad_buf[part, :, PART:] = dot(low_t[...], glow_ref[:, part * HALF:(part + 1) * HALF]).astype(BF16)
    low_t[...] = low_ref[...].T
    low, near, far = lane_marks()

    for part in (0, 1):
        @pl.loop(0, 4)
        def _(pair, part=part):
            start = pl.multiple_of(pair * 128, 128)
            lanes = pl.ds(pl.multiple_of(pair * 128 + part * HALF, 128), 128)
            for block in range(TOK // BLOCK):
                rows = slice(block * BLOCK, (block + 1) * BLOCK)
                query = qkv_ref[part, rows, pl.ds(start, 128)]
                key = qkv_ref[part, rows, pl.ds(start + HALF, 128)]
                value = qkv_ref[part, rows, pl.ds(start + 2 * HALF, 128)]
                gmix = gmix_ref[rows, lanes]
                gmix = jnp.concatenate([gmix * near, gmix * far], axis=0)
                query = jnp.concatenate([query * (near * 0.125), query * (far * 0.125)], axis=0)
                prob_low = prob_ref[pair + 4 * part, block]
                prob = prob_low.astype(F32)
                gprob = dot_t(gmix, value)
                gscore = (prob * (gprob - jnp.sum(prob * gprob, axis=-1, keepdims=True))).astype(BF16)
                both = dot(gscore, key) * 0.125
                gqkv_ref[part, rows, pl.ds(start, 128)] = jnp.where(low, both[:BLOCK], both[BLOCK:]).astype(BF16)
                gqkv_ref[part, rows, pl.ds(start + HALF, 128)] = dot(gscore.T, query).astype(BF16)
                gqkv_ref[part, rows, pl.ds(start + 2 * HALF, 128)] = dot(prob_low.T, gmix).astype(BF16)

        for n in range(3):
            cols = slice(n * HALF, (n + 1) * HALF)
            grad_buf[part, :, cols] = dot(low_t[...], gqkv_ref[part, :, cols]).astype(BF16)
        for side, place, yh, rows in part_tiles(slots, part, None):
            pltpu.make_async_copy(grad_buf.at[part, rows], ((down0, dother0), (down1, dother1))[part][side].at[place, yh], grad_sem.at[part]).start()
        more = dot_t(gqkv_ref[part], buf[part, :, :PART])
        if part == 0:
            total[...] = more
        else:
            total[...] += more
        vec_ref[2:3, part * HALF:(part + 1) * HALF] = jnp.sum(gqkv_ref[part, :, :HALF].astype(F32), axis=0, keepdims=True)
        vec_ref[3:4, part * HALF:(part + 1) * HALF] = jnp.sum(gqkv_ref[part, :, 2 * HALF:].astype(F32), axis=0, keepdims=True)

    @pl.loop(0, TOK // 128)
    def _(i):
        rows = pl.ds(i * 128, 128)
        unit, scale = normed(tok_ref[rows, :].astype(F32))
        grad = total[rows, :]
        edge = grad * ln1_ref[0:1, :]
        gin_ref[rows, :] = ghid_ref[rows, :] + (
            edge - jnp.mean(edge, axis=-1, keepdims=True) - unit * jnp.mean(edge * unit, axis=-1, keepdims=True)
        ) * scale
        vec_ref[0:1, :] += jnp.sum(grad * unit, axis=0, keepdims=True)
        vec_ref[1:2, :] += jnp.sum(grad, axis=0, keepdims=True)

    wait_part(grad_buf, 0, grad_sem)
    wait_part(grad_buf, 1, grad_sem)


def back(slots, ghid, glow, tokens, ln1, low, qkv, prob, mixed, parts):
    shape = jax.ShapeDtypeStruct
    tile = shape((16, 2, 16, 2048), BF16)
    return pl.pallas_call(
        back_kernel,
        in_specs=[pl.BlockSpec(memory_space=pltpu.SMEM)] + [VMEM] * 8 + [ANY] * 4,
        out_specs=[VMEM] * 2 + [ANY] * 4,
        out_shape=[shape((TOK, WIDTH), F32), shape((8, WIDTH), F32), tile, tile, tile, tile],
        scratch_shapes=[
            pltpu.VMEM((2, WIDTH, 2048), BF16),
            pltpu.VMEM((2, WIDTH, 2048), BF16),
            pltpu.VMEM((TOK, WIDTH), BF16),
            pltpu.VMEM((2, TOK, PART), BF16),
            pltpu.VMEM((WIDTH, TOK), BF16),
            pltpu.VMEM((TOK, WIDTH), F32),
            pltpu.SemaphoreType.DMA((2,)),
            pltpu.SemaphoreType.DMA((2,)),
        ],
        compiler_params=pltpu.CompilerParams(vmem_limit_bytes=48 * 2**20),
        cost_estimate=pl.CostEstimate(flops=2 * TOK * WIDTH * 4096 * 4, bytes_accessed=40 * 2**20, transcendentals=0),
        name="back",
    )(slots, ghid, glow, tokens, ln1, low, qkv, prob, mixed, *parts[0], *parts[1])


AXES = ("z", "yh", "c", "x", "yl")
UP_ORDER, DOWN_ORDER = ("z", "x", "y"), ("x", "y", "z")


def device_number(place):
    return (
        ((place["z"] * 2 + place["y"] // 2) * 2 + place["c"]) * 4 + place["x"]
    ) * 2 + place["y"] % 2


def exchange_pairs(axis, second):
    pairs = []
    for z, y, c, x in itertools.product(range(4), range(4), range(2), range(4)):
        here = {"z": z, "y": y, "c": c, "x": x}
        mask = 1 if (c == 0) != second else 3
        there = dict(here)
        there[axis] = here[axis] ^ mask
        pairs.append((device_number(here), device_number(there)))
    return pairs


def swap_axis(values, axis, second):
    return lax.ppermute(values, AXES, exchange_pairs(axis, second))


def swap_core(values):
    return lax.ppermute(values, "c", [(0, 1), (1, 0)])


def position(axis):
    if axis == "y":
        return lax.axis_index("yh") * 2 + lax.axis_index("yl")
    return lax.axis_index(axis)


def slot_of(core, distance):
    return jnp.where(
        core == 0, distance ^ (distance >> 1), ((distance << 1) & 3) ^ (3 * (distance >> 1))
    )


def slot_table():
    core, places = lax.axis_index("c"), jnp.arange(4, dtype=jnp.int32)
    rows = [
        slot_of(side, places ^ position(axis)) for side in (core, 1 - core) for axis in ("x", "y", "z")
    ]
    return jnp.concatenate(rows + [jnp.full((8,), core, jnp.int32)])


def steps_of(order):
    return [(axis, second) for axis in order for second in (False, True)]


def gather(values, order):
    for axis, second in steps_of(order):
        values = jnp.concatenate([values, swap_axis(values, axis, second)])
    return values


def add(left, right, dtype=BF16):
    return (left.astype(F32) + right.astype(F32)).astype(dtype)


def scatter(own, other, order):
    got = swap_core(other)
    count = own.shape[0]
    for axis, second in reversed(steps_of(order)):
        count //= 2
        moving = add(own[count:], got[count:])
        own = add(own[:count], got[:count])
        got = swap_axis(moving, axis, second)
    return own, got


def gather_rows(shard, order):
    pieces = gather(shard[None], ("y",))
    here, core = position("y"), lax.axis_index("c")
    pieces = [
        lax.dynamic_index_in_dim(pieces, slot_of(core, at ^ here), 0, keepdims=False)
        for at in range(4)
    ]
    return gather(jnp.stack(pieces).reshape(1, 2, 16, shard.shape[1]), order)


def scatter_rows(own, other, order):
    own, got = scatter(own, other, order)
    pieces = add(own, got).reshape(4, 8, -1)
    here, core = position("y"), lax.axis_index("c")
    first = jnp.where(core == 0, 1, 3)
    second = 4 - first

    def at(slot):
        return lax.dynamic_index_in_dim(pieces, slot, 0, keepdims=False)

    far = swap_axis(jnp.stack([at(here ^ second), at(here ^ second ^ first)]), "y", True)
    near = swap_axis(add(at(here ^ first), far[1]), "y", False)
    return at(here).astype(F32) + far[0].astype(F32) + near.astype(F32)


def sum_everywhere(values):
    for axis, second in steps_of(("x", "y", "z")):
        values = values + swap_axis(values, axis, second)
    return values + swap_core(values)


def pair_bias(clip_ids):
    clips = clip_ids.reshape(-1, BLOCK)
    row = lax.broadcasted_iota(jnp.int32, (BLOCK, BLOCK), 0)
    col = lax.broadcasted_iota(jnp.int32, (BLOCK, BLOCK), 1)
    allowed = (clips[:, :, None] == clips[:, None, :]) & (row >= col)[None]
    return jnp.where(allowed, 0.0, -1e30).astype(F32)


def on_device(
    tokens,
    qkv_weight,
    out_weight,
    up_weight,
    down_weight,
    ln1_gain,
    ln1_bias,
    q_bias,
    v_bias,
    out_bias,
    ln2_gain,
    ln2_bias,
    up_bias,
    down_bias,
    segment_ids,
    cotangent,
):
    slots = slot_table()
    heads = qkv_weight.reshape(8, 3, WIDTH)
    parts = []
    for part, order in enumerate(ORDERS):
        cols = slice(part * HALF, (part + 1) * HALF)
        shard = jnp.concatenate([heads[:, :, cols].reshape(8, PART), out_weight[:, cols]], axis=1)
        own = gather_rows(shard, order[1:])
        parts.append((own, swap_core(own)))
    up_own = gather(up_weight[None], UP_ORDER)
    up_other = swap_core(up_own)
    down_own = gather(down_weight[None], DOWN_ORDER)
    down_other = swap_core(down_own)

    ln1 = jnp.stack([ln1_gain, ln1_bias])
    nothing = jnp.zeros((HALF,), F32)
    qkv_bias = jnp.stack(
        [
            jnp.concatenate([q_bias[cols], nothing, v_bias[cols]])[None]
            for cols in (slice(0, HALF), slice(HALF, WIDTH))
        ]
    )
    low, qkv, prob, mixed, hidden, low2 = front(
        slots, tokens, pair_bias(segment_ids), ln1, qkv_bias, out_bias, jnp.stack([ln2_gain, ln2_bias]), parts
    )
    output, ghid, glow, up_bias_grad, vec2, dup_own, dup_other, ddown_own, ddown_other = ffn(
        slots, low2, cotangent, hidden, ln2_gain, down_bias, up_bias,
        up_own, up_other, down_own, down_other, UP_ORDER, DOWN_ORDER,
    )
    up_grad = add(*scatter(dup_own, dup_other, UP_ORDER), F32)[0]
    down_grad = add(*scatter(ddown_own, ddown_other, DOWN_ORDER), F32)[0]
    grad_tokens, vec1, *grads = back(slots, ghid, glow, tokens, ln1, low, qkv, prob, mixed, parts)
    sums = [
        scatter_rows(grads[2 * part], grads[2 * part + 1], order[1:]) for part, order in enumerate(ORDERS)
    ]
    qkv_grad = jnp.stack([s[:, :PART].reshape(8, 3, HALF) for s in sums], axis=2).reshape(8, 3 * WIDTH)
    out_grad = jnp.concatenate([s[:, PART:] for s in sums], axis=1)
    summed = sum_everywhere(
        jnp.concatenate([vec1[:4].reshape(-1, 128), vec2[:4].reshape(-1, 128), up_bias_grad.reshape(-1, 128)])
    ).reshape(-1)
    vectors = [summed[i * WIDTH : (i + 1) * WIDTH] for i in range(8)]
    return (
        output,
        grad_tokens,
        qkv_grad,
        out_grad,
        up_grad,
        down_grad,
        *vectors[:7],
        summed[8 * WIDTH :],
        vectors[7],
    )


def solution(mesh):
    fine = Mesh(mesh.devices.reshape(4, 2, 2, 4, 2), AXES)
    every, hidden, model = AXES, ("z", "yh", "c"), ("x", "yl")
    weights = (P(every, None), P(every, None), P(model, hidden), P(hidden, model))
    return jax.shard_map(
        on_device,
        mesh=fine,
        in_specs=(P(every, None), *weights, *[P()] * 9, P(every), P(every, None)),
        out_specs=(P(every, None), P(every, None), *weights, *[P()] * 9),
        check_vma=False,
    )
```

time: 568 us -> 412 us (0.73)
  the two profiles are of different devices: /device:TPU:12 before, /device:TPU:0 now
where the time goes in v2:
time: 412 us; the launch traced here: 404 us
  waiting for transfers between devices  146 us (35%)
  starting transfers between devices  117 us (28%)
  Pallas kernels  90 us (22%)
  local copies, waits for them, and re-layouts  26.8 us (7%)
  other arithmetic  22.3 us (5%)
    ppermute x54, waiting for transfers between devices, swap_axis(): return lax.ppermute(values, AXES, exchange_pairs(axis, second))  140 us
    ppermute x54, starting transfers between devices, swap_axis(): return lax.ppermute(values, AXES, exchange_pairs(axis, second))  102 us
    pallas_call x1, Pallas kernels, ffn(): pl.pallas_call(functools.partial(ffn_kernel, up_order, down_order), in_sp...  39.9 us
    pallas_call x1, Pallas kernels, back(): pl.pallas_call(back_kernel, in_specs=[pl.BlockSpec(memory_space=pltpu.SME...  30.7 us
    pallas_call x1, Pallas kernels, front(): pl.pallas_call(front_kernel, in_specs=[pl.BlockSpec(memory_space=pltpu.SM...  19.4 us
    convert_element_type x24, other arithmetic, add(): return (left.astype(F32) + right.astype(F32)).astype(dtype)  17.6 us
    unnamed x66, local copies, waits for them, and re-layouts  16.6 us
    ppermute x9, starting transfers between devices, swap_core(): return lax.ppermute(values, 'c', [(0, 1), (1, 0)])  15.3 us
  transfers between devices with their start and end apart: 63, of which 29 were waited for; matrix products, arithmetic and copies ran while one was open for 11% of the time, Pallas kernels for 5%

profile of v2, /device:TPU:0, one launch (start us, length us, event | category | flops | bytes accessed | tf_op | source)
XLA Modules:
  0.0 404.2 jit_solution(8148088135125563805)
XLA Ops:
  10.8 3.1 collective-permute-start.1
  25.1 3.5 collective-permute-done.23
  45.9 9.2 %collective-permute-done.25 = bf16[16,256,128]{2,1,0:T(8,128)(2,1)S(1)} collective-permute-done((bf16[16,256,128]{2,1,0:T(8,128)(2,1)S(1)}, bf16[16,256,128]{2,1,0:T(8,128)(2,1)S(1)}, u32[]{:S(2)}, u32[]{:S(2)}) %collective-permute-start.25) | collective-permute-done | bytes 1048608 | tf_op jit(solution)/shard_map/ppermute | solution.py:396
  56.6 5.1 %collective-permute-start.26 = (bf16[32,256,128]{2,1,0:T(8,128)(2,1)S(1)}, bf16[32,256,128]{2,1,0:T(8,128)(2,1)S(1)}, u32[]{:S(2)}, u32[]{:S(2)}) collective-permute-start(bf16[32,256,128]{2,1,0:T(8,128)(2,1)S(1)} %get-tuple-element.85), channel_id=1, source_target_pairs={{0,96},{2,98},{4,100},{6,102},{8,40},{10,42},{12,44},{14,46},{1,97... | collective-permute-start | bytes 6291464 | tf_op jit(solution)/shard_map/ppermute | solution.py:396
  62.8 3.2 collective-permute-start.19
  68.8 8.6 %collective-permute-start.3 = (bf16[2,2,16,2048]{3,2,1,0:T(8,128)(2,1)S(1)}, bf16[2,2,16,2048]{3,2,1,0:T(8,128)(2,1)S(1)}, u32[]{:S(2)}, u32[]{:S(2)}) collective-permute-start(bf16[2,2,16,2048]{3,2,1,0:T(8,128)(2,1)S(1)} %pad_maximum_fusion.6), channel_id=1, source_target_pairs={{0,6},{2,4},{4,2},{6,0},{8,10},{10,8},{12,14},{14,12},{1,7},{3,5},... | collective-permute-start | bytes 786440 | tf_op jit(solution)/shard_map/ppermute | solution.py:396
  77.4 11.1 %collective-permute-done.10 = bf16[2,2,16,2048]{3,2,1,0:T(8,128)(2,1)S(1)} collective-permute-done((bf16[2,2,16,2048]{3,2,1,0:T(8,128)(2,1)S(1)}, bf16[2,2,16,2048]{3,2,1,0:T(8,128)(2,1)S(1)}, u32[]{:S(2)}, u32[]{:S(2)}) %collective-permute-start.10) | collective-permute-done | bytes 262176 | tf_op jit(solution)/shard_map/ppermute | solution.py:396
  91.4 10.1 %collective-permute-done.11 = bf16[4,2,16,2048]{3,2,1,0:T(8,128)(2,1)S(1)} collective-permute-done((bf16[4,2,16,2048]{3,2,1,0:T(8,128)(2,1)S(1)}, bf16[4,2,16,2048]{3,2,1,0:T(8,128)(2,1)S(1)}, u32[]{:S(2)}, u32[]{:S(2)}) %collective-permute-start.11) | collective-permute-done | bytes 524320 | tf_op jit(solution)/shard_map/ppermute | solution.py:396
  101.6 11.1 %collective-permute-start.12 = (bf16[8,2,16,2048]{3,2,1,0:T(8,128)(2,1)S(1)}, bf16[8,2,16,2048]{3,2,1,0:T(8,128)(2,1)S(1)}, u32[]{:S(2)}, u32[]{:S(2)}) collective-permute-start(bf16[8,2,16,2048]{3,2,1,0:T(8,128)(2,1)S(1)} %pad_maximum_fusion.1), channel_id=1, source_target_pairs={{0,6},{2,4},{4,2},{6,0},{8,10},{10,8},{12,14},{14,12},{1,7},{3,5},... | collective-permute-start | bytes 3145736 | tf_op jit(solution)/shard_map/ppermute | solution.py:396
  112.8 6.6 %collective-permute-start.5 = (bf16[8,2,16,2048]{3,2,1,0:T(8,128)(2,1)S(1)}, bf16[8,2,16,2048]{3,2,1,0:T(8,128)(2,1)S(1)}, u32[]{:S(2)}, u32[]{:S(2)}) collective-permute-start(bf16[8,2,16,2048]{3,2,1,0:T(8,128)(2,1)S(1)} %pad_maximum_fusion), channel_id=1, source_target_pairs={{0,96},{2,98},{4,100},{6,102},{8,40},{10,42},{12,44},{14,46},{1,97... | collective-permute-start | bytes 3145736 | tf_op jit(solution)/shard_map/ppermute | solution.py:396
  126.6 5.7 %collective-permute-done.5 = bf16[8,2,16,2048]{3,2,1,0:T(8,128)(2,1)S(1)} collective-permute-done((bf16[8,2,16,2048]{3,2,1,0:T(8,128)(2,1)S(1)}, bf16[8,2,16,2048]{3,2,1,0:T(8,128)(2,1)S(1)}, u32[]{:S(2)}, u32[]{:S(2)}) %collective-permute-start.5) | collective-permute-done | bytes 1048608 | tf_op jit(solution)/shard_map/ppermute | solution.py:396
  132.3 12.0 %collective-permute-start.6 = (bf16[16,2,16,2048]{3,2,1,0:T(8,128)(2,1)S(1)}, bf16[16,2,16,2048]{3,2,1,0:T(8,128)(2,1)}, u32[]{:S(2)}, u32[]{:S(2)}) collective-permute-start(bf16[16,2,16,2048]{3,2,1,0:T(8,128)(2,1)S(1)} %constant_dynamic-update-slice_fusion.own0), channel_id=1, source_target_pairs={{0,8},{8,0},{1,9},{9,1},{2,10},{10,2},{3,11},{11,3},{4,12},{12,4},... | collective-permute-start | bytes 6291464 | tf_op jit(solution)/shard_map/ppermute | solution.py:400
  144.8 3.8 collective-permute-done.6.other0
  148.6 19.4 %front.1 = (bf16[512,1024]{1,0:T(8,128)(2,1)S(1)}, bf16[2,512,1536]{2,1,0:T(8,128)(2,1)}, bf16[8,4,256,128]{3,2,1,0:T(8,128)(2,1)S(1)}, bf16[512,1024]{1,0:T(8,1...) custom-call(s32[32]{0:T(128)S(1)} %concatenate.111.slots, bf16[512,1024]{1,0:T(8,128)(2,1)S(1)} %copy-done.3, ...), custom_call_target="tpu_custom_call" | custom-call | flops 8589934592 | bytes 20971520 | tf_op jit(solution)/shard_map/front/pallas_call | solution.py:265
  170.7 39.9 %ffn.1 = (bf16[512,1024]{1,0:T(8,128)(2,1)}, f32[512,1024]{1,0:T(8,128)S(1)}, bf16[512,1024]{1,0:T(8,128)(2,1)S(1)}, f32[16,1,256]{2,1,0:T(1,128)S(1)}, f32[8,10...) custom-call(s32[32]{0:T(128)S(1)} %concatenate.111.slots, ...), custom_call_target="tpu_custom_call" | custom-call | flops 25769803776 | bytes 41943040 | tf_op jit(solution)/shard_map/ffn/pallas_call | solution.py:146
  211.9 30.7 %back.1 = (f32[512,1024]{1,0:T(8,128)}, f32[8,1024]{1,0:T(8,128)S(1)}, bf16[16,2,16,2048]{3,2,1,0:T(8,128)(2,1)}, bf16[16,2,16,2048]{3,2,1,0:T(8,128)(2,1)}, bf1...) custom-call(s32[32]{0:T(128)S(1)} %concatenate.111.slots, f32[512,1024]{1,0:T(8,128)} %copy-done.9, ...), custom_call_target="tpu_custom_call" | custom-call | flops 17179869184 | bytes 41943040 | tf_op jit(solution)/shard_map/back/pallas_call | solution.py:353
  247.2 4.2 %add_convert_fusion.11 = (bf16[8,2,16,2048]{3,2,1,0:T(8,128)(2,1)S(1)}, bf16[8,2,16,2048]{3,2,1,0:T(8,128)(2,1)}) fusion(bf16[16,2,16,2048]{3,2,1,0:T(8,128)(2,1)} %collective-permute-done.28, bf16[16,2,16,2048]{3,2,1,0:T(8,128)(2,1)} %get-tuple-element.46), kind=kLoop, calls=%fused_computation.11 | loop fusion | flops 4194304 | bytes 6291456 | tf_op jit(solution)/shard_map/convert_element_type | solution.py:434
  251.4 3.2 collective-permute-start.29
  254.6 3.3 add_convert_fusion.9
  261.3 13.4 %collective-permute-done.57 = f32[96,128]{1,0:T(8,128)S(1)} collective-permute-done((f32[96,128]{1,0:T(8,128)S(1)}, f32[96,128]{1,0:T(8,128)S(1)}, u32[]{:S(2)}, u32[]{:S(2)}) %collective-permute-start.57) | collective-permute-done | bytes 49184 | tf_op jit(solution)/shard_map/ppermute | solution.py:396
  274.8 4.4 %collective-permute-done.58 = f32[96,128]{1,0:T(8,128)S(1)} collective-permute-done((f32[96,128]{1,0:T(8,128)S(1)}, f32[96,128]{1,0:T(8,128)S(1)}, u32[]{:S(2)}, u32[]{:S(2)}) %collective-permute-start.58) | collective-permute-done | bytes 49184 | tf_op jit(solution)/shard_map/ppermute | solution.py:396
  279.2 3.2 collective-permute-start.59
  285.0 3.8 collective-permute-done.60
  289.1 5.0 %collective-permute-done.61 = f32[96,128]{1,0:T(8,128)S(1)} collective-permute-done((f32[96,128]{1,0:T(8,128)S(1)}, f32[96,128]{1,0:T(8,128)S(1)}, u32[]{:S(2)}, u32[]{:S(2)}) %collective-permute-start.61) | collective-permute-done | bytes 49184 | tf_op jit(solution)/shard_map/ppermute | solution.py:396
  299.0 7.9 %collective-permute-done.30 = bf16[4,2,16,2048]{3,2,1,0:T(8,128)(2,1)S(1)} collective-permute-done((bf16[4,2,16,2048]{3,2,1,0:T(8,128)(2,1)S(1)}, bf16[4,2,16,2048]{3,2,1,0:T(8,128)(2,1)S(1)}, u32[]{:S(2)}, u32[]{:S(2)}) %collective-permute-start.30) | collective-permute-done | bytes 524320 | tf_op jit(solution)/shard_map/ppermute | solution.py:396
  309.7 5.0 %collective-permute-done.31 = bf16[2,2,16,2048]{3,2,1,0:T(8,128)(2,1)S(1)} collective-permute-done((bf16[2,2,16,2048]{3,2,1,0:T(8,128)(2,1)S(1)}, bf16[2,2,16,2048]{3,2,1,0:T(8,128)(2,1)S(1)}, u32[]{:S(2)}, u32[]{:S(2)}) %collective-permute-start.31) | collective-permute-done | bytes 262176 | tf_op jit(solution)/shard_map/ppermute | solution.py:396
  319.9 3.3 add_convert_fusion.1
  331.8 21.5 %collective-permute-done.33 = bf16[2,8,2048]{2,1,0:T(8,128)(2,1)S(1)} collective-permute-done((bf16[2,8,2048]{2,1,0:T(8,128)(2,1)S(1)}, bf16[2,8,2048]{2,1,0:T(8,128)(2,1)S(1)}, u32[]{:S(2)}, u32[]{:S(2)}) %collective-permute-start.33) | collective-permute-done | bytes 65568 | tf_op jit(solution)/shard_map/ppermute | solution.py:396
  357.5 11.7 %collective-permute-done.51 = bf16[16,256,128]{2,1,0:T(8,128)(2,1)S(1)} collective-permute-done((bf16[16,256,128]{2,1,0:T(8,128)(2,1)S(1)}, bf16[16,256,128]{2,1,0:T(8,128)(2,1)S(1)}, u32[]{:S(2)}, u32[]{:S(2)}) %collective-permute-start.51) | collective-permute-done | bytes 1048608 | tf_op jit(solution)/shard_map/ppermute | solution.py:396
  375.8 4.1 %collective-permute-done.52 = bf16[8,256,128]{2,1,0:T(8,128)(2,1)S(1)} collective-permute-done((bf16[8,256,128]{2,1,0:T(8,128)(2,1)S(1)}, bf16[8,256,128]{2,1,0:T(8,128)(2,1)S(1)}, u32[]{:S(2)}, u32[]{:S(2)}) %collective-permute-start.52) | collective-permute-done | bytes 524320 | tf_op jit(solution)/shard_map/ppermute | solution.py:396
  390.5 4.5 %collective-permute-start.47 = (bf16[2,128,256]{2,1,0:T(8,128)(2,1)S(1)}, bf16[2,128,256]{2,1,0:T(8,128)(2,1)S(1)}, u32[]{:S(2)}, u32[]{:S(2)}) collective-permute-start(bf16[2,128,256]{2,1,0:T(8,128)(2,1)S(1)} %get-tuple-element.92), channel_id=1, source_target_pairs={{0,96},{2,98},{4,100},{6,102},{8,40},{10,42},{12,44},{14,46},{1,97... | collective-permute-start | bytes 393224 | tf_op jit(solution)/shard_map/ppermute | solution.py:396
  395.2 3.2 collective-permute-done.47
  (261 shorter events, 117.6 us)
Async XLA Ops:
  0.7 13.5 %collective-permute-start.21 = (bf16[1,256,128]{2,1,0:T(8,128)(2,1)}, bf16[1,256,128]{2,1,0:T(8,128)(2,1)S(1)}, u32[]{:S(2)}, u32[]{:S(2)}) collective-permute-start(bf16[1,256,128]{2,1,0:T(8,128)(2,1)} %bitcast.78), channel_id=1, source_target_pairs={{0,2},{2,0},{4,6},{6,4},{8,14},{10,12},{12,10},{14,8},{1,3},{3,1},... | collective-permute-start | bytes 196616 | tf_op jit(solution)/shard_map/ppermute | solution.py:396
  2.3 14.9 %collective-permute-start.14 = (bf16[1,128,256]{2,1,0:T(8,128)(2,1)}, bf16[1,128,256]{2,1,0:T(8,128)(2,1)S(1)}, u32[]{:S(2)}, u32[]{:S(2)}) collective-permute-start(bf16[1,128,256]{2,1,0:T(8,128)(2,1)} %bitcast.82), channel_id=1, source_target_pairs={{0,32},{2,34},{4,36},{6,38},{8,104},{10,106},{12,108},{14,110},{1,... | collective-permute-start | bytes 196616 | tf_op jit(solution)/shard_map/ppermute | solution.py:396
  40.3 14.8 %collective-permute-start.25 = (bf16[16,256,128]{2,1,0:T(8,128)(2,1)S(1)}, bf16[16,256,128]{2,1,0:T(8,128)(2,1)S(1)}, u32[]{:S(2)}, u32[]{:S(2)}) collective-permute-start(bf16[16,256,128]{2,1,0:T(8,128)(2,1)S(1)} %get-tuple-element.95), channel_id=1, source_target_pairs={{0,32},{2,34},{4,36},{6,38},{8,104},{10,106},{12,108},{14,110},{1,... | collective-permute-start | bytes 3145736 | tf_op jit(solution)/shard_map/ppermute | solution.py:396
  44.0 17.7 %collective-permute-start.18 = (bf16[16,128,256]{2,1,0:T(8,128)(2,1)S(1)}, bf16[16,128,256]{2,1,0:T(8,128)(2,1)S(1)}, u32[]{:S(2)}, u32[]{:S(2)}) collective-permute-start(bf16[16,128,256]{2,1,0:T(8,128)(2,1)S(1)} %get-tuple-element.98), channel_id=1, source_target_pairs={{0,1},{2,3},{4,5},{6,7},{8,25},{10,27},{12,29},{14,31},{1,0},{3,2}... | collective-permute-start | bytes 3145736 | tf_op jit(solution)/shard_map/ppermute | solution.py:396
  44.0 22.0 %collective-permute-start.9 = (bf16[1,2,16,2048]{3,2,1,0:T(8,128)(2,1)S(1)}, bf16[1,2,16,2048]{3,2,1,0:T(8,128)(2,1)S(1)}, u32[]{:S(2)}, u32[]{:S(2)}) collective-permute-start(bf16[1,2,16,2048]{3,2,1,0:T(8,128)(2,1)S(1)} %bitcast.73), channel_id=1, source_target_pairs={{0,32},{2,34},{4,36},{6,38},{8,104},{10,106},{12,108},{14,110},{1,... | collective-permute-start | bytes 393224 | tf_op jit(solution)/shard_map/ppermute | solution.py:396
  45.1 23.7 %collective-permute-start.2 = (bf16[1,2,16,2048]{3,2,1,0:T(8,128)(2,1)S(1)}, bf16[1,2,16,2048]{3,2,1,0:T(8,128)(2,1)S(1)}, u32[]{:S(2)}, u32[]{:S(2)}) collective-permute-start(bf16[1,2,16,2048]{3,2,1,0:T(8,128)(2,1)S(1)} %bitcast.68), channel_id=1, source_target_pairs={{0,2},{2,0},{4,6},{6,4},{8,14},{10,12},{12,10},{14,8},{1,3},{3,1},... | collective-permute-start | bytes 393224 | tf_op jit(solution)/shard_map/ppermute | solution.py:396
  56.6 62.9 %collective-permute-start.26 = (bf16[32,256,128]{2,1,0:T(8,128)(2,1)S(1)}, bf16[32,256,128]{2,1,0:T(8,128)(2,1)S(1)}, u32[]{:S(2)}, u32[]{:S(2)}) collective-permute-start(bf16[32,256,128]{2,1,0:T(8,128)(2,1)S(1)} %get-tuple-element.85), channel_id=1, source_target_pairs={{0,96},{2,98},{4,100},{6,102},{8,40},{10,42},{12,44},{14,46},{1,97... | collective-permute-start | bytes 6291464 | tf_op jit(solution)/shard_map/ppermute | solution.py:396
  62.8 58.1 %collective-permute-start.19 = (bf16[32,128,256]{2,1,0:T(8,128)(2,1)S(1)}, bf16[32,128,256]{2,1,0:T(8,128)(2,1)S(1)}, u32[]{:S(2)}, u32[]{:S(2)}) collective-permute-start(bf16[32,128,256]{2,1,0:T(8,128)(2,1)S(1)} %get-tuple-element.87), channel_id=1, source_target_pairs={{0,17},{2,19},{4,21},{6,23},{8,9},{10,11},{12,13},{14,15},{1,16},{... | collective-permute-start | bytes 6291464 | tf_op jit(solution)/shard_map/ppermute | solution.py:396
  66.1 22.4 %collective-permute-start.10 = (bf16[2,2,16,2048]{3,2,1,0:T(8,128)(2,1)S(1)}, bf16[2,2,16,2048]{3,2,1,0:T(8,128)(2,1)S(1)}, u32[]{:S(2)}, u32[]{:S(2)}) collective-permute-start(bf16[2,2,16,2048]{3,2,1,0:T(8,128)(2,1)S(1)} %pad_maximum_fusion.7), channel_id=1, source_target_pairs={{0,96},{2,98},{4,100},{6,102},{8,40},{10,42},{12,44},{14,46},{1,97... | collective-permute-start | bytes 786440 | tf_op jit(solution)/shard_map/ppermute | solution.py:396
  68.8 19.8 %collective-permute-start.3 = (bf16[2,2,16,2048]{3,2,1,0:T(8,128)(2,1)S(1)}, bf16[2,2,16,2048]{3,2,1,0:T(8,128)(2,1)S(1)}, u32[]{:S(2)}, u32[]{:S(2)}) collective-permute-start(bf16[2,2,16,2048]{3,2,1,0:T(8,128)(2,1)S(1)} %pad_maximum_fusion.6), channel_id=1, source_target_pairs={{0,6},{2,4},{4,2},{6,0},{8,10},{10,8},{12,14},{14,12},{1,7},{3,5},... | collective-permute-start | bytes 786440 | tf_op jit(solution)/shard_map/ppermute | solution.py:396
  88.6 12.9 %collective-permute-start.11 = (bf16[4,2,16,2048]{3,2,1,0:T(8,128)(2,1)S(1)}, bf16[4,2,16,2048]{3,2,1,0:T(8,128)(2,1)S(1)}, u32[]{:S(2)}, u32[]{:S(2)}) collective-permute-start(bf16[4,2,16,2048]{3,2,1,0:T(8,128)(2,1)S(1)} %pad_maximum_fusion.3), channel_id=1, source_target_pairs={{0,2},{2,0},{4,6},{6,4},{8,14},{10,12},{12,10},{14,8},{1,3},{3,1},... | collective-permute-start | bytes 1572872 | tf_op jit(solution)/shard_map/ppermute | solution.py:396
  88.7 24.0 %collective-permute-start.4 = (bf16[4,2,16,2048]{3,2,1,0:T(8,128)(2,1)S(1)}, bf16[4,2,16,2048]{3,2,1,0:T(8,128)(2,1)S(1)}, u32[]{:S(2)}, u32[]{:S(2)}) collective-permute-start(bf16[4,2,16,2048]{3,2,1,0:T(8,128)(2,1)S(1)} %pad_maximum_fusion.2), channel_id=1, source_target_pairs={{0,32},{2,34},{4,36},{6,38},{8,104},{10,106},{12,108},{14,110},{1,... | collective-permute-start | bytes 1572872 | tf_op jit(solution)/shard_map/ppermute | solution.py:396
  101.6 23.9 %collective-permute-start.12 = (bf16[8,2,16,2048]{3,2,1,0:T(8,128)(2,1)S(1)}, bf16[8,2,16,2048]{3,2,1,0:T(8,128)(2,1)S(1)}, u32[]{:S(2)}, u32[]{:S(2)}) collective-permute-start(bf16[8,2,16,2048]{3,2,1,0:T(8,128)(2,1)S(1)} %pad_maximum_fusion.1), channel_id=1, source_target_pairs={{0,6},{2,4},{4,2},{6,0},{8,10},{10,8},{12,14},{14,12},{1,7},{3,5},... | collective-permute-start | bytes 3145736 | tf_op jit(solution)/shard_map/ppermute | solution.py:396
  112.8 19.4 %collective-permute-start.5 = (bf16[8,2,16,2048]{3,2,1,0:T(8,128)(2,1)S(1)}, bf16[8,2,16,2048]{3,2,1,0:T(8,128)(2,1)S(1)}, u32[]{:S(2)}, u32[]{:S(2)}) collective-permute-start(bf16[8,2,16,2048]{3,2,1,0:T(8,128)(2,1)S(1)} %pad_maximum_fusion), channel_id=1, source_target_pairs={{0,96},{2,98},{4,100},{6,102},{8,40},{10,42},{12,44},{14,46},{1,97... | collective-permute-start | bytes 3145736 | tf_op jit(solution)/shard_map/ppermute | solution.py:396
  120.9 49.7 %collective-permute-start.27 = (bf16[64,256,128]{2,1,0:T(8,128)(2,1)}, bf16[64,256,128]{2,1,0:T(8,128)(2,1)}, u32[]{:S(2)}, u32[]{:S(2)}) collective-permute-start(bf16[64,256,128]{2,1,0:T(8,128)(2,1)} %constant_dynamic-update-slice_fusion.39.down_own), channel_id=1, source_target_pairs={{0,8},{8,0},{1,9},{9,1},{2,10},{10,2},{3,11},{11,3},{4,12},{12,4},... | collective-permute-start | bytes 12582920 | tf_op jit(solution)/shard_map/ppermute | solution.py:400
  122.4 48.2 %collective-permute-start.20 = (bf16[64,128,256]{2,1,0:T(8,128)(2,1)}, bf16[64,128,256]{2,1,0:T(8,128)(2,1)}, u32[]{:S(2)}, u32[]{:S(2)}) collective-permute-start(bf16[64,128,256]{2,1,0:T(8,128)(2,1)} %constant_dynamic-update-slice_fusion.21.up_own), channel_id=1, source_target_pairs={{0,8},{8,0},{1,9},{9,1},{2,10},{10,2},{3,11},{11,3},{4,12},{12,4},... | collective-permute-start | bytes 12582920 | tf_op jit(solution)/shard_map/ppermute | solution.py:400
  126.6 18.2 %collective-permute-start.13 = (bf16[16,2,16,2048]{3,2,1,0:T(8,128)(2,1)}, bf16[16,2,16,2048]{3,2,1,0:T(8,128)(2,1)}, u32[]{:S(2)}, u32[]{:S(2)}) collective-permute-start(bf16[16,2,16,2048]{3,2,1,0:T(8,128)(2,1)} %constant_dynamic-update-slice_fusion.5.own1), channel_id=1, source_target_pairs={{0,8},{8,0},{1,9},{9,1},{2,10},{10,2},{3,11},{11,3},{4,12},{12,4},... | collective-permute-start | bytes 6291464 | tf_op jit(solution)/shard_map/ppermute | solution.py:400
  132.3 16.2 %collective-permute-start.6 = (bf16[16,2,16,2048]{3,2,1,0:T(8,128)(2,1)S(1)}, bf16[16,2,16,2048]{3,2,1,0:T(8,128)(2,1)}, u32[]{:S(2)}, u32[]{:S(2)}) collective-permute-start(bf16[16,2,16,2048]{3,2,1,0:T(8,128)(2,1)S(1)} %constant_dynamic-update-slice_fusion.own0), channel_id=1, source_target_pairs={{0,8},{8,0},{1,9},{9,1},{2,10},{10,2},{3,11},{11,3},{4,12},{12,4},... | collective-permute-start | bytes 6291464 | tf_op jit(solution)/shard_map/ppermute | solution.py:400
  242.8 11.8 %collective-permute-start.35 = (bf16[16,2,16,2048]{3,2,1,0:T(8,128)(2,1)}, bf16[16,2,16,2048]{3,2,1,0:T(8,128)(2,1)}, u32[]{:S(2)}, u32[]{:S(2)}) collective-permute-start(bf16[16,2,16,2048]{3,2,1,0:T(8,128)(2,1)} %get-tuple-element.49), channel_id=1, source_target_pairs={{0,8},{8,0},{1,9},{9,1},{2,10},{10,2},{3,11},{11,3},{4,12},{12,4},... | collective-permute-start | bytes 6291464 | tf_op jit(solution)/shard_map/ppermute | solution.py:400
  243.3 16.5 %collective-permute-start.56 = (f32[96,128]{1,0:T(8,128)S(1)}, f32[96,128]{1,0:T(8,128)S(1)}, u32[]{:S(2)}, u32[]{:S(2)}) collective-permute-start(f32[96,128]{1,0:T(8,128)S(1)} %pad_maximum_fusion.21), channel_id=1, source_target_pairs={{0,2},{2,0},{4,6},{6,4},{8,14},{10,12},{12,10},{14,8},{1,3},{3,1},... | collective-permute-start | bytes 147464 | tf_op jit(solution)/shard_map/ppermute | solution.py:396
  243.3 76.5 %collective-permute-start.49 = (bf16[64,256,128]{2,1,0:T(8,128)(2,1)}, bf16[64,256,128]{2,1,0:T(8,128)(2,1)}, u32[]{:S(2)}, u32[]{:S(2)}) collective-permute-start(bf16[64,256,128]{2,1,0:T(8,128)(2,1)} %get-tuple-element.53), channel_id=1, source_target_pairs={{0,8},{8,0},{1,9},{9,1},{2,10},{10,2},{3,11},{11,3},{4,12},{12,4},... | collective-permute-start | bytes 12582920 | tf_op jit(solution)/shard_map/ppermute | solution.py:400
  251.4 44.7 %collective-permute-start.29 = (bf16[8,2,16,2048]{3,2,1,0:T(8,128)(2,1)}, bf16[8,2,16,2048]{3,2,1,0:T(8,128)(2,1)}, u32[]{:S(2)}, u32[]{:S(2)}) collective-permute-start(bf16[8,2,16,2048]{3,2,1,0:T(8,128)(2,1)} %get-tuple-element.66), channel_id=1, source_target_pairs={{0,96},{2,98},{4,100},{6,102},{8,40},{10,42},{12,44},{14,46},{1,97... | collective-permute-start | bytes 3145736 | tf_op jit(solution)/shard_map/ppermute | solution.py:396
  257.9 39.8 %collective-permute-start.36 = (bf16[8,2,16,2048]{3,2,1,0:T(8,128)(2,1)}, bf16[8,2,16,2048]{3,2,1,0:T(8,128)(2,1)S(1)}, u32[]{:S(2)}, u32[]{:S(2)}) collective-permute-start(bf16[8,2,16,2048]{3,2,1,0:T(8,128)(2,1)} %get-tuple-element.68), channel_id=1, source_target_pairs={{0,6},{2,4},{4,2},{6,0},{8,10},{10,8},{12,14},{14,12},{1,7},{3,5},... | collective-permute-start | bytes 3145736 | tf_op jit(solution)/shard_map/ppermute | solution.py:396
  259.7 14.9 %collective-permute-start.57 = (f32[96,128]{1,0:T(8,128)S(1)}, f32[96,128]{1,0:T(8,128)S(1)}, u32[]{:S(2)}, u32[]{:S(2)}) collective-permute-start(f32[96,128]{1,0:T(8,128)S(1)} %fusion.7), channel_id=1, source_target_pairs={{0,6},{2,4},{4,2},{6,0},{8,10},{10,8},{12,14},{14,12},{1,7},{3,5},... | collective-permute-start | bytes 147464 | tf_op jit(solution)/shard_map/ppermute | solution.py:396
  294.2 29.3 %collective-permute-start.42 = (bf16[64,128,256]{2,1,0:T(8,128)(2,1)}, bf16[64,128,256]{2,1,0:T(8,128)(2,1)S(1)}, u32[]{:S(2)}, u32[]{:S(2)}) collective-permute-start(bf16[64,128,256]{2,1,0:T(8,128)(2,1)} %get-tuple-element.51), channel_id=1, source_target_pairs={{0,8},{8,0},{1,9},{9,1},{2,10},{10,2},{3,11},{11,3},{4,12},{12,4},... | collective-permute-start | bytes 12582920 | tf_op jit(solution)/shard_map/ppermute | solution.py:400
  323.1 30.3 %collective-permute-start.50 = (bf16[32,256,128]{2,1,0:T(8,128)(2,1)S(1)}, bf16[32,256,128]{2,1,0:T(8,128)(2,1)S(1)}, u32[]{:S(2)}, u32[]{:S(2)}) collective-permute-start(bf16[32,256,128]{2,1,0:T(8,128)(2,1)S(1)} %get-tuple-element.58), channel_id=1, source_target_pairs={{0,96},{2,98},{4,100},{6,102},{8,40},{10,42},{12,44},{14,46},{1,97... | collective-permute-start | bytes 6291464 | tf_op jit(solution)/shard_map/ppermute | solution.py:396
  325.2 29.2 %collective-permute-start.43 = (bf16[32,128,256]{2,1,0:T(8,128)(2,1)S(1)}, bf16[32,128,256]{2,1,0:T(8,128)(2,1)S(1)}, u32[]{:S(2)}, u32[]{:S(2)}) collective-permute-start(bf16[32,128,256]{2,1,0:T(8,128)(2,1)S(1)} %get-tuple-element.60), channel_id=1, source_target_pairs={{0,17},{2,19},{4,21},{6,23},{8,9},{10,11},{12,13},{14,15},{1,16},{... | collective-permute-start | bytes 6291464 | tf_op jit(solution)/shard_map/ppermute | solution.py:396
  328.3 25.0 %collective-permute-start.33 = (bf16[2,8,2048]{2,1,0:T(8,128)(2,1)S(1)}, bf16[2,8,2048]{2,1,0:T(8,128)(2,1)S(1)}, u32[]{:S(2)}, u32[]{:S(2)}) collective-permute-start(bf16[2,8,2048]{2,1,0:T(8,128)(2,1)S(1)} %pad_maximum_fusion.19), channel_id=1, source_target_pairs={{0,17},{2,19},{4,21},{6,23},{8,9},{10,11},{12,13},{14,15},{1,16},{... | collective-permute-start | bytes 196616 | tf_op jit(solution)/shard_map/ppermute | solution.py:396
  328.8 28.6 %collective-permute-start.40 = (bf16[2,8,2048]{2,1,0:T(8,128)(2,1)S(1)}, bf16[2,8,2048]{2,1,0:T(8,128)(2,1)S(1)}, u32[]{:S(2)}, u32[]{:S(2)}) collective-permute-start(bf16[2,8,2048]{2,1,0:T(8,128)(2,1)S(1)} %pad_maximum_fusion.20), channel_id=1, source_target_pairs={{0,17},{2,19},{4,21},{6,23},{8,9},{10,11},{12,13},{14,15},{1,16},{... | collective-permute-start | bytes 196616 | tf_op jit(solution)/shard_map/ppermute | solution.py:396
  354.3 14.9 %collective-permute-start.51 = (bf16[16,256,128]{2,1,0:T(8,128)(2,1)S(1)}, bf16[16,256,128]{2,1,0:T(8,128)(2,1)S(1)}, u32[]{:S(2)}, u32[]{:S(2)}) collective-permute-start(bf16[16,256,128]{2,1,0:T(8,128)(2,1)S(1)} %get-tuple-element.62), channel_id=1, source_target_pairs={{0,32},{2,34},{4,36},{6,38},{8,104},{10,106},{12,108},{14,110},{1,... | collective-permute-start | bytes 3145736 | tf_op jit(solution)/shard_map/ppermute | solution.py:396
  355.3 17.2 %collective-permute-start.44 = (bf16[16,128,256]{2,1,0:T(8,128)(2,1)S(1)}, bf16[16,128,256]{2,1,0:T(8,128)(2,1)S(1)}, u32[]{:S(2)}, u32[]{:S(2)}) collective-permute-start(bf16[16,128,256]{2,1,0:T(8,128)(2,1)S(1)} %get-tuple-element.64), channel_id=1, source_target_pairs={{0,1},{2,3},{4,5},{6,7},{8,25},{10,27},{12,29},{14,31},{1,0},{3,2}... | collective-permute-start | bytes 3145736 | tf_op jit(solution)/shard_map/ppermute | solution.py:396
  357.4 18.3 %collective-permute-start.41 = (bf16[8,2048]{1,0:T(8,128)(2,1)S(1)}, bf16[8,2048]{1,0:T(8,128)(2,1)S(1)}, u32[]{:S(2)}, u32[]{:S(2)}) collective-permute-start(bf16[8,2048]{1,0:T(8,128)(2,1)S(1)} %fusion.1), channel_id=1, source_target_pairs={{0,1},{2,3},{4,5},{6,7},{8,25},{10,27},{12,29},{14,31},{1,0},{3,2}... | collective-permute-start | bytes 98312 | tf_op jit(solution)/shard_map/ppermute | solution.py:396
  (56 other events, 637.3 us)

commit v3 on v2

v3 whole, which is shorter than its diff:
```python
import functools
import itertools

import jax
import jax.numpy as jnp
from jax import lax
from jax.experimental import pallas as pl
from jax.experimental.pallas import tpu as pltpu
from jax.sharding import Mesh, PartitionSpec as P

F32, BF16 = jnp.float32, jnp.bfloat16
TOK, WIDTH, FF = 512, 1024, 4096
BOTH = 2 * TOK
CHUNK = 1024
UNIT = 256
ROOT = 0.7978845608028654
CUBE = 0.044715
VMEM, ANY, HBM, SMEM = (
    pl.BlockSpec(memory_space=kind) for kind in (pltpu.VMEM, pl.ANY, pltpu.HBM, pltpu.SMEM)
)
ONE = pltpu.SemaphoreType.DMA
TWO = pltpu.SemaphoreType.DMA((2,))
FEW = pltpu.SemaphoreType.DMA((8,))


def shape(*dims, dtype=BF16):
    return jax.ShapeDtypeStruct(dims, dtype)


def work(flops):
    return pl.CostEstimate(flops=int(flops), bytes_accessed=1 << 20, transcendentals=0)


def dot(a, b):
    return lax.dot_general(a, b, (((1,), (0,)), ((), ())), preferred_element_type=F32)


def dot_t(a, b):
    return lax.dot_general(a, b, (((1,), (1,)), ((), ())), preferred_element_type=F32)


def normed(values):
    center = values - jnp.mean(values, axis=-1, keepdims=True)
    scale = lax.rsqrt(jnp.mean(center * center, axis=-1, keepdims=True) + 1e-05)
    return center * scale, scale


def norm_back(edge, unit, scale):
    return (edge - jnp.mean(edge, axis=-1, keepdims=True) - unit * jnp.mean(edge * unit, axis=-1, keepdims=True)) * scale


def start(source, target, sem):
    pltpu.make_async_copy(source, target, sem).start()


def wait(ref, sem):
    pltpu.make_async_copy(ref, ref, sem).wait()


def place_of(places, side, axis, slot):
    return places[side * 12 + "xyz".index(axis) * 4 + slot]


def ffn_kernel(places, bias_ref, low_own, low_other, grad_own, grad_other, up, down_low, down_high,
               bias_grad_ref, feed_ref, feed_low_ref, gc_ref, gc_low_ref, dup, ddown_keep, ddown_move0, ddown_move1,
               up_buf, down_buf, dup_buf, ddown_buf, low, grad, low_t, act_buf, gpre_buf, total, grad_total,
               feed_low, gc_low, in_sem, up_sem, down_sem, out_sem):
    core = places[24]

    def tiles(chunk):
        for part in (0, 1):
            for sy in range(4):
                y = place_of(places, 0, "y", sy)
                yh, yl = lax.div(y, 2), lax.rem(y, 2)
                unit = pl.ds(pl.multiple_of((part * 2 + yh) * UNIT, UNIT), UNIT)
                for x in range(4):
                    yield sy, chunk * 2 + part, x, yl, unit

    def model(x, yl):
        return pl.ds(pl.multiple_of((x * 2 + yl) * 128, 128), 128)

    def fetch(chunk):
        for sy, sz, x, yl, unit in tiles(chunk):
            start(up.at[x * 16 + sy * 4 + sz], up_buf.at[chunk, model(x, yl), unit], up_sem.at[chunk])
        for sy, sz, sx, yl, unit in tiles(chunk):
            cols = model(place_of(places, 0, "x", sx), yl)
            start((down_low, down_high)[sy // 2].at[sy % 2 * 16 + sz * 4 + sx], down_buf.at[chunk, unit, cols], down_sem.at[chunk])

    def send_down(chunk):
        for sy, sz, sx, yl, unit in tiles(chunk):
            source = ddown_buf.at[chunk, unit, model(place_of(places, 0, "x", sx), yl)]
            if sy < 2:
                start(source, ddown_keep.at[sy * 16 + sz * 4 + sx], out_sem)
            else:
                start(source, (ddown_move0, ddown_move1)[sy - 2].at[sz * 4 + sx], out_sem)

    def send_up(chunk):
        for sy, sz, x, yl, unit in tiles(chunk):
            start(dup_buf.at[chunk, model(x, yl), unit], dup.at[x * 16 + sy * 4 + sz], out_sem)

    start(low_own, low.at[pl.ds(0, TOK)], in_sem.at[0])
    start(low_other, low.at[pl.ds(TOK, TOK)], in_sem.at[0])
    fetch(0)
    start(grad_own, grad.at[pl.ds(0, TOK)], in_sem.at[1])
    start(grad_other, grad.at[pl.ds(TOK, TOK)], in_sem.at[1])
    fetch(1)
    bias_grad_ref[...] = jnp.zeros_like(bias_grad_ref)
    wait(low, in_sem.at[0])
    low_t[...] = low[...].T
    wait(grad, in_sem.at[1])

    for chunk in (0, 1):
        wait(up_buf.at[chunk], up_sem.at[chunk])
        wait(down_buf.at[chunk], down_sem.at[chunk])
        for n in range(CHUNK // UNIT):
            cols = slice(n * UNIT, (n + 1) * UNIT)
            block = (place_of(places, 0, "z", chunk * 2 + n // 2) * 2 + n % 2) * 2 + core
            pre = dot(low[...], up_buf[chunk, :, cols]) + bias_ref[block]
            gact = dot_t(grad[...], down_buf[chunk, cols, :])
            square = pre * pre
            bend = jnp.tanh(ROOT * (pre + CUBE * square * pre))
            half = 0.5 + 0.5 * bend
            act = (pre * half).astype(BF16)
            slope = half + 0.5 * pre * (1.0 - bend * bend) * (ROOT + 3.0 * ROOT * CUBE * square)
            gpre = (gact * slope).astype(BF16)
            act_buf[:, cols] = act
            gpre_buf[:, cols] = gpre
            bias_grad_ref[block] = jnp.sum(gpre.astype(F32), axis=0, keepdims=True)
            ddown_buf[chunk, cols, :] = dot(act.T, grad[...]).astype(BF16)
            dup_buf[chunk, :, cols] = dot(low_t[...], gpre).astype(BF16)
        send_up(chunk)
        send_down(chunk)
        more = dot_t(gpre_buf[...], up_buf[chunk])
        feed = dot(act_buf[...], down_buf[chunk])
        if chunk == 0:
            grad_total[...] = more
            total[...] = feed
        else:
            grad_total[...] += more
            gc_low[...] = grad_total[TOK:, :].astype(BF16)
            start(gc_low, gc_low_ref, out_sem)
            start(grad_total.at[pl.ds(0, TOK)], gc_ref, out_sem)
            total[...] += feed
            feed_low[...] = total[TOK:, :].astype(BF16)
            start(feed_low, feed_low_ref, out_sem)
            start(total.at[pl.ds(0, TOK)], feed_ref, out_sem)
    for ref in (dup_buf, ddown_buf, gc_low, feed_low, grad_total.at[pl.ds(0, TOK)], total.at[pl.ds(0, TOK)]):
        wait(ref, out_sem)


def ffn(places, up_bias, low_own, low_other, grad_own, grad_other, weights):
    big = pltpu.VMEM((2, CHUNK, CHUNK), BF16)
    rows = pltpu.VMEM((BOTH, WIDTH), BF16)
    sums = pltpu.VMEM((BOTH, WIDTH), F32)
    half = pltpu.VMEM((TOK, WIDTH), BF16)
    return pl.pallas_call(
        ffn_kernel,
        in_specs=[SMEM, VMEM] + [ANY] * 4 + [HBM] * 3,
        out_specs=[VMEM] + [HBM] * 8,
        out_shape=[
            shape(16, 1, UNIT, dtype=F32),
            shape(TOK, WIDTH, dtype=F32),
            shape(TOK, WIDTH),
            shape(TOK, WIDTH, dtype=F32),
            shape(TOK, WIDTH),
            shape(64, 128, 256),
            shape(32, 256, 128),
            shape(16, 256, 128),
            shape(16, 256, 128),
        ],
        scratch_shapes=[
            big, big, big, big, rows, rows, rows,
            pltpu.VMEM((BOTH, CHUNK), BF16),
            pltpu.VMEM((BOTH, CHUNK), BF16),
            sums, sums, half, half, TWO, TWO, TWO, ONE,
        ],
        compiler_params=pltpu.CompilerParams(vmem_limit_bytes=56 * 2**20),
        cost_estimate=work(40e9),
        name="ffn",
    )(places, up_bias.reshape(16, 1, UNIT), low_own, low_other, grad_own, grad_other, *weights)


BLOCK = 128
HALF = 512
PART = 3 * HALF
ORDERS = (("y", "x", "z"), ("y", "z", "x"))


def row_tiles(places, order):
    core = places[24]
    for side in (0, 1):
        for sx in range(4):
            for sz in range(4):
                last, middle = (sz, sx) if order[2] == "z" else (sx, sz)
                x, z = place_of(places, side, "x", sx), place_of(places, side, "z", sz)
                yield side, last // 2, last % 2 * 4 + middle, z, core if side == 0 else 1 - core, x


def fetch_part(places, part, pieces, buf, sem, cols):
    cols = slice(part * 2048 + cols.start, part * 2048 + cols.stop)
    for side, high, within, z, c, x in row_tiles(places, ORDERS[0]):
        start(pieces[2 * side + high].at[within, :, :, cols], buf.at[z, :, c, x], sem)


def matrix(ref):
    return ref.reshape(WIDTH, ref.shape[-1])


def parts_buffer(cols):
    return pltpu.VMEM((4, 2, 2, 4, 16, cols), BF16)


def lane_marks():
    low = lax.broadcasted_iota(jnp.int32, (1, 128), 1) < 64
    return low, jnp.where(low, 1.0, 0.0).astype(BF16), jnp.where(low, 0.0, 1.0).astype(BF16)


def project_kernel(places, tok_ref, ln1_ref, qkv_bias_ref, *refs):
    pieces, (qkv_ref, low_out, qkv_out, buf0, buf1, low_ref, sem, out_sem) = refs[:4], refs[4:]
    for part, buf in ((0, buf0), (1, buf1)):
        fetch_part(places, part, pieces, buf, sem.at[part], slice(0, PART))

    @pl.loop(0, TOK // 128)
    def _(i):
        rows = pl.ds(i * 128, 128)
        unit, _ = normed(tok_ref[rows, :].astype(F32))
        low_ref[rows, :] = (unit * ln1_ref[0:1, :] + ln1_ref[1:2, :]).astype(BF16)

    start(low_ref, low_out, out_sem)
    for part, buf in ((0, buf0), (1, buf1)):
        wait(buf, sem.at[part])
        for n in range(3):
            cols = slice(n * HALF, (n + 1) * HALF)
            qkv_ref[part, :, cols] = (dot(low_ref[...], matrix(buf)[:, cols]) + qkv_bias_ref[part, :, cols]).astype(BF16)
        start(qkv_ref.at[part], qkv_out.at[part], out_sem)
    wait(low_ref, out_sem)
    wait(qkv_ref, out_sem)


def project(places, tokens, ln1, qkv_bias, pieces):
    return pl.pallas_call(
        project_kernel,
        in_specs=[SMEM] + [VMEM] * 3 + [HBM] * 4,
        out_specs=[VMEM] + [HBM] * 2,
        out_shape=[shape(2, TOK, PART), shape(TOK, WIDTH), shape(2, TOK, PART)],
        scratch_shapes=[parts_buffer(PART), parts_buffer(PART), pltpu.VMEM((TOK, WIDTH), BF16), TWO, ONE],
        compiler_params=pltpu.CompilerParams(vmem_limit_bytes=24 * 2**20),
        cost_estimate=work(8e9),
        name="project",
    )(places, tokens, ln1, qkv_bias, *pieces)


def attend_kernel(places, tok_ref, pair_ref, qkv_ref, out_bias_ref, ln2_ref, *refs):
    pieces, refs = refs[:4], refs[4:]
    prob_out, mixed_out, hidden_out, normed_out, buf0, buf1, prob_ref, mixed_ref, hidden_ref, normed_ref, sem, out_sem = refs
    for part, buf in ((0, buf0), (1, buf1)):
        fetch_part(places, part, pieces, buf, sem.at[part], slice(PART, 2048))
    low, near, far = lane_marks()
    near, far = near * 0.125, far * 0.125

    @pl.loop(0, 8)
    def _(pair):
        part = lax.div(pair, 4)
        begin = pl.multiple_of(lax.rem(pair, 4) * 128, 128)
        lanes = pl.ds(pl.multiple_of(pair * 128, 128), 128)
        for block in range(TOK // BLOCK):
            rows = slice(block * BLOCK, (block + 1) * BLOCK)
            query = qkv_ref[part, rows, pl.ds(begin, 128)]
            key = qkv_ref[part, rows, pl.ds(begin + HALF, 128)]
            value = qkv_ref[part, rows, pl.ds(begin + 2 * HALF, 128)]
            bias = pair_ref[block]
            score = dot_t(jnp.concatenate([query * near, query * far], axis=0), key) + jnp.concatenate([bias, bias], axis=0)
            power = jnp.exp(score - jnp.max(score, axis=-1, keepdims=True))
            prob = (power * (1.0 / jnp.sum(power, axis=-1, keepdims=True))).astype(BF16)
            prob_ref[pair, block] = prob
            both = dot(prob, value)
            mixed_ref[rows, lanes] = jnp.where(low, both[:BLOCK], both[BLOCK:]).astype(BF16)

    start(prob_ref, prob_out, out_sem)
    start(mixed_ref, mixed_out, out_sem)
    for part, buf in ((0, buf0), (1, buf1)):
        cols = slice(part * HALF, (part + 1) * HALF)
        wait(buf, sem.at[part])
        hidden_ref[:, cols] = tok_ref[:, cols].astype(F32) + dot(mixed_ref[...], matrix(buf)[...]) + out_bias_ref[:, cols]
    start(hidden_ref, hidden_out, out_sem)

    @pl.loop(0, TOK // 128)
    def _(i):
        rows = pl.ds(i * 128, 128)
        unit, _ = normed(hidden_ref[rows, :])
        normed_ref[rows, :] = (unit * ln2_ref[0:1, :] + ln2_ref[1:2, :]).astype(BF16)

    start(normed_ref, normed_out, out_sem)
    for ref in (prob_ref, mixed_ref, hidden_ref, normed_ref):
        wait(ref, out_sem)


def attend(places, tokens, pair_bias, qkv, out_bias, ln2, pieces):
    outs = [((8, 4, 2 * BLOCK, BLOCK), BF16), ((TOK, WIDTH), BF16), ((TOK, WIDTH), F32), ((TOK, WIDTH), BF16)]
    return pl.pallas_call(
        attend_kernel,
        in_specs=[SMEM] + [VMEM] * 5 + [HBM] * 4,
        out_specs=[HBM] * 4,
        out_shape=[jax.ShapeDtypeStruct(*out) for out in outs],
        scratch_shapes=[parts_buffer(HALF), parts_buffer(HALF)] + [pltpu.VMEM(*out) for out in outs] + [TWO, ONE],
        compiler_params=pltpu.CompilerParams(vmem_limit_bytes=32 * 2**20),
        cost_estimate=work(16e9),
        name="attend",
    )(places, tokens, pair_bias, qkv, out_bias.reshape(1, WIDTH), ln2, *pieces)


def turn(hidden_ref, gain_ref, gc_ref, got_ref, grad_ref, ghid_ref, glow_ref, vec_ref):
    vec_ref[...] = jnp.zeros_like(vec_ref)

    @pl.loop(0, TOK // 128)
    def _(part):
        rows = pl.ds(part * 128, 128)
        unit, scale = normed(hidden_ref[rows, :])
        gc = gc_ref[rows, :] + got_ref[rows, :].astype(F32)
        gout = grad_ref[rows, :].astype(F32)
        ghid = gout + norm_back(gc * gain_ref[...], unit, scale)
        ghid_ref[rows, :] = ghid
        glow_ref[rows, :] = ghid.astype(BF16)
        vec_ref[0:1, :] += jnp.sum(ghid, axis=0, keepdims=True)
        vec_ref[1:2, :] += jnp.sum(gc * unit, axis=0, keepdims=True)
        vec_ref[2:3, :] += jnp.sum(gc, axis=0, keepdims=True)
        vec_ref[3:4, :] += jnp.sum(gout, axis=0, keepdims=True)


TURN_SHAPES = [((TOK, WIDTH), F32), ((TOK, WIDTH), F32), ((TOK, WIDTH), BF16), ((TOK, WIDTH), BF16)]


def back_kernel(part, places, low_in, qkv_in, prob_in, mixed_in, *refs):
    pieces, refs = refs[:4], refs[4:]
    if part == 0:
        gain_ref, turn_in, refs = refs[0], refs[1:5], refs[5:]
        sum_ref, vec_ref, gqkv_out, *outs = refs[:7]
        ghid_out, glow_out = refs[7:9]
        turn_refs, refs = refs[9:13], refs[13:]
        ghid_ref, refs = refs[0], refs[1:]
    else:
        glow_in, refs = refs[0], refs[1:]
        sum_ref, gqkv_out, *outs = refs[:6]
        refs = refs[6:]
    low_ref, qkv_ref, prob_ref, mixed_ref, glow_ref, buf, side_buf, grad_buf, gmix_ref, gqkv_ref, flip, sem, out_sem = refs
    tail = slice(PART, 2048)
    if part == 0:
        for source, target in zip(turn_in, turn_refs):
            start(source, target, sem.at[0])
    else:
        start(glow_in, glow_ref, sem.at[0])
    start(mixed_in, mixed_ref, sem.at[1])
    fetch_part(places, part, pieces, buf, sem.at[2], tail)
    fetch_part(places, 1 - part, pieces, side_buf, sem.at[3], tail)
    start(qkv_in.at[part], qkv_ref, sem.at[4])
    start(prob_in.at[pl.ds(part * 4, 4)], prob_ref, sem.at[4])
    start(low_in, low_ref, sem.at[5])
    wait(mixed_ref, sem.at[1])
    flip[...] = mixed_ref[...].T
    if part == 0:
        for ref in turn_refs:
            wait(ref, sem.at[0])
        turn(turn_refs[0], gain_ref, turn_refs[1], turn_refs[2], turn_refs[3], ghid_ref, glow_ref, vec_ref)
        start(ghid_ref, ghid_out, out_sem)
        start(glow_ref, glow_out, out_sem)
    else:
        wait(glow_ref, sem.at[0])
    heads = slice(part * HALF, (part + 1) * HALF)
    rest = slice((1 - part) * HALF, (2 - part) * HALF)
    grad_matrix = matrix(grad_buf)
    grad_matrix[:, PART:] = dot(flip[...], glow_ref[:, heads]).astype(BF16)
    wait(buf, sem.at[2])
    wait(side_buf, sem.at[3])
    gmix_ref[...] = (
        dot_t(glow_ref[:, heads], matrix(buf)[heads, :]) + dot_t(glow_ref[:, rest], matrix(side_buf)[heads, :])
    ).astype(BF16)
    wait(low_ref, sem.at[5])
    flip[...] = low_ref[...].T
    wait(qkv_ref, sem.at[4])
    wait(prob_ref, sem.at[4])
    low, near, far = lane_marks()

    @pl.loop(0, 4)
    def _(pair):
        begin = pl.multiple_of(pair * 128, 128)
        for block in range(TOK // BLOCK):
            rows = slice(block * BLOCK, (block + 1) * BLOCK)
            query = qkv_ref[rows, pl.ds(begin, 128)]
            key = qkv_ref[rows, pl.ds(begin + HALF, 128)]
            value = qkv_ref[rows, pl.ds(begin + 2 * HALF, 128)]
            gmix = gmix_ref[rows, pl.ds(begin, 128)]
            gmix = jnp.concatenate([gmix * near, gmix * far], axis=0)
            query = jnp.concatenate([query * (near * 0.125), query * (far * 0.125)], axis=0)
            prob_low = prob_ref[pair, block]
            prob = prob_low.astype(F32)
            gprob = dot_t(gmix, value)
            gscore = (prob * (gprob - jnp.sum(prob * gprob, axis=-1, keepdims=True))).astype(BF16)
            both = dot(gscore, key) * 0.125
            gqkv_ref[rows, pl.ds(begin, 128)] = jnp.where(low, both[:BLOCK], both[BLOCK:]).astype(BF16)
            gqkv_ref[rows, pl.ds(begin + HALF, 128)] = dot(gscore.T, query).astype(BF16)
            gqkv_ref[rows, pl.ds(begin + 2 * HALF, 128)] = dot(prob_low.T, gmix).astype(BF16)

    start(gqkv_ref, gqkv_out, out_sem)
    for n in range(3):
        cols = slice(n * HALF, (n + 1) * HALF)
        grad_matrix[:, cols] = dot(flip[...], gqkv_ref[:, cols]).astype(BF16)
    for side, high, within, z, c, x in row_tiles(places, ORDERS[part]):
        start(grad_buf.at[z, :, c, x], outs[2 * side + high].at[within], out_sem)
    sum_ref[...] = jnp.sum(gqkv_ref[...].astype(F32), axis=0, keepdims=True)
    wait(grad_buf, out_sem)
    wait(gqkv_ref, out_sem)
    if part == 0:
        wait(ghid_ref, out_sem)
        wait(glow_ref, out_sem)


def back(part, places, low, qkv, prob, mixed, pieces, *more):
    tile = shape(8, 2, 16, 2048)
    first = part == 0
    wide = pltpu.VMEM((TOK, WIDTH), BF16)
    return pl.pallas_call(
        functools.partial(back_kernel, part),
        in_specs=[SMEM] + [HBM] * 8 + ([VMEM] + [ANY] * 4 if first else [HBM]),
        out_specs=[VMEM] * (2 if first else 1) + [HBM] * (7 if first else 5),
        out_shape=[shape(1, PART, dtype=F32)]
        + ([shape(8, WIDTH, dtype=F32)] if first else [])
        + [shape(TOK, PART), tile, tile, tile, tile]
        + ([shape(TOK, WIDTH, dtype=F32), shape(TOK, WIDTH)] if first else []),
        scratch_shapes=([pltpu.VMEM(*s) for s in TURN_SHAPES] + [pltpu.VMEM((TOK, WIDTH), F32)] if first else [])
        + [
            wide,
            pltpu.VMEM((TOK, PART), BF16),
            pltpu.VMEM((4, 4, 2 * BLOCK, BLOCK), BF16),
            wide,
            wide,
            parts_buffer(HALF),
            parts_buffer(HALF),
            parts_buffer(2048),
            pltpu.VMEM((TOK, HALF), BF16),
            pltpu.VMEM((TOK, PART), BF16),
            pltpu.VMEM((WIDTH, TOK), BF16),
            FEW,
            ONE,
        ],
        compiler_params=pltpu.CompilerParams(vmem_limit_bytes=44 * 2**20),
        cost_estimate=work(20e9),
        name="back" + str(part),
    )(places, low, qkv, prob, mixed, *pieces, *more)


def end_kernel(places, ln1_ref, down_bias_ref, gqkv0, gqkv1, ghid, tok, hidden, feed, feed_got, *refs):
    pieces, refs = refs[:4], refs[4:]
    gin_out, out_out, vec_ref, buf0, buf1, gqkv0_ref, gqkv1_ref, ghid_ref, tok_ref, hidden_ref, feed_ref, got_ref, out_ref, total, sem, out_sem = refs
    start(gqkv0, gqkv0_ref, sem.at[0])
    fetch_part(places, 0, pieces, buf0, sem.at[0], slice(0, PART))
    start(gqkv1, gqkv1_ref, sem.at[1])
    fetch_part(places, 1, pieces, buf1, sem.at[1], slice(0, PART))
    start(ghid, ghid_ref, sem.at[2])
    start(tok, tok_ref, sem.at[2])
    for source, target in ((hidden, hidden_ref), (feed, feed_ref), (feed_got, got_ref)):
        start(source, target, sem.at[3])
    vec_ref[...] = jnp.zeros_like(vec_ref)
    wait(gqkv0_ref, sem.at[0])
    wait(buf0, sem.at[0])
    total[...] = dot_t(gqkv0_ref[...], matrix(buf0)[...])
    wait(gqkv1_ref, sem.at[1])
    wait(buf1, sem.at[1])
    total[...] += dot_t(gqkv1_ref[...], matrix(buf1)[...])
    wait(ghid_ref, sem.at[2])
    wait(tok_ref, sem.at[2])

    @pl.loop(0, TOK // 128)
    def _(i):
        rows = pl.ds(i * 128, 128)
        unit, scale = normed(tok_ref[rows, :].astype(F32))
        grad = total[rows, :]
        ghid_ref[rows, :] += norm_back(grad * ln1_ref[0:1, :], unit, scale)
        vec_ref[0:1, :] += jnp.sum(grad * unit, axis=0, keepdims=True)
        vec_ref[1:2, :] += jnp.sum(grad, axis=0, keepdims=True)

    start(ghid_ref, gin_out, out_sem)
    for ref in (hidden_ref, feed_ref, got_ref):
        wait(ref, sem.at[3])
    out_ref[...] = (hidden_ref[...] + feed_ref[...] + got_ref[...].astype(F32) + down_bias_ref[...]).astype(BF16)
    start(out_ref, out_out, out_sem)
    wait(ghid_ref, out_sem)
    wait(out_ref, out_sem)


def end(places, ln1, down_bias, gqkv0, gqkv1, ghid, tokens, hidden, feed, feed_got, pieces):
    low, high = pltpu.VMEM((TOK, WIDTH), BF16), pltpu.VMEM((TOK, WIDTH), F32)
    heads = pltpu.VMEM((TOK, PART), BF16)
    return pl.pallas_call(
        end_kernel,
        in_specs=[SMEM] + [VMEM] * 2 + [ANY] * 7 + [HBM] * 4,
        out_specs=[HBM] * 2 + [VMEM],
        out_shape=[shape(TOK, WIDTH, dtype=F32), shape(TOK, WIDTH), shape(8, WIDTH, dtype=F32)],
        scratch_shapes=[parts_buffer(PART), parts_buffer(PART), heads, heads, high, low, high, high, low, low, high, FEW, ONE],
        compiler_params=pltpu.CompilerParams(vmem_limit_bytes=40 * 2**20),
        cost_estimate=work(10e9),
        name="end",
    )(places, ln1, down_bias.reshape(1, WIDTH), gqkv0, gqkv1, ghid, tokens, hidden, feed, feed_got, *pieces)


AXES = ("z", "yh", "c", "x", "yl")


def device_number(place):
    return (
        ((place["z"] * 2 + place["y"] // 2) * 2 + place["c"]) * 4 + place["x"]
    ) * 2 + place["y"] % 2


def exchange_pairs(axis, second, alike=False):
    pairs = []
    for z, y, c, x in itertools.product(range(4), range(4), range(2), range(4)):
        here = {"z": z, "y": y, "c": c, "x": x}
        mask = 1 if (c == 0 or alike) != second else 3
        there = dict(here)
        there[axis] = here[axis] ^ mask
        pairs.append((device_number(here), device_number(there)))
    return pairs


def swap_axis(values, axis, second, alike=False):
    return lax.ppermute(values, AXES, exchange_pairs(axis, second, alike))


def swap_core(values):
    return lax.ppermute(values, "c", [(0, 1), (1, 0)])


def position(axis):
    if axis == "y":
        return lax.axis_index("yh") * 2 + lax.axis_index("yl")
    return lax.axis_index(axis)


def distance_of(core, slot):
    return jnp.where(core == 0, slot ^ (slot >> 1), ((slot << 1) & 3) ^ ((slot ^ (slot >> 1)) & 1))


def place_table():
    core, slots = lax.axis_index("c"), jnp.arange(4, dtype=jnp.int32)
    rows = [
        distance_of(side, slots) ^ position(axis)
        for side in (core, 1 - core)
        for axis in ("x", "y", "z")
    ]
    return jnp.concatenate(rows + [jnp.full((8,), core, jnp.int32)])


def add(left, right, dtype=BF16):
    return (left.astype(F32) + right.astype(F32)).astype(dtype)


def halves(own, got):
    count = own.shape[0] // 2
    return add(own[count:], got[count:]), add(own[:count], got[:count])


def natural_y(pieces):
    here, core = position("y"), lax.axis_index("c")
    away = [jnp.int32(at) ^ here for at in range(4)]
    slots = [jnp.where(core == 0, d ^ (d >> 1), ((d << 1) & 3) ^ (3 * (d >> 1))) for d in away]
    return jnp.stack([lax.dynamic_index_in_dim(pieces, slot, 0, keepdims=False) for slot in slots])


def together(*values):
    return lax.optimization_barrier(values)


def pair_bias(clip_ids):
    clips = clip_ids.reshape(-1, BLOCK)
    row = lax.broadcasted_iota(jnp.int32, (BLOCK, BLOCK), 0)
    col = lax.broadcasted_iota(jnp.int32, (BLOCK, BLOCK), 1)
    allowed = (clips[:, :, None] == clips[:, None, :]) & (row >= col)[None]
    return jnp.where(allowed, 0.0, -1e30).astype(F32)


def on_device(
    tokens,
    qkv_weight,
    out_weight,
    up_weight,
    down_weight,
    ln1_gain,
    ln1_bias,
    q_bias,
    v_bias,
    out_bias,
    ln2_gain,
    ln2_bias,
    up_bias,
    down_bias,
    segment_ids,
    cotangent,
):
    places = place_table()
    heads = qkv_weight.reshape(8, 3, WIDTH)
    pieces = []
    for cols in (slice(0, HALF), slice(HALF, WIDTH)):
        pieces += [heads[:, :, cols].reshape(8, PART), out_weight[:, cols]]
    rows, down, up = jnp.concatenate(pieces, axis=1)[None], down_weight[None], up_weight[None]
    for stage, axes in enumerate((("y", "x", "z"), ("x", "z", "y"))):
        for second in (False, True):
            values = (rows, down, up)
            got = [swap_axis(v, axis, second) for v, axis in zip(values, axes)]
            if stage == 0 and not second:
                *got, grad_other = together(*got, swap_core(cotangent))
            else:
                got = together(*got)
            rows, down, up = [jnp.concatenate(pair) for pair in zip(values, got)]
        if stage == 0:
            rows = natural_y(rows).reshape(1, 2, 16, 4096)
    up = lax.all_gather(up, "x", axis=0).reshape(64, 128, 256)
    rows_got, down_got = together(swap_axis(rows, "z", False), swap_axis(down, "y", False))
    rows, down = jnp.concatenate([rows, rows_got]), jnp.concatenate([down, down_got])
    rows_got, down_got, other_rows = together(
        swap_axis(rows, "z", True), swap_axis(down, "y", True), swap_core(rows)
    )
    pieces = (rows, rows_got, other_rows, swap_core(rows_got))

    ln1 = jnp.stack([ln1_gain, ln1_bias])
    nothing = jnp.zeros((HALF,), F32)
    qkv_bias = jnp.stack(
        [
            jnp.concatenate([q_bias[cols], nothing, v_bias[cols]])[None]
            for cols in (slice(0, HALF), slice(HALF, WIDTH))
        ]
    )
    qkv, low, qkv_kept = project(places, tokens, ln1, qkv_bias, pieces)
    prob, mixed, hidden, low2 = attend(
        places, tokens, pair_bias(segment_ids), qkv, out_bias, jnp.stack([ln2_gain, ln2_bias]), pieces
    )
    up_bias_grad, feed, feed_low, gc, gc_low, dup, keep_down, *move_down = ffn(
        places, up_bias, low2, swap_core(low2), cotangent, grad_other, (up, down, down_got)
    )
    dup = lax.psum_scatter(dup.reshape(4, 16, 128, 256), "x", scatter_dimension=0, tiled=True)[0]

    down_got0 = swap_axis(move_down[0], "y", True)
    sum0, vec2, gqkv0, *main_a, ghid, glow = back(
        0, places, low, qkv_kept, prob, mixed, pieces,
        ln2_gain.reshape(1, WIDTH), hidden, gc, swap_core(gc_low), cotangent,
    )
    down_got0, glow, feed_got, *main_a = together(down_got0, glow, swap_core(feed_low), *main_a)
    move_a = add(main_a[1], swap_core(main_a[3]))
    move_a, move_down, glow = together(move_a, move_down[1], glow)
    got_a, down_got1 = swap_axis(move_a, "z", True), swap_axis(move_down, "y", True)
    got_keep = swap_core(main_a[2])
    sum1, gqkv1, *main_b = back(1, places, low, qkv_kept, prob, mixed, pieces, glow)
    got_a, down_got1, got_keep, gqkv1, *main_b = together(got_a, down_got1, got_keep, gqkv1, *main_b)

    swapped = swap_core(main_b[3])
    move_a, keep_a = halves(add(main_a[0], got_keep), got_a)
    move_down, keep_down = add(keep_down[16:], down_got1), add(keep_down[:16], down_got0)
    swapped, move_a, move_down, gqkv1 = together(swapped, move_a, move_down, gqkv1)
    move_b = add(main_b[1], swapped)
    move_b, gqkv1 = together(move_b, gqkv1)
    got_b, got_a = swap_axis(move_b, "x", True), swap_axis(move_a, "z", False)
    down_got = swap_axis(move_down, "y", False)
    got_keep = swap_core(main_b[2])
    grad_tokens, output, vec1 = end(
        places, ln1, down_bias, gqkv0, gqkv1, ghid, tokens, hidden, feed, feed_got, pieces
    )
    got_b, got_a, down_got, got_keep, dup, vec1 = together(got_b, got_a, down_got, got_keep, dup, vec1)
    sums = jnp.concatenate([sum0.reshape(3, HALF), sum1.reshape(3, HALF)], axis=1)
    blocks = [vec1[0:2], sums[0:1], sums[2:3], vec2[0:4]]
    vector = jnp.concatenate(
        [block.reshape(-1, 128) for block in blocks] + [up_bias_grad.reshape(-1, 128)]
    )
    vector = vector + swap_core(vector)

    def vector_step(axis, second):
        return vector + swap_axis(vector, axis, second, True)

    move_b, keep_b = halves(add(main_b[0], got_keep), got_b)
    move_a, keep_a = halves(keep_a, got_a)
    move_down, keep_down = halves(keep_down, down_got)
    got_b, got_a = swap_axis(move_b, "x", False), swap_axis(move_a, "x", True)
    down_got, up_got = swap_axis(move_down, "z", True), swap_axis(dup[8:], "y", True)
    vector = vector_step("x", False)
    vector = vector_step("x", True)
    got_b, got_a, down_got, up_got, vector = together(got_b, got_a, down_got, up_got, vector)

    move_b, keep_b = halves(keep_b, got_b)
    move_a, keep_a = halves(keep_a, got_a)
    move_down, keep_down = halves(keep_down, down_got)
    move_up, keep_up = halves(dup[:8], up_got)
    got_b, got_a = swap_axis(move_b, "z", True), swap_axis(move_a, "x", False)
    down_got, up_got = swap_axis(move_down, "z", False), swap_axis(move_up, "y", False)
    vector_got = swap_axis(vector, "y", False, True)
    got_b, got_a, down_got, up_got, vector_got = together(got_b, got_a, down_got, up_got, vector_got)

    move_b, keep_b = halves(keep_b, got_b)
    move_down, keep_down = halves(keep_down, down_got)
    move_up, keep_up = halves(keep_up, up_got)
    vector = vector + vector_got
    got_b = swap_axis(move_b, "z", False)
    down_got, up_got = swap_axis(move_down, "x", True), swap_axis(move_up, "z", True)
    vector_got = swap_axis(vector, "y", True, True)
    got_b, down_got, up_got, vector_got = together(got_b, down_got, up_got, vector_got)

    both = jnp.concatenate(
        [add(k, g).reshape(4, 8, 2048) for k, g in ((keep_a, got_a), (keep_b, got_b))], axis=2
    )
    here, core = position("y"), lax.axis_index("c")
    first = jnp.where(core == 0, 1, 3)
    second = 4 - first

    def at(slot):
        return lax.dynamic_index_in_dim(both, slot, 0, keepdims=False)

    move_down, keep_down = halves(keep_down, down_got)
    move_up, keep_up = halves(keep_up, up_got)
    vector = vector + vector_got
    far = swap_axis(jnp.stack([at(here ^ second), at(here ^ second ^ first)]), "y", True)
    down_got, up_got = swap_axis(move_down, "x", False), swap_axis(move_up, "z", False)
    vector_got = swap_axis(vector, "z", False, True)
    far, down_got, up_got, vector_got = together(far, down_got, up_got, vector_got)

    vector = vector + vector_got
    near = swap_axis(add(at(here ^ first), far[1]), "y", False)
    vector = vector_step("z", True)
    down_grad = add(keep_down, down_got, F32)[0]
    up_grad = add(keep_up, up_got, F32)[0]
    row = (at(here).astype(F32) + far[0].astype(F32) + near.astype(F32)).reshape(8, 2, 2048)
    qkv_grad = row[:, :, :PART].reshape(8, 2, 3, HALF).transpose(0, 2, 1, 3).reshape(8, 3 * WIDTH)
    out_grad = row[:, :, PART:].reshape(8, WIDTH)
    summed = vector.reshape(-1)
    vectors = [summed[i * WIDTH : (i + 1) * WIDTH] for i in range(8)]
    return (
        output,
        grad_tokens,
        qkv_grad,
        out_grad,
        up_grad,
        down_grad,
        *vectors[:7],
        summed[8 * WIDTH :],
        vectors[7],
    )


def solution(mesh):
    fine = Mesh(mesh.devices.reshape(4, 2, 2, 4, 2), AXES)
    every, hidden, model = AXES, ("z", "yh", "c"), ("x", "yl")
    weights = (P(every, None), P(every, None), P(model, hidden), P(hidden, model))
    return jax.shard_map(
        on_device,
        mesh=fine,
        in_specs=(P(every, None), *weights, *[P()] * 9, P(every), P(every, None)),
        out_specs=(P(every, None), P(every, None), *weights, *[P()] * 9),
        check_vma=False,
    )
```

time: 412 us -> 333 us (0.81)
  starting transfers between devices: 117 us -> 58 us
  waiting for transfers between devices: 146 us -> 100 us
  between operations: 1.78 us -> 15.3 us
  Pallas kernels: 90 us -> 96.8 us
  local copies, waits for them, and re-layouts: 26.8 us -> 31.5 us
    ppermute x54 -> x43, waiting for transfers between devices: 140 us -> 88.8 us  [swap_axis(): return lax.ppermute(values, AXES, exchange_pairs(axis, second, alike))]
    ppermute x54 -> x43, starting transfers between devices: 102 us -> 55.5 us  [swap_axis(): return lax.ppermute(values, AXES, exchange_pairs(axis, second, alike))]
    ppermute x9 -> x11, starting transfers between devices: 15.3 us -> 2.41 us  [swap_core(): return lax.ppermute(values, 'c', [(0, 1), (1, 0)])]
    unnamed x66 -> x118, local copies, waits for them, and re-layouts: 16.6 us -> 25.3 us
    pallas_call x3 -> x6, Pallas kernels: 90 us -> 96.8 us  [the longest x1 37.7 us: ffn(): pl.pallas_call(ffn_kernel, in_specs=[SMEM, VMEM] + [ANY] * 4 + [HBM] * 3,...]
    concatenate x7 -> x5, local copies, waits for them, and re-layouts: 6.78 us -> 1.33 us  [the longest x1 1.2 us: on_device(): jnp.concatenate([down, down_got])]
    ppermute x9 -> x11, waiting for transfers between devices: 6.7 us -> 11.3 us  [swap_core(): return lax.ppermute(values, 'c', [(0, 1), (1, 0)])]
    convert_element_type x24 -> x21, other arithmetic: 17.6 us -> 21.1 us  [add(): return (left.astype(F32) + right.astype(F32)).astype(dtype)]
  transfers between devices with their start and end apart: 63 -> 56, of which waited for: 29 -> 27; matrix products, arithmetic and copies ran while one was open for 11% -> 9% of each run, Pallas kernels for 5% -> 18%
where the time goes in v3:
time: 333 us; the launch traced here: 327 us
  waiting for transfers between devices  100 us (30%)
  Pallas kernels  96.8 us (29%)
  starting transfers between devices  58 us (17%)
  local copies, waits for them, and re-layouts  31.5 us (9%)
  other arithmetic  25.2 us (8%)
  between operations  15.3 us (5%)
    ppermute x43, waiting for transfers between devices, swap_axis(): return lax.ppermute(values, AXES, exchange_pairs(axis, second, alike))  88.8 us
    ppermute x43, starting transfers between devices, swap_axis(): return lax.ppermute(values, AXES, exchange_pairs(axis, second, alike))  55.5 us
    pallas_call x1, Pallas kernels, ffn(): pl.pallas_call(ffn_kernel, in_specs=[SMEM, VMEM] + [ANY] * 4 + [HBM] * 3,...  37.7 us
    pallas_call x2, Pallas kernels, back(): pl.pallas_call(functools.partial(back_kernel, part), in_specs=[SMEM] + [H...  32 us
    unnamed x118, local copies, waits for them, and re-layouts  25.3 us
    convert_element_type x21, other arithmetic, add(): return (left.astype(F32) + right.astype(F32)).astype(dtype)  21.1 us
    ppermute x11, waiting for transfers between devices, swap_core(): return lax.ppermute(values, 'c', [(0, 1), (1, 0)])  11.3 us
    pallas_call x1, Pallas kernels, attend(): pl.pallas_call(attend_kernel, in_specs=[SMEM] + [VMEM] * 5 + [HBM] * 4, o...  11.1 us
  transfers between devices with their start and end apart: 56, of which 27 were waited for; matrix products, arithmetic and copies ran while one was open for 9% of the time, Pallas kernels for 18%

profile of v3, /device:TPU:0, one launch (start us, length us, event | category | flops | bytes accessed | tf_op | source)
XLA Modules:
  0.0 326.9 jit_solution(16424715548434240350)
XLA Ops:
  17.6 2.3 collective-permute-start.4
  20.7 2.2 collective-permute-start.5
  23.7 4.1 %collective-permute-start.6 = (bf16[2,128,256]{2,1,0:T(8,128)(2,1)S(1)}, bf16[2,128,256]{2,1,0:T(8,128)(2,1)S(1)}, u32[]{:S(2)}, u32[]{:S(2)}) collective-permute-start(bf16[2,128,256]{2,1,0:T(8,128)(2,1)S(1)} %pad_maximum_fusion.11), channel_id=1, source_target_pairs={{0,96},{2,98},{4,100},{6,102},{8,40},{10,42},{12,44},{14,46},{1,97... | collective-permute-start | bytes 393224 | tf_op jit(solution)/shard_map/ppermute | solution.py:526
  27.9 2.9 collective-permute-done.6
  32.5 4.8 %collective-permute-done.7 = bf16[1,2,16,4096]{3,2,1,0:T(8,128)(2,1)S(1)} collective-permute-done((bf16[1,2,16,4096]{3,2,1,0:T(8,128)(2,1)S(1)}, bf16[1,2,16,4096]{3,2,1,0:T(8,128)(2,1)S(1)}, u32[]{:S(2)}, u32[]{:S(2)}) %collective-permute-start.7) | collective-permute-done | bytes 262176 | tf_op jit(solution)/shard_map/ppermute | solution.py:526
  39.0 3.3 %collective-permute-start.11 = (bf16[8,256,128]{2,1,0:T(8,128)(2,1)S(1)}, bf16[8,256,128]{2,1,0:T(8,128)(2,1)S(1)}, u32[]{:S(2)}, u32[]{:S(2)}) collective-permute-start(bf16[8,256,128]{2,1,0:T(8,128)(2,1)S(1)} %pad_maximum_fusion.3), channel_id=1, source_target_pairs={{0,96},{2,98},{4,100},{6,102},{8,40},{10,42},{12,44},{14,46},{1,97... | collective-permute-start | bytes 1572872 | tf_op jit(solution)/shard_map/ppermute | solution.py:526
  46.2 2.5 collective-permute-done.10
  50.5 3.2 collective-permute-done.12
  56.0 14.5 %collective-permute-done.13 = bf16[4,2,16,4096]{3,2,1,0:T(8,128)(2,1)S(1)} collective-permute-done((bf16[4,2,16,4096]{3,2,1,0:T(8,128)(2,1)S(1)}, bf16[4,2,16,4096]{3,2,1,0:T(8,128)(2,1)S(1)}, u32[]{:S(2)}, u32[]{:S(2)}) %collective-permute-start.13) | collective-permute-done | bytes 1048608 | tf_op jit(solution)/shard_map/ppermute | solution.py:526
  76.3 23.5 %collective-permute-done.15.refs_1_ = bf16[8,2,16,4096]{3,2,1,0:T(8,128)(2,1)} collective-permute-done((bf16[8,2,16,4096]{3,2,1,0:T(8,128)(2,1)S(1)}, bf16[8,2,16,4096]{3,2,1,0:T(8,128)(2,1)}, u32[]{:S(2)}, u32[]{:S(2)}) %collective-permute-start.15) | collective-permute-done | bytes 2097184 | tf_op jit(solution)/shard_map/ppermute | solution.py:526
  102.1 4.0 %collective-permute-done.18.refs_3_ = bf16[8,2,16,4096]{3,2,1,0:T(8,128)(2,1)} collective-permute-done((bf16[8,2,16,4096]{3,2,1,0:T(8,128)(2,1)}, bf16[8,2,16,4096]{3,2,1,0:T(8,128)(2,1)}, u32[]{:S(2)}, u32[]{:S(2)}) %collective-permute-start.18) | collective-permute-done | bytes 2097184 | tf_op jit(solution)/shard_map/ppermute | solution.py:530
  107.4 6.5 %project.1 = (bf16[2,512,1536]{2,1,0:T(8,128)(2,1)S(1)}, bf16[512,1024]{1,0:T(8,128)(2,1)S(1)}, bf16[2,512,1536]{2,1,0:T(8,128)(2,1)S(1)}) custom-call(s32[32]{0:T(128)S(1)} %concatenate.73.places, bf16[512,1024]{1,0:T(8,128)(2,1)S(1)} %copy-done.6, f32[2,1024]{1,0:T(2,128)S(1)} %pad_maximum_fusion.16.ln1_ref, ...), custom_call_target="tpu_custom_call" | custom-call | flops 8000000000 | bytes 1048576 | tf_op jit(solution)/shard_map/project/pallas_call | solution.py:241
  116.6 11.1 %attend.1 = (bf16[8,4,256,128]{3,2,1,0:T(8,128)(2,1)S(1)}, bf16[512,1024]{1,0:T(8,128)(2,1)S(1)}, f32[512,1024]{1,0:T(8,128)S(1)}, bf16[512,1024]{1,0:T(8,128)(2,1)S(1)}) custom-call(s32[32]{0:T(128)S(1)} %concatenate.73.places, bf16[512,1024]{1,0:T(8,128)(2,1)S(1)} %copy-done.7, f32[4,128,128]{2,1,0:T(8,128)S(1)} %and_select_fusion.pair_ref, ...), custom_call_target="tpu_custom_call" | custom-call | flops 16000000000 | bytes 1048576 | tf_op jit(solution)/shard_map/attend/pallas_call | solution.py:300
  132.1 2.5 collective-permute-done.19.low_other
  135.5 37.7 %ffn.1 = (f32[16,1,256]{2,1,0:T(1,128)}, f32[512,1024]{1,0:T(8,128)}, bf16[512,1024]{1,0:T(8,128)(2,1)}, f32[512,1024]{1,0:T(8,128)}, bf16[512,1024]{1,0:T(8,128...) custom-call(s32[32]{0:T(128)} %copy-done.3, ...), custom_call_target="tpu_custom_call" | custom-call | flops 40000000000 | bytes 1048576 | tf_op jit(solution)/shard_map/ffn/pallas_call | solution.py:156
  182.1 17.4 %back0.1 = (f32[1,1536]{1,0:T(1,128)S(1)}, f32[8,1024]{1,0:T(8,128)S(1)}, bf16[512,1536]{1,0:T(8,128)(2,1)}, bf16[8,2,16,2048]{3,2,1,0:T(8,128)(2,1)S(1)}, bf16[...) custom-call(s32[32]{0:T(128)S(1)} %copy-done.4, ...), custom_call_target="tpu_custom_call" | custom-call | flops 20000000000 | bytes 1048576 | tf_op jit(solution)/shard_map/back0/pallas_call | solution.py:421
  201.2 2.2 collective-permute-done.23
  203.3 2.6 add_convert_fusion.5
  206.0 3.7 %collective-permute-start.24 = (bf16[8,2,16,2048]{3,2,1,0:T(8,128)(2,1)}, bf16[8,2,16,2048]{3,2,1,0:T(8,128)(2,1)}, u32[]{:S(2)}, u32[]{:S(2)}) collective-permute-start(bf16[8,2,16,2048]{3,2,1,0:T(8,128)(2,1)} %add_convert_fusion.5), channel_id=1, source_target_pairs={{0,96},{2,98},{4,100},{6,102},{8,40},{10,42},{12,44},{14,46},{1,97... | collective-permute-start | bytes 3145736 | tf_op jit(solution)/shard_map/ppermute | solution.py:526
  210.7 14.6 %back1.1 = (f32[1,1536]{1,0:T(1,128)S(1)}, bf16[512,1536]{1,0:T(8,128)(2,1)S(1)}, bf16[8,2,16,2048]{3,2,1,0:T(8,128)(2,1)S(1)}, bf16[8,2,16,2048]{3,2,1,0:T(8,12...) custom-call(s32[32]{0:T(128)S(1)} %copy-done.4, ...), custom_call_target="tpu_custom_call" | custom-call | flops 20000000000 | bytes 1048576 | tf_op jit(solution)/shard_map/back1/pallas_call | solution.py:421
  229.1 4.2 %add_convert_fusion = (bf16[16,256,128]{2,1,0:T(8,128)(2,1)}, bf16[16,256,128]{2,1,0:T(8,128)(2,1)S(1)}) fusion(bf16[16,256,128]{2,1,0:T(8,128)(2,1)} %collective-permute-done.21, bf16[32,256,128]{2,1,0:T(8,128)(2,1)} %get-tuple-element.168, bf16[16,256,128]{2,1,0:T(8,128)(2,1)} %collective-permute-done.25), kind=kLoop, calls=%fused_computation.1 | loop fusion | flops 4194304 | bytes 6291456 | tf_op jit(solution)/shard_map/convert_element_type | solution.py:554
  237.4 4.9 %collective-permute-start.28 = (bf16[8,2,16,2048]{3,2,1,0:T(8,128)(2,1)S(1)}, bf16[8,2,16,2048]{3,2,1,0:T(8,128)(2,1)}, u32[]{:S(2)}, u32[]{:S(2)}) collective-permute-start(bf16[8,2,16,2048]{3,2,1,0:T(8,128)(2,1)S(1)} %add_convert_fusion.2), channel_id=1, source_target_pairs={{0,6},{2,4},{4,2},{6,0},{8,10},{10,8},{12,14},{14,12},{1,7},{3,5},... | collective-permute-start | bytes 3145736 | tf_op jit(solution)/shard_map/ppermute | solution.py:526
  242.5 9.5 %end.1 = (f32[512,1024]{1,0:T(8,128)}, bf16[512,1024]{1,0:T(8,128)(2,1)}, f32[8,1024]{1,0:T(8,128)S(1)}) custom-call(s32[32]{0:T(128)S(1)} %copy-done.4, f32[2,1024]{1,0:T(2,128)S(1)} %pad_maximum_fusion.16.ln1_ref, f32[1,1024]{1,0:T(1,128)S(1)} %bitcast.61, bf16[512,1536]{1,0:T(8,128)(2,1)S(1)} %copy-done.21, bf16[512,1536]{1,0:T(8,128)(2,1)S(1)} %copy-done.23, ...), custom_call_target="tpu_custom_call" | custom-call | flops 10000000000 | bytes 1048576 | tf_op jit(solution)/shard_map/end/pallas_call | solution.py:493
  252.0 3.2 collective-permute-done.28
  258.7 2.5 add_convert_fusion.9
  270.2 4.5 %collective-permute-done.37 = f32[96,128]{1,0:T(8,128)S(1)} collective-permute-done((f32[96,128]{1,0:T(8,128)S(1)}, f32[96,128]{1,0:T(8,128)S(1)}, u32[]{:S(2)}, u32[]{:S(2)}) %collective-permute-start.37) | collective-permute-done | bytes 49184 | tf_op jit(solution)/shard_map/ppermute | solution.py:526
  275.3 4.7 %collective-permute-done.38 = f32[96,128]{1,0:T(8,128)S(1)} collective-permute-done((f32[96,128]{1,0:T(8,128)S(1)}, f32[96,128]{1,0:T(8,128)S(1)}, u32[]{:S(2)}, u32[]{:S(2)}) %collective-permute-start.38) | collective-permute-done | bytes 49184 | tf_op jit(solution)/shard_map/ppermute | solution.py:526
  287.5 4.5 %collective-permute-done.43 = f32[96,128]{1,0:T(8,128)S(1)} collective-permute-done((f32[96,128]{1,0:T(8,128)S(1)}, f32[96,128]{1,0:T(8,128)S(1)}, u32[]{:S(2)}, u32[]{:S(2)}) %collective-permute-start.43) | collective-permute-done | bytes 49184 | tf_op jit(solution)/shard_map/ppermute | solution.py:526
  292.0 2.1 collective-permute-start.44
  299.6 2.4 collective-permute-done.47
  307.0 2.8 collective-permute-done.51
  313.1 4.1 %collective-permute-done.53 = f32[96,128]{1,0:T(8,128)S(1)} collective-permute-done((f32[96,128]{1,0:T(8,128)S(1)}, f32[96,128]{1,0:T(8,128)S(1)}, u32[]{:S(2)}, u32[]{:S(2)}) %collective-permute-start.53) | collective-permute-done | bytes 49184 | tf_op jit(solution)/shard_map/ppermute | solution.py:526
  (289 shorter events, 96.3 us)
Async XLA Ops:
  7.2 127.4 %all-gather.3.cloned.1.call-start = ((), (), s32[]{:S(2)}) async-start(), calls=%async_computation.2 | async-start | bytes 5242880 | tf_op jit(solution)/shard_map/all_gather | solution.py:616
  7.2 9.3 %collective-permute-start.3 = (bf16[512,1024]{1,0:T(8,128)(2,1)}, bf16[512,1024]{1,0:T(8,128)(2,1)S(1)}, u32[]{:S(2)}, u32[]{:S(2)}) collective-permute-start(bf16[512,1024]{1,0:T(8,128)(2,1)} %refs_8_.1), channel_id=1, source_target_pairs={{0,8},{8,0},{1,9},{9,1},{2,10},{10,2},{3,11},{11,3},{4,12},{12,4},... | collective-permute-start | bytes 3145736 | tf_op jit(solution)/shard_map/ppermute | solution.py:530
  17.6 10.3 %collective-permute-start.4 = (bf16[2,8,4096]{2,1,0:T(8,128)(2,1)S(1)}, bf16[2,8,4096]{2,1,0:T(8,128)(2,1)S(1)}, u32[]{:S(2)}, u32[]{:S(2)}) collective-permute-start(bf16[2,8,4096]{2,1,0:T(8,128)(2,1)S(1)} %pad_maximum_fusion.9), channel_id=1, source_target_pairs={{0,17},{2,19},{4,21},{6,23},{8,9},{10,11},{12,13},{14,15},{1,16},{... | collective-permute-start | bytes 393224 | tf_op jit(solution)/shard_map/ppermute | solution.py:526
  38.3 10.5 %collective-permute-start.10 = (bf16[2,2,16,4096]{3,2,1,0:T(8,128)(2,1)S(1)}, bf16[2,2,16,4096]{3,2,1,0:T(8,128)(2,1)S(1)}, u32[]{:S(2)}, u32[]{:S(2)}) collective-permute-start(bf16[2,2,16,4096]{3,2,1,0:T(8,128)(2,1)S(1)} %pad_maximum_fusion.2), channel_id=1, source_target_pairs={{0,6},{2,4},{4,2},{6,0},{8,10},{10,8},{12,14},{14,12},{1,7},{3,5},... | collective-permute-start | bytes 1572872 | tf_op jit(solution)/shard_map/ppermute | solution.py:526
  39.0 11.4 %collective-permute-start.11 = (bf16[8,256,128]{2,1,0:T(8,128)(2,1)S(1)}, bf16[8,256,128]{2,1,0:T(8,128)(2,1)S(1)}, u32[]{:S(2)}, u32[]{:S(2)}) collective-permute-start(bf16[8,256,128]{2,1,0:T(8,128)(2,1)S(1)} %pad_maximum_fusion.3), channel_id=1, source_target_pairs={{0,96},{2,98},{4,100},{6,102},{8,40},{10,42},{12,44},{14,46},{1,97... | collective-permute-start | bytes 1572872 | tf_op jit(solution)/shard_map/ppermute | solution.py:526
  42.4 11.3 %collective-permute-start.12 = (bf16[8,128,256]{2,1,0:T(8,128)(2,1)S(1)}, bf16[8,128,256]{2,1,0:T(8,128)(2,1)S(1)}, u32[]{:S(2)}, u32[]{:S(2)}) collective-permute-start(bf16[8,128,256]{2,1,0:T(8,128)(2,1)S(1)} %pad_maximum_fusion.4), channel_id=1, source_target_pairs={{0,17},{2,19},{4,21},{6,23},{8,9},{10,11},{12,13},{14,15},{1,16},{... | collective-permute-start | bytes 1572872 | tf_op jit(solution)/shard_map/ppermute | solution.py:526
  53.8 16.7 %collective-permute-start.13 = (bf16[4,2,16,4096]{3,2,1,0:T(8,128)(2,1)S(1)}, bf16[4,2,16,4096]{3,2,1,0:T(8,128)(2,1)S(1)}, u32[]{:S(2)}, u32[]{:S(2)}) collective-permute-start(bf16[4,2,16,4096]{3,2,1,0:T(8,128)(2,1)S(1)} %pad_maximum_fusion.1), channel_id=1, source_target_pairs={{0,32},{2,34},{4,36},{6,38},{8,104},{10,106},{12,108},{14,110},{1,... | collective-permute-start | bytes 3145736 | tf_op jit(solution)/shard_map/ppermute | solution.py:526
  56.0 16.2 %collective-permute-start.14 = (bf16[16,256,128]{2,1,0:T(8,128)(2,1)S(1)}, bf16[16,256,128]{2,1,0:T(8,128)(2,1)S(1)}, u32[]{:S(2)}, u32[]{:S(2)}) collective-permute-start(bf16[16,256,128]{2,1,0:T(8,128)(2,1)S(1)} %get-tuple-element.236), channel_id=1, source_target_pairs={{0,1},{2,3},{4,5},{6,7},{8,25},{10,27},{12,29},{14,31},{1,0},{3,2}... | collective-permute-start | bytes 3145736 | tf_op jit(solution)/shard_map/ppermute | solution.py:526
  72.4 27.4 %collective-permute-start.15 = (bf16[8,2,16,4096]{3,2,1,0:T(8,128)(2,1)S(1)}, bf16[8,2,16,4096]{3,2,1,0:T(8,128)(2,1)}, u32[]{:S(2)}, u32[]{:S(2)}) collective-permute-start(bf16[8,2,16,4096]{3,2,1,0:T(8,128)(2,1)S(1)} %pad_maximum_fusion.refs_0_), channel_id=1, source_target_pairs={{0,96},{2,98},{4,100},{6,102},{8,40},{10,42},{12,44},{14,46},{1,97... | collective-permute-start | bytes 6291464 | tf_op jit(solution)/shard_map/ppermute | solution.py:526
  73.7 27.6 %collective-permute-start.16 = (bf16[32,256,128]{2,1,0:T(8,128)(2,1)}, bf16[32,256,128]{2,1,0:T(8,128)(2,1)}, u32[]{:S(2)}, u32[]{:S(2)}) collective-permute-start(bf16[32,256,128]{2,1,0:T(8,128)(2,1)} %constant_dynamic-update-slice_fusion.5.down_low), channel_id=1, source_target_pairs={{0,17},{2,19},{4,21},{6,23},{8,9},{10,11},{12,13},{14,15},{1,16},{... | collective-permute-start | bytes 6291464 | tf_op jit(solution)/shard_map/ppermute | solution.py:526
  75.2 26.2 %collective-permute-start.17 = (bf16[8,2,16,4096]{3,2,1,0:T(8,128)(2,1)S(1)}, bf16[8,2,16,4096]{3,2,1,0:T(8,128)(2,1)}, u32[]{:S(2)}, u32[]{:S(2)}) collective-permute-start(bf16[8,2,16,4096]{3,2,1,0:T(8,128)(2,1)S(1)} %pad_maximum_fusion.refs_0_), channel_id=1, source_target_pairs={{0,8},{8,0},{1,9},{9,1},{2,10},{10,2},{3,11},{11,3},{4,12},{12,4},... | collective-permute-start | bytes 6291464 | tf_op jit(solution)/shard_map/ppermute | solution.py:530
  76.3 180.8 %reduce-scatter.2.cloned.1.call-start = ((), (), s32[]{:S(2)}) async-start(), calls=%async_computation.1 | async-start | bytes 5242880 | tf_op jit(solution)/shard_map/reduce_scatter | solution.py:639
  173.5 27.1 %collective-permute-start.21 = (bf16[16,256,128]{2,1,0:T(8,128)(2,1)}, bf16[16,256,128]{2,1,0:T(8,128)(2,1)}, u32[]{:S(2)}, u32[]{:S(2)}) collective-permute-start(bf16[16,256,128]{2,1,0:T(8,128)(2,1)} %get-tuple-element.143), channel_id=1, source_target_pairs={{0,17},{2,19},{4,21},{6,23},{8,9},{10,11},{12,13},{14,15},{1,16},{... | collective-permute-start | bytes 3145736 | tf_op jit(solution)/shard_map/ppermute | solution.py:526
  174.8 25.7 %collective-permute-start.22 = (bf16[512,1024]{1,0:T(8,128)(2,1)}, bf16[512,1024]{1,0:T(8,128)(2,1)}, u32[]{:S(2)}, u32[]{:S(2)}) collective-permute-start(bf16[512,1024]{1,0:T(8,128)(2,1)} %get-tuple-element.145), channel_id=1, source_target_pairs={{0,8},{8,0},{1,9},{9,1},{2,10},{10,2},{3,11},{11,3},{4,12},{12,4},... | collective-permute-start | bytes 3145736 | tf_op jit(solution)/shard_map/ppermute | solution.py:530
  200.8 27.7 %collective-permute-start.26 = (bf16[8,2,16,2048]{3,2,1,0:T(8,128)(2,1)}, bf16[8,2,16,2048]{3,2,1,0:T(8,128)(2,1)}, u32[]{:S(2)}, u32[]{:S(2)}) collective-permute-start(bf16[8,2,16,2048]{3,2,1,0:T(8,128)(2,1)} %get-tuple-element.156), channel_id=1, source_target_pairs={{0,8},{8,0},{1,9},{9,1},{2,10},{10,2},{3,11},{11,3},{4,12},{12,4},... | collective-permute-start | bytes 3145736 | tf_op jit(solution)/shard_map/ppermute | solution.py:530
  206.0 22.6 %collective-permute-start.24 = (bf16[8,2,16,2048]{3,2,1,0:T(8,128)(2,1)}, bf16[8,2,16,2048]{3,2,1,0:T(8,128)(2,1)}, u32[]{:S(2)}, u32[]{:S(2)}) collective-permute-start(bf16[8,2,16,2048]{3,2,1,0:T(8,128)(2,1)} %add_convert_fusion.5), channel_id=1, source_target_pairs={{0,96},{2,98},{4,100},{6,102},{8,40},{10,42},{12,44},{14,46},{1,97... | collective-permute-start | bytes 3145736 | tf_op jit(solution)/shard_map/ppermute | solution.py:526
  209.7 18.8 %collective-permute-start.25 = (bf16[16,256,128]{2,1,0:T(8,128)(2,1)}, bf16[16,256,128]{2,1,0:T(8,128)(2,1)}, u32[]{:S(2)}, u32[]{:S(2)}) collective-permute-start(bf16[16,256,128]{2,1,0:T(8,128)(2,1)} %get-tuple-element.155), channel_id=1, source_target_pairs={{0,17},{2,19},{4,21},{6,23},{8,9},{10,11},{12,13},{14,15},{1,16},{... | collective-permute-start | bytes 3145736 | tf_op jit(solution)/shard_map/ppermute | solution.py:526
  228.5 8.4 %collective-permute-start.27 = (bf16[8,2,16,2048]{3,2,1,0:T(8,128)(2,1)}, bf16[8,2,16,2048]{3,2,1,0:T(8,128)(2,1)S(1)}, u32[]{:S(2)}, u32[]{:S(2)}) collective-permute-start(bf16[8,2,16,2048]{3,2,1,0:T(8,128)(2,1)} %copy-done.10), channel_id=1, source_target_pairs={{0,8},{8,0},{1,9},{9,1},{2,10},{10,2},{3,11},{11,3},{4,12},{12,4},... | collective-permute-start | bytes 3145736 | tf_op jit(solution)/shard_map/ppermute | solution.py:530
  228.6 23.3 %collective-permute-start.31 = (bf16[8,2,16,2048]{3,2,1,0:T(8,128)(2,1)}, bf16[8,2,16,2048]{3,2,1,0:T(8,128)(2,1)}, u32[]{:S(2)}, u32[]{:S(2)}) collective-permute-start(bf16[8,2,16,2048]{3,2,1,0:T(8,128)(2,1)} %copy-done.9), channel_id=1, source_target_pairs={{0,8},{8,0},{1,9},{9,1},{2,10},{10,2},{3,11},{11,3},{4,12},{12,4},... | collective-permute-start | bytes 3145736 | tf_op jit(solution)/shard_map/ppermute | solution.py:530
  237.4 17.8 %collective-permute-start.28 = (bf16[8,2,16,2048]{3,2,1,0:T(8,128)(2,1)S(1)}, bf16[8,2,16,2048]{3,2,1,0:T(8,128)(2,1)}, u32[]{:S(2)}, u32[]{:S(2)}) collective-permute-start(bf16[8,2,16,2048]{3,2,1,0:T(8,128)(2,1)S(1)} %add_convert_fusion.2), channel_id=1, source_target_pairs={{0,6},{2,4},{4,2},{6,0},{8,10},{10,8},{12,14},{14,12},{1,7},{3,5},... | collective-permute-start | bytes 3145736 | tf_op jit(solution)/shard_map/ppermute | solution.py:526
  242.3 14.8 %collective-permute-start.30 = (bf16[16,256,128]{2,1,0:T(8,128)(2,1)S(1)}, bf16[16,256,128]{2,1,0:T(8,128)(2,1)S(1)}, u32[]{:S(2)}, u32[]{:S(2)}) collective-permute-start(bf16[16,256,128]{2,1,0:T(8,128)(2,1)S(1)} %get-tuple-element.181), channel_id=1, source_target_pairs={{0,1},{2,3},{4,5},{6,7},{8,25},{10,27},{12,29},{14,31},{1,0},{3,2}... | collective-permute-start | bytes 3145736 | tf_op jit(solution)/shard_map/ppermute | solution.py:526
  242.3 9.6 %collective-permute-start.29 = (bf16[4,2,16,2048]{3,2,1,0:T(8,128)(2,1)S(1)}, bf16[4,2,16,2048]{3,2,1,0:T(8,128)(2,1)S(1)}, u32[]{:S(2)}, u32[]{:S(2)}) collective-permute-start(bf16[4,2,16,2048]{3,2,1,0:T(8,128)(2,1)S(1)} %get-tuple-element.180), channel_id=1, source_target_pairs={{0,32},{2,34},{4,36},{6,38},{8,104},{10,106},{12,108},{14,110},{1,... | collective-permute-start | bytes 1572872 | tf_op jit(solution)/shard_map/ppermute | solution.py:526
  261.3 18.8 %collective-permute-start.32 = (bf16[4,2,16,2048]{3,2,1,0:T(8,128)(2,1)}, bf16[4,2,16,2048]{3,2,1,0:T(8,128)(2,1)S(1)}, u32[]{:S(2)}, u32[]{:S(2)}) collective-permute-start(bf16[4,2,16,2048]{3,2,1,0:T(8,128)(2,1)} %get-tuple-element.221), channel_id=1, source_target_pairs={{0,2},{2,0},{4,6},{6,4},{8,14},{10,12},{12,10},{14,8},{1,3},{3,1},... | collective-permute-start | bytes 1572872 | tf_op jit(solution)/shard_map/ppermute | solution.py:526
  262.3 17.8 %collective-permute-start.33 = (bf16[2,2,16,2048]{3,2,1,0:T(8,128)(2,1)}, bf16[2,2,16,2048]{3,2,1,0:T(8,128)(2,1)}, u32[]{:S(2)}, u32[]{:S(2)}) collective-permute-start(bf16[2,2,16,2048]{3,2,1,0:T(8,128)(2,1)} %get-tuple-element.230), channel_id=1, source_target_pairs={{0,6},{2,4},{4,2},{6,0},{8,10},{10,8},{12,14},{14,12},{1,7},{3,5},... | collective-permute-start | bytes 786440 | tf_op jit(solution)/shard_map/ppermute | solution.py:526
  264.7 15.4 %collective-permute-start.34 = (bf16[8,256,128]{2,1,0:T(8,128)(2,1)}, bf16[8,256,128]{2,1,0:T(8,128)(2,1)}, u32[]{:S(2)}, u32[]{:S(2)}) collective-permute-start(bf16[8,256,128]{2,1,0:T(8,128)(2,1)} %get-tuple-element.216), channel_id=1, source_target_pairs={{0,96},{2,98},{4,100},{6,102},{8,40},{10,42},{12,44},{14,46},{1,97... | collective-permute-start | bytes 1572872 | tf_op jit(solution)/shard_map/ppermute | solution.py:526
  265.7 14.4 %collective-permute-start.35 = (bf16[8,128,256]{2,1,0:T(8,128)(2,1)}, bf16[8,128,256]{2,1,0:T(8,128)(2,1)S(1)}, u32[]{:S(2)}, u32[]{:S(2)}) collective-permute-start(bf16[8,128,256]{2,1,0:T(8,128)(2,1)} %slice.293), channel_id=1, source_target_pairs={{0,17},{2,19},{4,21},{6,23},{8,9},{10,11},{12,13},{14,15},{1,16},{... | collective-permute-start | bytes 1572872 | tf_op jit(solution)/shard_map/ppermute | solution.py:526
  281.0 10.9 %collective-permute-start.39 = (bf16[2,2,16,2048]{3,2,1,0:T(8,128)(2,1)S(1)}, bf16[2,2,16,2048]{3,2,1,0:T(8,128)(2,1)S(1)}, u32[]{:S(2)}, u32[]{:S(2)}) collective-permute-start(bf16[2,2,16,2048]{3,2,1,0:T(8,128)(2,1)S(1)} %get-tuple-element.228), channel_id=1, source_target_pairs={{0,96},{2,98},{4,100},{6,102},{8,40},{10,42},{12,44},{14,46},{1,97... | collective-permute-start | bytes 786440 | tf_op jit(solution)/shard_map/ppermute | solution.py:526
  283.4 8.6 %collective-permute-start.41 = (bf16[4,256,128]{2,1,0:T(8,128)(2,1)S(1)}, bf16[4,256,128]{2,1,0:T(8,128)(2,1)S(1)}, u32[]{:S(2)}, u32[]{:S(2)}) collective-permute-start(bf16[4,256,128]{2,1,0:T(8,128)(2,1)S(1)} %get-tuple-element.226), channel_id=1, source_target_pairs={{0,32},{2,34},{4,36},{6,38},{8,104},{10,106},{12,108},{14,110},{1,... | collective-permute-start | bytes 786440 | tf_op jit(solution)/shard_map/ppermute | solution.py:526
  284.3 7.7 %collective-permute-start.42 = (bf16[4,128,256]{2,1,0:T(8,128)(2,1)}, bf16[4,128,256]{2,1,0:T(8,128)(2,1)S(1)}, u32[]{:S(2)}, u32[]{:S(2)}) collective-permute-start(bf16[4,128,256]{2,1,0:T(8,128)(2,1)} %get-tuple-element.224), channel_id=1, source_target_pairs={{0,1},{2,3},{4,5},{6,7},{8,25},{10,27},{12,29},{14,31},{1,0},{3,2}... | collective-permute-start | bytes 786440 | tf_op jit(solution)/shard_map/ppermute | solution.py:526
  292.0 10.0 %collective-permute-start.44 = (bf16[1,2,16,2048]{3,2,1,0:T(8,128)(2,1)S(1)}, bf16[1,2,16,2048]{3,2,1,0:T(8,128)(2,1)S(1)}, u32[]{:S(2)}, u32[]{:S(2)}) collective-permute-start(bf16[1,2,16,2048]{3,2,1,0:T(8,128)(2,1)S(1)} %add_convert_fusion.25), channel_id=1, source_target_pairs={{0,32},{2,34},{4,36},{6,38},{8,104},{10,106},{12,108},{14,110},{1,... | collective-permute-start | bytes 393224 | tf_op jit(solution)/shard_map/ppermute | solution.py:526
  294.1 7.9 %collective-permute-start.45 = (bf16[2,256,128]{2,1,0:T(8,128)(2,1)S(1)}, bf16[2,256,128]{2,1,0:T(8,128)(2,1)S(1)}, u32[]{:S(2)}, u32[]{:S(2)}) collective-permute-start(bf16[2,256,128]{2,1,0:T(8,128)(2,1)S(1)} %get-tuple-element.234), channel_id=1, source_target_pairs={{0,6},{2,4},{4,2},{6,0},{8,10},{10,8},{12,14},{14,12},{1,7},{3,5},... | collective-permute-start | bytes 393224 | tf_op jit(solution)/shard_map/ppermute | solution.py:526
  309.8 8.7 %collective-permute-start.52 = (bf16[8,4096]{1,0:T(8,128)(2,1)S(1)}, bf16[8,4096]{1,0:T(8,128)(2,1)S(1)}, u32[]{:S(2)}, u32[]{:S(2)}) collective-permute-start(bf16[8,4096]{1,0:T(8,128)(2,1)S(1)} %fusion), channel_id=1, source_target_pairs={{0,1},{2,3},{4,5},{6,7},{8,25},{10,27},{12,29},{14,31},{1,0},{3,2}... | collective-permute-start | bytes 196616 | tf_op jit(solution)/shard_map/ppermute | solution.py:526
  (76 other events, 612.4 us)
Sparse Core Ops, SparseCore 0:
  76.4 49.0 all-gather.2
  175.0 47.6 reduce-scatter.1
